TPU v7x, 768 devices: a whole 4x8x12 slice. The times are simulated.
768 devices in a mesh: img: 192 (over y, z, x_hi), txt: 4 (over x_lo, core).
Axes of the slice: x: 4 (x_hi: 2, x_lo: 2; x = x_hi * 2 + x_lo), y: 8, z: 12, core: 2. Of those that a mesh axis runs over, the one named last changes fastest.
Arguments:
- images: bfloat16 [147456, 1152], P(('img', 'txt')), may hold values from -0.1875 to 0.1875
- texts: bfloat16 [147456, 1152], P(('img', 'txt')), may hold values from -0.1875 to 0.1875
- log_temp: float32 [], replicated, may hold values from 1.8 to 2.6
- bias: float32 [], replicated, may hold values from -4 to -2
Outputs:
- text_loss: float32 [147456], P(('img', 'txt'))
- image_grad: float32 [147456, 1152], P(('img', 'txt'))
- text_grad: float32 [147456, 1152], P(('img', 'txt'))
All inputs are finite; a program needn't handle non-finite values.
Results may differ from a plain program's by a relative error of at most 0.0043.
Values may be sent and summed in bfloat16 or wider, within the bound.
No kernel may reach another device: no remote copies, remote signals or barrier semaphores. Data moves between devices by JAX's collectives and lax.ppermute only.
A program may use at most 32 MiB of HBM per device.

v0:
```python
import jax
import jax.numpy as jnp
from jax import lax
from jax.sharding import PartitionSpec as P

VISITS = 4


EPSILON = 1e-06


def shifted(block, axis, distance):
    devices = range(lax.axis_size(axis))
    route = [((i - distance) % len(devices), i) for i in devices]
    return lax.ppermute(block, axis, route)


def unit_rows(values):
    wide = values.astype(jnp.float32)
    length = jnp.sqrt(jnp.sum(wide * wide, axis=-1, keepdims=True) + EPSILON)
    return (wide / length, length)


def pair_tiles(image_group, text_block, anchor, img_place, txt_place, temper, offset_bias):
    shard_rows = text_block.shape[0]
    logits = (
        temper
        * jnp.einsum("gd,rd->gr", image_group, text_block, preferred_element_type=jnp.float32)
        + offset_bias
    )
    row_ids = lax.broadcasted_iota(jnp.int32, logits.shape, 0)
    col_ids = lax.broadcasted_iota(jnp.int32, logits.shape, 1)
    positive = (anchor == img_place) & (row_ids == txt_place * shard_rows + col_ids)
    labels = jnp.where(positive, 1.0, -1.0).astype(jnp.float32)
    margin = -labels * logits
    losses = jnp.sum(jax.nn.softplus(margin), axis=0)
    slopes = (-labels * jax.nn.sigmoid(margin)).astype(jnp.bfloat16)
    image_part = temper * jnp.einsum(
        "gr,rd->gd", slopes, text_block, preferred_element_type=jnp.float32
    )
    text_part = temper * jnp.einsum(
        "gr,gd->rd", slopes, image_group, preferred_element_type=jnp.float32
    )
    return (losses, image_part, text_part)


def on_device(images, texts, log_temp, bias):
    temper = jnp.exp(log_temp)
    img_place = lax.axis_index("img")
    txt_place = lax.axis_index("txt")
    img_count = lax.axis_size("img")
    shard_rows, width = texts.shape
    image_unit, image_length = unit_rows(images)
    text_unit, text_length = unit_rows(texts)
    image_half = image_unit.astype(jnp.bfloat16)
    text_half = text_unit.astype(jnp.bfloat16)
    image_group = lax.all_gather(image_half, "txt", axis=0, tiled=True)
    group_rows = image_group.shape[0]
    image_dir = jnp.zeros((group_rows, width), jnp.float32)
    text_dir = jnp.zeros((shard_rows, width), jnp.float32)
    loss_sum = jnp.zeros((shard_rows,), jnp.float32)
    block = text_half
    for step in range(VISITS):
        if step + 1 < VISITS:
            coming = shifted(block, "img", 1)
        anchor = (img_place - step) % img_count
        losses, image_part, text_part = pair_tiles(
            image_group, block, anchor, img_place, txt_place, temper, bias
        )
        image_dir = image_dir + image_part
        text_dir = text_dir + text_part
        loss_sum = loss_sum + losses
        if step + 1 < VISITS:
            text_dir, loss_sum = shifted((text_dir, loss_sum), "img", 1)
        if step + 1 < VISITS:
            block = coming
    text_dir, loss_sum = shifted((text_dir, loss_sum), "img", 1 - VISITS)
    image_total = lax.psum_scatter(image_dir, "txt", scatter_dimension=0, tiled=True)
    text_loss = loss_sum / (VISITS * group_rows)
    image_grad = (
        image_total - image_unit * jnp.sum(image_unit * image_total, axis=-1, keepdims=True)
    ) / image_length
    text_grad = (
        text_dir - text_unit * jnp.sum(text_unit * text_dir, axis=-1, keepdims=True)
    ) / text_length
    return (text_loss, image_grad, text_grad)


def solution(mesh):
    in_specs = (P(("img", "txt"), None), P(("img", "txt"), None), P(), P())
    out_specs = (P(("img", "txt")), P(("img", "txt"), None), P(("img", "txt"), None))
    return jax.shard_map(
        on_device, mesh=mesh, in_specs=in_specs, out_specs=out_specs, check_vma=False
    )
```

profile of v0, /device:TPU:32, one launch (start us, length us, event | category | flops | bytes accessed | tf_op | source)
XLA Modules:
  0.0 247.7 jit_solution(16098380716101138595)
XLA Ops:
  7.2 0.0 copy-start
  7.2 0.0 all-gather.2.cloned.1.call-start
  7.2 1.2 fusion.10
  8.5 1.9 fusion.20
  10.4 0.0 all-gather.2.cloned.1.call-update
  10.4 0.0 reduce-scatter.2.cloned.1.call-start
  10.5 0.0 copy-done
  10.5 0.2 fusion.11
  10.7 0.2 fusion.21
  10.8 4.9 %collective-permute-start.1 = (bf16[192,1152]{1,0:T(8,128)(2,1)S(1)}, bf16[192,1152]{1,0:T(8,128)(2,1)S(1)}, u32[]{:S(2)}, u32[]{:S(2)}) collective-permute-start(bf16[192,1152]{1,0:T(8,128)(2,1)S(1)} %fusion.21), channel_id=1, source_target_pairs={{764,0},{0,4},{4,8},{8,12},{12,16},{16,20},{20,24},{24,28},{28,32}... | collective-permute-start | bytes 1327112 | tf_op jit(solution)/shard_map/ppermute | solution.py:15
  15.8 22.2 %collective-permute-done.1 = bf16[192,1152]{1,0:T(8,128)(2,1)S(1)} collective-permute-done((bf16[192,1152]{1,0:T(8,128)(2,1)S(1)}, bf16[192,1152]{1,0:T(8,128)(2,1)S(1)}, u32[]{:S(2)}, u32[]{:S(2)}) %collective-permute-start.1) | collective-permute-done | bytes 442400 | tf_op jit(solution)/shard_map/ppermute | solution.py:15
  37.9 1.9 collective-permute-start.3
  41.3 17.9 %collective-permute-done.3 = bf16[192,1152]{1,0:T(8,128)(2,1)} collective-permute-done((bf16[192,1152]{1,0:T(8,128)(2,1)S(1)}, bf16[192,1152]{1,0:T(8,128)(2,1)}, u32[]{:S(2)}, u32[]{:S(2)}) %collective-permute-start.3) | collective-permute-done | bytes 442400 | tf_op jit(solution)/shard_map/ppermute | solution.py:15
  59.2 6.0 %collective-permute-start.5 = (bf16[192,1152]{1,0:T(8,128)(2,1)}, bf16[192,1152]{1,0:T(8,128)(2,1)}, u32[]{:S(2)}, u32[]{:S(2)}) collective-permute-start(bf16[192,1152]{1,0:T(8,128)(2,1)} %collective-permute-done.3), channel_id=1, source_target_pairs={{764,0},{0,4},{4,8},{8,12},{12,16},{16,20},{20,24},{24,28},{28,32}... | collective-permute-start | bytes 1327112 | tf_op jit(solution)/shard_map/ppermute | solution.py:15
  65.2 0.0 all-gather.2.cloned.1.call-done
  65.2 0.0 copy-start.3
  65.2 2.6 %fusion.12 = (f32[192]{0:T(256)S(1)}, f32[768,192]{0,1:T(8,128)S(1)}) fusion(f32[]{:T(128)S(6)} %copy.8, bf16[768,1152]{1,0:T(8,128)(2,1)} %all-gather.2.cloned.1.call-done, bf16[192,1152]{1,0:T(8,128)(2,1)S(1)} %fusion.21, f32[]{:T(128)S(6)} %exp.28, s32[192]{0:T(256)S(1)} %iota_add_fusion, pred[]{:T(512)S(6)} %eq.23), kind=kOutput, calls=%fused_computation.35 | convolution fusion | flops 341802816 | bytes 2803209 | tf_op jit(solution)/shard_map/gd,rd->gr/dot_general | solution.py:28
  67.8 0.0 copy-done.3
  67.8 1.0 fusion.13
  68.9 2.0 fusion.14
  70.9 0.9 fusion.22
  71.8 6.2 %collective-permute-done.5 = bf16[192,1152]{1,0:T(8,128)(2,1)} collective-permute-done((bf16[192,1152]{1,0:T(8,128)(2,1)}, bf16[192,1152]{1,0:T(8,128)(2,1)}, u32[]{:S(2)}, u32[]{:S(2)}) %collective-permute-start.5) | collective-permute-done | bytes 442400 | tf_op jit(solution)/shard_map/ppermute | solution.py:15
  78.1 2.0 fusion.15
  80.1 0.9 convolution_add_fusion.2
  81.0 2.0 convolution_add_fusion.1
  83.0 3.7 %fusion = f32[768,1152]{1,0:T(8,128)} fusion(f32[768,1152]{1,0:T(8,128)S(1)} %convolution_add_fusion.1, bf16[192,1152]{1,0:T(8,128)(2,1)} %collective-permute-done.5, f32[]{:T(128)S(6)} %exp.28, f32[768,192]{0,1:T(8,128)S(1)} %get-tuple-element.10, s32[192]{0:T(256)S(1)} %iota_add_fusion, pred[]{:T(512)S(6)} %eq.27), kind=kOutput, calls=%fused_computation.1 | convolution fusion | flops 342835200 | bytes 8110853 | tf_op jit(solution)/shard_map/gr,rd->gd/dot_general | solution.py:38
  86.7 0.0 reduce-scatter.2.cloned.1.call-update
  86.7 0.0 copy-start.4
  86.8 2.3 convolution_multiply_fusion.3
  89.1 1.9 collective-permute-start.7
  91.0 25.3 %collective-permute-done.7 = f32[192,1152]{1,0:T(8,128)S(1)} collective-permute-done((f32[192,1152]{1,0:T(8,128)S(1)}, f32[192,1152]{1,0:T(8,128)S(1)}, u32[]{:S(2)}, u32[]{:S(2)}) %collective-permute-start.7) | collective-permute-done | bytes 884768 | tf_op jit(solution)/shard_map/ppermute | solution.py:15
  116.3 0.0 copy-done.4
  116.3 0.7 fusion.1
  117.0 4.9 %collective-permute-start.8 = (f32[192,1152]{1,0:T(8,128)S(1)}, f32[192,1152]{1,0:T(8,128)S(1)}, u32[]{:S(2)}, u32[]{:S(2)}) collective-permute-start(f32[192,1152]{1,0:T(8,128)S(1)} %fusion.1), channel_id=1, source_target_pairs={{764,0},{0,4},{4,8},{8,12},{12,16},{16,20},{20,24},{24,28},{28,32}... | collective-permute-start | bytes 2654216 | tf_op jit(solution)/shard_map/ppermute | solution.py:15
  121.9 0.7 convolution_multiply_fusion.1
  122.6 33.0 %collective-permute-done.8 = f32[192,1152]{1,0:T(8,128)S(1)} collective-permute-done((f32[192,1152]{1,0:T(8,128)S(1)}, f32[192,1152]{1,0:T(8,128)S(1)}, u32[]{:S(2)}, u32[]{:S(2)}) %collective-permute-start.8) | collective-permute-done | bytes 884768 | tf_op jit(solution)/shard_map/ppermute | solution.py:15
  155.7 0.1 add.145
  155.8 5.9 %collective-permute-start.9 = (f32[192,1152]{1,0:T(8,128)S(1)}, f32[192,1152]{1,0:T(8,128)S(1)}, u32[]{:S(2)}, u32[]{:S(2)}) collective-permute-start(f32[192,1152]{1,0:T(8,128)S(1)} %add.145), channel_id=1, source_target_pairs={{764,0},{0,4},{4,8},{8,12},{12,16},{16,20},{20,24},{24,28},{28,32}... | collective-permute-start | bytes 2654216 | tf_op jit(solution)/shard_map/ppermute | solution.py:15
  161.7 0.7 convolution_multiply_fusion
  162.4 20.4 %collective-permute-done.9 = f32[192,1152]{1,0:T(8,128)S(1)} collective-permute-done((f32[192,1152]{1,0:T(8,128)S(1)}, f32[192,1152]{1,0:T(8,128)S(1)}, u32[]{:S(2)}, u32[]{:S(2)}) %collective-permute-start.9) | collective-permute-done | bytes 884768 | tf_op jit(solution)/shard_map/ppermute | solution.py:15
  182.8 0.1 add.146
  182.9 11.9 %collective-permute-start.10 = (f32[192,1152]{1,0:T(8,128)S(1)}, f32[192,1152]{1,0:T(8,128)S(1)}, u32[]{:S(2)}, u32[]{:S(2)}) collective-permute-start(f32[192,1152]{1,0:T(8,128)S(1)} %add.146), channel_id=1, source_target_pairs={{12,0},{16,4},{20,8},{24,12},{28,16},{32,20},{36,24},{40,28},{44,3... | collective-permute-start | bytes 2654216 | tf_op jit(solution)/shard_map/ppermute | solution.py:15
  194.8 2.2 collective-permute-start
  197.0 9.0 %collective-permute-done = f32[192]{0:T(256)S(1)} collective-permute-done((f32[192]{0:T(256)S(1)}, f32[192]{0:T(256)S(1)}, u32[]{:S(2)}, u32[]{:S(2)}) %collective-permute-start) | collective-permute-done | bytes 800 | tf_op jit(solution)/shard_map/ppermute | solution.py:15
  206.0 1.9 collective-permute-start.2
  207.9 9.3 %collective-permute-done.2 = f32[192]{0:T(256)S(1)} collective-permute-done((f32[192]{0:T(256)S(1)}, f32[192]{0:T(256)S(1)}, u32[]{:S(2)}, u32[]{:S(2)}) %collective-permute-start.2) | collective-permute-done | bytes 800 | tf_op jit(solution)/shard_map/ppermute | solution.py:15
  217.2 1.9 collective-permute-start.4
  219.1 9.3 %collective-permute-done.4 = f32[192]{0:T(256)S(1)} collective-permute-done((f32[192]{0:T(256)S(1)}, f32[192]{0:T(256)S(1)}, u32[]{:S(2)}, u32[]{:S(2)}) %collective-permute-start.4) | collective-permute-done | bytes 800 | tf_op jit(solution)/shard_map/ppermute | solution.py:15
  228.3 1.9 collective-permute-start.6
  230.3 5.9 %collective-permute-done.6 = f32[192]{0:T(256)S(1)} collective-permute-done((f32[192]{0:T(256)S(1)}, f32[192]{0:T(256)S(1)}, u32[]{:S(2)}, u32[]{:S(2)}) %collective-permute-start.6) | collective-permute-done | bytes 800 | tf_op jit(solution)/shard_map/ppermute | solution.py:15
  236.2 0.6 broadcast_multiply_fusion
  236.8 0.0 copy-start.1
  236.8 0.0 collective-permute-done.10
  236.8 0.3 multiply_reduce_fusion
  237.0 1.1 subtract_divide_fusion
  238.2 0.0 reduce-scatter.2.cloned.1.call-done
  238.2 0.0 copy-done.1
  238.2 0.0 copy-start.2
  238.2 1.5 multiply_reduce_fusion.1
  239.7 0.0 copy-done.2
  239.7 1.1 subtract_divide_fusion.1
  (6 shorter events, 0.0 us)
Async XLA Ops:
  7.2 3.3 %copy-start = (bf16[192,1152]{1,0:T(8,128)(2,1)S(1)}, bf16[192,1152]{1,0:T(8,128)(2,1)}, u32[]{:S(2)}) copy-start(bf16[192,1152]{1,0:T(8,128)(2,1)} %param.5) | copy-start | bytes 1327108
  7.2 58.0 %all-gather.2.cloned.1.call-start = ((), (), s32[]{:S(2)}) async-start(), calls=%async_computation.1 | async-start | bytes 2211840 | tf_op jit(solution)/shard_map/all_gather | solution.py:57
  10.4 227.8 %reduce-scatter.2.cloned.1.call-start = ((), (), s32[]{:S(2)}) async-start(), calls=%async_computation.2 | async-start | bytes 4423680 | tf_op jit(solution)/shard_map/reduce_scatter | solution.py:78
  10.8 27.1 %collective-permute-start.1 = (bf16[192,1152]{1,0:T(8,128)(2,1)S(1)}, bf16[192,1152]{1,0:T(8,128)(2,1)S(1)}, u32[]{:S(2)}, u32[]{:S(2)}) collective-permute-start(bf16[192,1152]{1,0:T(8,128)(2,1)S(1)} %fusion.21), channel_id=1, source_target_pairs={{764,0},{0,4},{4,8},{8,12},{12,16},{16,20},{20,24},{24,28},{28,32}... | collective-permute-start | bytes 1327112 | tf_op jit(solution)/shard_map/ppermute | solution.py:15
  37.9 21.3 %collective-permute-start.3 = (bf16[192,1152]{1,0:T(8,128)(2,1)S(1)}, bf16[192,1152]{1,0:T(8,128)(2,1)}, u32[]{:S(2)}, u32[]{:S(2)}) collective-permute-start(bf16[192,1152]{1,0:T(8,128)(2,1)S(1)} %collective-permute-done.1), channel_id=1, source_target_pairs={{764,0},{0,4},{4,8},{8,12},{12,16},{16,20},{20,24},{24,28},{28,32}... | collective-permute-start | bytes 1327112 | tf_op jit(solution)/shard_map/ppermute | solution.py:15
  59.2 18.9 %collective-permute-start.5 = (bf16[192,1152]{1,0:T(8,128)(2,1)}, bf16[192,1152]{1,0:T(8,128)(2,1)}, u32[]{:S(2)}, u32[]{:S(2)}) collective-permute-start(bf16[192,1152]{1,0:T(8,128)(2,1)} %collective-permute-done.3), channel_id=1, source_target_pairs={{764,0},{0,4},{4,8},{8,12},{12,16},{16,20},{20,24},{24,28},{28,32}... | collective-permute-start | bytes 1327112 | tf_op jit(solution)/shard_map/ppermute | solution.py:15
  65.2 2.6 %copy-start.3 = (bf16[768,1152]{1,0:T(8,128)(2,1)S(1)}, bf16[768,1152]{1,0:T(8,128)(2,1)}, u32[]{:S(2)}) copy-start(bf16[768,1152]{1,0:T(8,128)(2,1)} %all-gather.2.cloned.1.call-done) | copy-start | bytes 5308420
  86.7 29.6 %copy-start.4 = (bf16[768,1152]{1,0:T(8,128)(2,1)S(1)}, bf16[768,1152]{1,0:T(8,128)(2,1)}, u32[]{:S(2)}) copy-start(bf16[768,1152]{1,0:T(8,128)(2,1)} %all-gather.2.cloned.1.call-done) | copy-start | bytes 5308420
  89.1 27.2 %collective-permute-start.7 = (f32[192,1152]{1,0:T(8,128)S(1)}, f32[192,1152]{1,0:T(8,128)S(1)}, u32[]{:S(2)}, u32[]{:S(2)}) collective-permute-start(f32[192,1152]{1,0:T(8,128)S(1)} %convolution_multiply_fusion.3), channel_id=1, source_target_pairs={{764,0},{0,4},{4,8},{8,12},{12,16},{16,20},{20,24},{24,28},{28,32}... | collective-permute-start | bytes 2654216 | tf_op jit(solution)/shard_map/ppermute | solution.py:15
  117.0 38.7 %collective-permute-start.8 = (f32[192,1152]{1,0:T(8,128)S(1)}, f32[192,1152]{1,0:T(8,128)S(1)}, u32[]{:S(2)}, u32[]{:S(2)}) collective-permute-start(f32[192,1152]{1,0:T(8,128)S(1)} %fusion.1), channel_id=1, source_target_pairs={{764,0},{0,4},{4,8},{8,12},{12,16},{16,20},{20,24},{24,28},{28,32}... | collective-permute-start | bytes 2654216 | tf_op jit(solution)/shard_map/ppermute | solution.py:15
  155.8 27.0 %collective-permute-start.9 = (f32[192,1152]{1,0:T(8,128)S(1)}, f32[192,1152]{1,0:T(8,128)S(1)}, u32[]{:S(2)}, u32[]{:S(2)}) collective-permute-start(f32[192,1152]{1,0:T(8,128)S(1)} %add.145), channel_id=1, source_target_pairs={{764,0},{0,4},{4,8},{8,12},{12,16},{16,20},{20,24},{24,28},{28,32}... | collective-permute-start | bytes 2654216 | tf_op jit(solution)/shard_map/ppermute | solution.py:15
  182.9 53.9 %collective-permute-start.10 = (f32[192,1152]{1,0:T(8,128)S(1)}, f32[192,1152]{1,0:T(8,128)S(1)}, u32[]{:S(2)}, u32[]{:S(2)}) collective-permute-start(f32[192,1152]{1,0:T(8,128)S(1)} %add.146), channel_id=1, source_target_pairs={{12,0},{16,4},{20,8},{24,12},{28,16},{32,20},{36,24},{40,28},{44,3... | collective-permute-start | bytes 2654216 | tf_op jit(solution)/shard_map/ppermute | solution.py:15
  194.8 11.2 %collective-permute-start = (f32[192]{0:T(256)S(1)}, f32[192]{0:T(256)S(1)}, u32[]{:S(2)}, u32[]{:S(2)}) collective-permute-start(f32[192]{0:T(256)S(1)} %get-tuple-element.3), channel_id=1, source_target_pairs={{764,0},{0,4},{4,8},{8,12},{12,16},{16,20},{20,24},{24,28},{28,32}... | collective-permute-start | bytes 2312 | tf_op jit(solution)/shard_map/ppermute | solution.py:15
  206.0 11.2 %collective-permute-start.2 = (f32[192]{0:T(256)S(1)}, f32[192]{0:T(256)S(1)}, u32[]{:S(2)}, u32[]{:S(2)}) collective-permute-start(f32[192]{0:T(256)S(1)} %add.128), channel_id=1, source_target_pairs={{764,0},{0,4},{4,8},{8,12},{12,16},{16,20},{20,24},{24,28},{28,32}... | collective-permute-start | bytes 2312 | tf_op jit(solution)/shard_map/ppermute | solution.py:15
  217.2 11.2 %collective-permute-start.4 = (f32[192]{0:T(256)S(1)}, f32[192]{0:T(256)S(1)}, u32[]{:S(2)}, u32[]{:S(2)}) collective-permute-start(f32[192]{0:T(256)S(1)} %add.132), channel_id=1, source_target_pairs={{764,0},{0,4},{4,8},{8,12},{12,16},{16,20},{20,24},{24,28},{28,32}... | collective-permute-start | bytes 2312 | tf_op jit(solution)/shard_map/ppermute | solution.py:15
  228.3 7.9 %collective-permute-start.6 = (f32[192]{0:T(256)S(1)}, f32[192]{0:T(256)S(1)}, u32[]{:S(2)}, u32[]{:S(2)}) collective-permute-start(f32[192]{0:T(256)S(1)} %add.136), channel_id=1, source_target_pairs={{12,0},{16,4},{20,8},{24,12},{28,16},{32,20},{36,24},{40,28},{44,3... | collective-permute-start | bytes 2312 | tf_op jit(solution)/shard_map/ppermute | solution.py:15
  236.8 1.4 copy-start.1
  238.2 1.5 copy-start.2
Sparse Core Ops, SparseCore 0:
  11.0 50.2 all-gather.1
  86.9 69.7 reduce-scatter.1
where the time goes:
time: 248 us
  waiting for transfers between devices  159 us (64%)
  starting transfers between devices  45.5 us (18%)
  matrix products  19.6 us (8%)
  between operations  15.7 us (6%)
  other arithmetic  8.33 us (3%)
    ppermute x11, waiting for transfers between devices, shifted(): return lax.ppermute(block, axis, route)  158 us
    ppermute x11, starting transfers between devices, shifted(): return lax.ppermute(block, axis, route)  45.4 us
    dot_general x4, matrix products, pair_tiles(): jnp.einsum('gd,rd->gr', image_group, text_block, preferred_element_type=j...  7.68 us
    dot_general x4, matrix products, pair_tiles(): jnp.einsum('gr,rd->gd', slopes, text_block, preferred_element_type=jnp.fl...  7.56 us
  transfers between devices with their start and end apart: 13, of which 10 were waited for; matrix products, arithmetic and copies ran while one was open for 5% of the time, Pallas kernels for 0%

commit v1 on v0

v1 whole, which is shorter than its diff:
```python
import functools

import jax
import jax.numpy as jnp
from jax import lax
from jax.experimental import pallas as pl
from jax.experimental.pallas import tpu as pltpu

EPSILON = 1e-06
VISITS = 4
TAIL = 16
AXES = ("img", "txt")
F32, BF16 = jnp.float32, jnp.bfloat16
VMEM = pl.BlockSpec(memory_space=pltpu.VMEM)
SMEM = pl.BlockSpec(memory_space=pltpu.SMEM)
PARAMS = pltpu.CompilerParams(vmem_limit_bytes=48 * 1024 * 1024)


def moved(value, lines, up=0, flip=0, other=0, odd_only=False):
    route = []
    for line in range(lines):
        for x in range(4):
            if odd_only and x < 2:
                continue
            for c in range(2):
                here = line * 8 + x * 2 + c
                there = (line + up) % lines * 8 + (x ^ flip) * 2 + (c ^ other)
                route.append((here, there))
    return lax.ppermute(value, AXES, route)


def unit_of(ref):
    wide = ref[...].astype(F32)
    length = jnp.sqrt(jnp.sum(wide * wide, axis=-1, keepdims=True) + EPSILON)
    return wide / length, length


def norm_kernel(images, texts, image_half, text_half):
    image_half[...] = unit_of(images)[0].astype(BF16)
    text_half[...] = unit_of(texts)[0].astype(BF16)


def tail_of(loss):
    rows = lax.broadcasted_iota(jnp.int32, (TAIL, loss.shape[1]), 0)
    wide = jnp.broadcast_to(loss, rows.shape)
    high = wide.astype(BF16).astype(F32)
    return jnp.where(rows == 0, high, jnp.where(rows == 1, wide - high, 0.0)).astype(BF16)


def pairs_kernel(
    scalars, odd, i0, i1, i2, i3, ao, as_, bo, bs, co, cs,
    image_own, image_1, image_2, image_3, text_own, text_send, loss_own,
    ih, tt, p, sums,
):
    r, width = i0.shape
    n = 2 * r
    temper, bias = scalars[0], scalars[1]
    for k, ref in enumerate((i0, i1, i2, i3, )):
        ih[pl.ds(k * r, r), :] = ref[...]
    for k, ref in enumerate((ao, as_, bo, bs)):
        tt[pl.ds(k * r, r), :] = ref[...]

    @pl.when(odd[0] == 0)
    def _():
        tt[pl.ds(2 * n, r), :] = ao[...]
        tt[pl.ds(2 * n + r, r), :] = as_[...]

    @pl.when(odd[0] != 0)
    def _():
        tt[pl.ds(2 * n, r), :] = co[...]
        tt[pl.ds(2 * n + r, r), :] = cs[...]

    sums[...] = jnp.zeros_like(sums)
    step = 2 * n // 3
    for half in range(2):
        for piece in range(3):
            at = half * n + piece * step
            logits = bias + temper * lax.dot_general(
                ih[pl.ds(half * n, n), :],
                tt[pl.ds(at, step), :],
                (((1,), (1,)), ((), ())),
                preferred_element_type=F32,
            )
            if at < r:
                rows = lax.broadcasted_iota(jnp.int32, logits.shape, 0)
                cols = lax.broadcasted_iota(jnp.int32, logits.shape, 1) + at
                positive = (rows == cols) & (cols < r)
                margin = jnp.where(positive, -logits, logits)
            else:
                margin = logits
            grown = jnp.exp(margin)
            whole = 1.0 + grown
            slope = grown / whole
            losses = jnp.where(
                grown < 0.00390625,
                grown * (1.0 - grown * (0.5 - grown * (1.0 / 3.0))),
                jnp.log(whole),
            )
            if at < r:
                slope = jnp.where(positive, -slope, slope)
            p[pl.ds(half * n, n), pl.ds(at, step)] = slope.astype(BF16)
            sums[:, pl.ds(at, step)] += jnp.sum(losses.reshape(n // 8, 8, step), axis=0)

    nn = (((1,), (0,)), ((), ()))
    tn = (((0,), (0,)), ((), ()))

    def text_part(place, first, rows, at):
        part = lax.dot_general(
            p[pl.ds(first, rows), pl.ds(at, n)],
            ih[pl.ds(first, rows), :],
            tn,
            preferred_element_type=F32,
        )
        text_own[place] = part[:r]
        text_send[place, pl.ds(0, r), :] = part[r:].astype(BF16)
        loss = jnp.sum(sums[:, pl.ds(at, n)], axis=0, keepdims=True)
        loss = jnp.broadcast_to(loss, (8, n))
        loss_own[place] = loss
        text_send[place, pl.ds(r, TAIL), :] = jnp.zeros((TAIL, width), BF16)
        text_send[place, pl.ds(r, TAIL), pl.ds(0, n)] = tail_of(pltpu.roll(loss, r, 1)[:1])

    text_part(0, 0, 2 * n, n)
    text_part(1, n, n, 2 * n)
    text_part(2, 0, n, 0)
    other = lax.dot_general(
        p[pl.ds(n, n), pl.ds(n, 2 * n)], tt[pl.ds(n, 2 * n), :], nn, preferred_element_type=F32
    )
    image_2[...] = other[:r].astype(BF16)
    image_3[...] = other[r:].astype(BF16)
    own = lax.dot_general(
        p[pl.ds(0, n), pl.ds(0, 2 * n)], tt[pl.ds(0, 2 * n), :], nn, preferred_element_type=F32
    )
    image_own[...] = own[:r]
    image_1[...] = own[r:].astype(BF16)


def join_kernel(text_own, got, loss_own, b_back, c_back):
    r = text_own.shape[1]
    for place, out in ((0, b_back), (1, c_back)):
        out[pl.ds(0, r), :] = (text_own[place] + got[place, pl.ds(0, r), :].astype(F32)).astype(BF16)
        tail = got[place, pl.ds(r, TAIL), :].astype(F32)
        n = loss_own.shape[2]
        loss = loss_own[place][:1] + tail[0:1, :n] + tail[1:2, :n]
        out[pl.ds(r, TAIL), :] = jnp.zeros((TAIL, out.shape[1]), BF16)
        out[pl.ds(r, TAIL), pl.ds(0, n)] = tail_of(loss)


def tangent(total, ref, temper):
    unit, length = unit_of(ref)
    total = temper * total
    return (total - unit * jnp.sum(unit * total, axis=-1, keepdims=True)) / length


def image_end_kernel(scalars, images, own, a, b, c, grad):
    total = own[...] + a[...].astype(F32) + b[...].astype(F32) + c[...].astype(F32)
    grad[...] = tangent(total, images, scalars[0])


def text_end_kernel(scalars, odd, texts, own, got, loss_own, b_got, c_got, grad, loss):
    r = texts.shape[0]
    n = loss_own.shape[2]
    even = odd[0] == 0

    def here(place):
        rows = own[place] + got[place, pl.ds(0, r), :].astype(F32)
        tail = got[place, pl.ds(r, TAIL), :].astype(F32)
        return rows, loss_own[place][:1] + tail[0:1, :n] + tail[1:2, :n]

    total, sums = here(2)
    more, more_sums = here(1)
    total = total + jnp.where(even, more, 0.0)
    sums = sums + jnp.where(even, more_sums, 0.0)
    for ref in (b_got, c_got):
        total = total + ref[pl.ds(0, r), :].astype(F32)
        tail = ref[pl.ds(r, TAIL), :].astype(F32)
        sums = sums + tail[0:1, :n] + tail[1:2, :n]
    grad[...] = tangent(total, texts, scalars[0])
    loss[...] = jnp.broadcast_to(sums / (VISITS * 4 * r), loss.shape)


def on_device(lines, images, texts, log_temp, bias):
    r, width = images.shape
    n = 2 * r
    shape = jax.ShapeDtypeStruct
    send = functools.partial(moved, lines=lines)
    scalars = jnp.stack([jnp.exp(log_temp), bias])
    odd = jnp.reshape(lax.axis_index("img") % 2, (1,)).astype(jnp.int32)
    half = shape((r, width), BF16)
    image_half, text_half = pl.pallas_call(
        norm_kernel, out_shape=(half, half), in_specs=[VMEM] * 2, out_specs=(VMEM,) * 2, compiler_params=PARAMS
    )(images, texts)

    text_sib = send(text_half, other=1)
    image_1 = send(image_half, flip=1)
    image_3 = send(image_half, flip=3)
    b_own = send(text_half, up=1)
    image_2 = send(image_half, flip=2)
    c_own = send(text_half, up=2, odd_only=True)
    b_sib = send(b_own, other=1)
    c_sib = send(c_own, other=1)

    long = shape((r, width), F32)
    sent = shape((3, r + TAIL, width), BF16)
    own, out_1, out_2, out_3, text_own, text_send, loss_own = pl.pallas_call(
        pairs_kernel,
        out_shape=(long, half, half, half, shape((3, r, width), F32), sent, shape((3, 8, n), F32)),
        in_specs=[SMEM] * 2 + [VMEM] * 10,
        out_specs=(VMEM,) * 7,
        scratch_shapes=[
            pltpu.VMEM((2 * n, width), BF16),
            pltpu.VMEM((3 * n, width), BF16),
            pltpu.VMEM((2 * n, 3 * n), BF16),
            pltpu.VMEM((8, 3 * n), F32),
        ],
        compiler_params=PARAMS,
    )(scalars, odd, image_half, image_1, image_2, image_3, text_half, text_sib, b_own, b_sib, c_own, c_sib)

    got = send(text_send, other=1)
    back_2 = send(out_2, flip=2)
    back_3 = send(out_3, flip=3)
    back_1 = send(out_1, flip=1)
    back = shape((r + TAIL, width), BF16)
    b_back, c_back = pl.pallas_call(
        join_kernel, out_shape=(back, back), in_specs=[VMEM] * 3, out_specs=(VMEM,) * 2, compiler_params=PARAMS
    )(text_own, got, loss_own)
    c_got = send(c_back, up=-2, odd_only=True)
    b_got = send(b_back, up=-1)
    image_grad = pl.pallas_call(
        image_end_kernel, out_shape=long, in_specs=[SMEM] + [VMEM] * 5, out_specs=VMEM, compiler_params=PARAMS
    )(scalars, images, own, back_1, back_2, back_3)
    text_grad, loss = pl.pallas_call(
        text_end_kernel,
        out_shape=(long, shape((8, n), F32)),
        in_specs=[SMEM] * 2 + [VMEM] * 6,
        out_specs=(VMEM,) * 2,
        compiler_params=PARAMS,
    )(scalars, odd, texts, text_own, got, loss_own, b_got, c_got)
    return loss[0, :r], image_grad, text_grad


def solution(mesh):
    from jax.sharding import PartitionSpec as P

    lines = mesh.shape["img"] // 2
    rows = P(AXES, None)
    return jax.shard_map(
        functools.partial(on_device, lines),
        mesh=mesh,
        in_specs=(rows, rows, P(), P()),
        out_specs=(P(AXES), rows, rows),
        check_vma=False,
    )
```

time: 248 us -> 115 us (0.46)
  the two profiles are of different devices: /device:TPU:32 before, /device:TPU:1 now
where the time goes in v1:
time: 115 us; the launch traced here: 114 us
  starting transfers between devices  70.3 us (61%)
  waiting for transfers between devices  24.2 us (21%)
  Pallas kernels  12.9 us (11%)
  local copies, waits for them, and re-layouts  4.35 us (4%)
  between operations  2.18 us (2%)
    ppermute x14, starting transfers between devices, moved(): return lax.ppermute(value, AXES, route)  70.3 us
    ppermute x14, waiting for transfers between devices, moved(): return lax.ppermute(value, AXES, route)  24.2 us
    pallas_call x1, Pallas kernels, on_device(): pl.pallas_call(pairs_kernel, out_shape=(long, half, half, half, shape((3,...  8.28 us
    unnamed x14, local copies, waits for them, and re-layouts  3.79 us
  transfers between devices with their start and end apart: 14, of which 4 were waited for; matrix products, arithmetic and copies ran while one was open for 0% of the time, Pallas kernels for 2%

profile of v1, /device:TPU:1, one launch (start us, length us, event | category | flops | bytes accessed | tf_op | source)
XLA Modules:
  0.0 113.9 jit_solution(11128860542962265848)
XLA Ops:
  0.6 0.0 copy-start.2
  0.6 1.0 copy-done.2
  1.6 0.0 copy-start.4
  1.6 1.0 copy-done.4
  2.7 0.3 shard_map.67
  3.0 5.2 %collective-permute-start.2 = (bf16[192,1152]{1,0:T(8,128)(2,1)S(1)}, bf16[192,1152]{1,0:T(8,128)(2,1)S(1)}, u32[]{:S(2)}, u32[]{:S(2)}) collective-permute-start(bf16[192,1152]{1,0:T(8,128)(2,1)S(1)} %get-tuple-element.16.i0), channel_id=1, source_target_pairs={{0,6},{1,7},{2,4},{3,5},{4,2},{5,3},{6,0},{7,1},{8,14},{9,15},{10,... | collective-permute-start | bytes 1327112 | tf_op jit(solution)/shard_map/ppermute | solution.py:29
  8.2 0.7 collective-permute-start.6
  8.9 4.0 %collective-permute-start.4 = (bf16[192,1152]{1,0:T(8,128)(2,1)S(1)}, bf16[192,1152]{1,0:T(8,128)(2,1)S(1)}, u32[]{:S(2)}, u32[]{:S(2)}) collective-permute-start(bf16[192,1152]{1,0:T(8,128)(2,1)S(1)} %get-tuple-element.17.ao), channel_id=1, source_target_pairs={{0,8},{1,9},{2,10},{3,11},{4,12},{5,13},{6,14},{7,15},{8,16},{9,17... | collective-permute-start | bytes 1327112 | tf_op jit(solution)/shard_map/ppermute | solution.py:29
  12.9 7.5 %collective-permute-start.1 = (bf16[192,1152]{1,0:T(8,128)(2,1)S(1)}, bf16[192,1152]{1,0:T(8,128)(2,1)S(1)}, u32[]{:S(2)}, u32[]{:S(2)}) collective-permute-start(bf16[192,1152]{1,0:T(8,128)(2,1)S(1)} %get-tuple-element.16.i0), channel_id=1, source_target_pairs={{0,4},{1,5},{2,6},{3,7},{4,0},{5,1},{6,2},{7,3},{8,12},{9,13},{10,... | collective-permute-start | bytes 1327112 | tf_op jit(solution)/shard_map/ppermute | solution.py:29
  20.5 2.2 %collective-permute-start = (bf16[192,1152]{1,0:T(8,128)(2,1)S(1)}, bf16[192,1152]{1,0:T(8,128)(2,1)S(1)}, u32[]{:S(2)}, u32[]{:S(2)}) collective-permute-start(bf16[192,1152]{1,0:T(8,128)(2,1)S(1)} %get-tuple-element.16.i0), channel_id=1, source_target_pairs={{0,2},{1,3},{2,0},{3,1},{4,6},{5,7},{6,4},{7,5},{8,10},{9,11},{10,... | collective-permute-start | bytes 1327112 | tf_op jit(solution)/shard_map/ppermute | solution.py:29
  22.6 0.0 collective-permute-done.2.i3
  22.7 13.5 %collective-permute-start.3 = (bf16[192,1152]{1,0:T(8,128)(2,1)S(1)}, bf16[192,1152]{1,0:T(8,128)(2,1)S(1)}, u32[]{:S(2)}, u32[]{:S(2)}) collective-permute-start(bf16[192,1152]{1,0:T(8,128)(2,1)S(1)} %get-tuple-element.17.ao), channel_id=1, source_target_pairs={{0,1},{1,0},{2,3},{3,2},{4,5},{5,4},{6,7},{7,6},{8,9},{9,8},{10,11... | collective-permute-start | bytes 1327112 | tf_op jit(solution)/shard_map/ppermute | solution.py:29
  36.1 0.0 collective-permute-done.6.co
  36.1 1.9 %collective-permute-start.7 = (bf16[192,1152]{1,0:T(8,128)(2,1)S(1)}, bf16[192,1152]{1,0:T(8,128)(2,1)}, u32[]{:S(2)}, u32[]{:S(2)}) collective-permute-start(bf16[192,1152]{1,0:T(8,128)(2,1)S(1)} %collective-permute-done.6.co), channel_id=1, source_target_pairs={{0,1},{1,0},{2,3},{3,2},{4,5},{5,4},{6,7},{7,6},{8,9},{9,8},{10,11... | collective-permute-start | bytes 1327112 | tf_op jit(solution)/shard_map/ppermute | solution.py:29
  38.1 0.0 collective-permute-done.4.bo
  38.1 2.4 %collective-permute-start.5 = (bf16[192,1152]{1,0:T(8,128)(2,1)S(1)}, bf16[192,1152]{1,0:T(8,128)(2,1)}, u32[]{:S(2)}, u32[]{:S(2)}) collective-permute-start(bf16[192,1152]{1,0:T(8,128)(2,1)S(1)} %collective-permute-done.4.bo), channel_id=1, source_target_pairs={{0,1},{1,0},{2,3},{3,2},{4,5},{5,4},{6,7},{7,6},{8,9},{9,8},{10,11... | collective-permute-start | bytes 1327112 | tf_op jit(solution)/shard_map/ppermute | solution.py:29
  41.8 0.1 pad_maximum_fusion.scalars
  41.9 0.0 collective-permute-done.1.i2
  41.9 0.0 collective-permute-done.i1
  41.9 0.0 collective-permute-done.3.as_
  41.9 0.0 collective-permute-done.7.cs
  41.9 0.1 collective-permute-done.5.bs
  42.0 8.3 %shard_map.68 = (f32[192,1152]{1,0:T(8,128)}, bf16[192,1152]{1,0:T(8,128)(2,1)S(1)}, bf16[192,1152]{1,0:T(8,128)(2,1)S(1)}, bf16[192,1152]{1,0:T(8,128)(2,1)S(1)...) custom-call(f32[2]{0:T(128)S(1)} %pad_maximum_fusion.scalars, s32[1]{0:T(128)} %bitcast.2.odd, ...), custom_call_target="tpu_custom_call" | custom-call | tf_op jit(solution)/shard_map/pallas_call | solution.py:204
  50.3 2.3 %collective-permute-start.8 = (bf16[3,208,1152]{2,1,0:T(8,128)(2,1)}, bf16[3,208,1152]{2,1,0:T(8,128)(2,1)S(1)}, u32[]{:S(2)}, u32[]{:S(2)}) collective-permute-start(bf16[3,208,1152]{2,1,0:T(8,128)(2,1)} %get-tuple-element.19), channel_id=1, source_target_pairs={{0,1},{1,0},{2,3},{3,2},{4,5},{5,4},{6,7},{7,6},{8,9},{9,8},{10,11... | collective-permute-start | bytes 4313096 | tf_op jit(solution)/shard_map/ppermute | solution.py:29
  52.6 3.0 %collective-permute-done.8.got = bf16[3,208,1152]{2,1,0:T(8,128)(2,1)S(1)} collective-permute-done((bf16[3,208,1152]{2,1,0:T(8,128)(2,1)}, bf16[3,208,1152]{2,1,0:T(8,128)(2,1)S(1)}, u32[]{:S(2)}, u32[]{:S(2)}) %collective-permute-start.8) | collective-permute-done | bytes 1437728 | tf_op jit(solution)/shard_map/ppermute | solution.py:29
  55.6 0.0 copy-start
  55.6 1.7 %copy-done = f32[3,192,1152]{2,1,0:T(8,128)S(1)} copy-done((f32[3,192,1152]{2,1,0:T(8,128)S(1)}, f32[3,192,1152]{2,1,0:T(8,128)}, u32[]{:S(2)}) %copy-start) | copy-done | bytes 2654232
  57.4 0.0 copy-start.5
  57.4 0.0 copy-start.6
  57.4 0.2 shard_map.69
  57.6 12.1 %collective-permute-start.9 = (bf16[208,1152]{1,0:T(8,128)(2,1)S(1)}, bf16[208,1152]{1,0:T(8,128)(2,1)S(1)}, u32[]{:S(2)}, u32[]{:S(2)}) collective-permute-start(bf16[208,1152]{1,0:T(8,128)(2,1)S(1)} %get-tuple-element.21), channel_id=1, source_target_pairs={{0,760},{1,761},{2,762},{3,763},{4,764},{5,765},{6,766},{7,767},{8... | collective-permute-start | bytes 1437704 | tf_op jit(solution)/shard_map/ppermute | solution.py:29
  69.7 0.7 collective-permute-start.10
  70.4 1.9 %collective-permute-start.11 = (bf16[192,1152]{1,0:T(8,128)(2,1)S(1)}, bf16[192,1152]{1,0:T(8,128)(2,1)S(1)}, u32[]{:S(2)}, u32[]{:S(2)}) collective-permute-start(bf16[192,1152]{1,0:T(8,128)(2,1)S(1)} %get-tuple-element.25), channel_id=1, source_target_pairs={{0,2},{1,3},{2,0},{3,1},{4,6},{5,7},{6,4},{7,5},{8,10},{9,11},{10,... | collective-permute-start | bytes 1327112 | tf_op jit(solution)/shard_map/ppermute | solution.py:29
  72.3 14.0 %collective-permute-start.12 = (bf16[192,1152]{1,0:T(8,128)(2,1)S(1)}, bf16[192,1152]{1,0:T(8,128)(2,1)S(1)}, u32[]{:S(2)}, u32[]{:S(2)}) collective-permute-start(bf16[192,1152]{1,0:T(8,128)(2,1)S(1)} %get-tuple-element.26), channel_id=1, source_target_pairs={{0,4},{1,5},{2,6},{3,7},{4,0},{5,1},{6,2},{7,3},{8,12},{9,13},{10,... | collective-permute-start | bytes 1327112 | tf_op jit(solution)/shard_map/ppermute | solution.py:29
  86.3 1.9 %collective-permute-start.13 = (bf16[192,1152]{1,0:T(8,128)(2,1)S(1)}, bf16[192,1152]{1,0:T(8,128)(2,1)S(1)}, u32[]{:S(2)}, u32[]{:S(2)}) collective-permute-start(bf16[192,1152]{1,0:T(8,128)(2,1)S(1)} %get-tuple-element.27), channel_id=1, source_target_pairs={{0,6},{1,7},{2,4},{3,5},{4,2},{5,3},{6,0},{7,1},{8,14},{9,15},{10,... | collective-permute-start | bytes 1327112 | tf_op jit(solution)/shard_map/ppermute | solution.py:29
  88.2 0.0 collective-permute-done.11.a
  88.2 14.9 %collective-permute-done.12.b = bf16[192,1152]{1,0:T(8,128)(2,1)S(1)} collective-permute-done((bf16[192,1152]{1,0:T(8,128)(2,1)S(1)}, bf16[192,1152]{1,0:T(8,128)(2,1)S(1)}, u32[]{:S(2)}, u32[]{:S(2)}) %collective-permute-start.12) | collective-permute-done | bytes 442400 | tf_op jit(solution)/shard_map/ppermute | solution.py:29
  103.2 6.1 %collective-permute-done.13.c = bf16[192,1152]{1,0:T(8,128)(2,1)S(1)} collective-permute-done((bf16[192,1152]{1,0:T(8,128)(2,1)S(1)}, bf16[192,1152]{1,0:T(8,128)(2,1)S(1)}, u32[]{:S(2)}, u32[]{:S(2)}) %collective-permute-start.13) | collective-permute-done | bytes 442400 | tf_op jit(solution)/shard_map/ppermute | solution.py:29
  109.3 0.0 copy-done.5
  109.3 0.0 copy-done.6
  109.3 0.0 copy-start.1
  109.3 0.0 copy-start.3
  109.3 2.0 %shard_map.71 = f32[192,1152]{1,0:T(8,128)} custom-call(f32[2]{0:T(128)S(1)} %pad_maximum_fusion.scalars, bf16[192,1152]{1,0:T(8,128)(2,1)S(1)} %copy-done.5, f32[192,1152]{1,0:T(8,128)S(1)} %copy-done.6, bf16[192,1152]{1,0:T(8,128)(2,1)S(1)} %collective-permute-done.11.a, bf16[192,1152]{1,0:T(8,128)(2,1)S(1)} %collective-permute-done.12.b, ...), custom_call_target="tpu_custom_call" | custom-call | tf_op jit(solution)/shard_map/pallas_call | solution.py:228
  111.2 0.0 collective-permute-done.9.b_got
  111.2 0.0 collective-permute-done.10.c_got
  111.2 0.0 copy-done.1
  111.3 0.0 copy-done.3
  111.3 2.1 %shard_map.70 = (f32[192,1152]{1,0:T(8,128)}, f32[8,384]{1,0:T(8,128)S(1)}) custom-call(f32[2]{0:T(128)S(1)} %pad_maximum_fusion.scalars, s32[1]{0:T(128)} %bitcast.2.odd, bf16[192,1152]{1,0:T(8,128)(2,1)S(1)} %copy-done.3, f32[3,192,1152]{2,1,0:T(8,128)S(1)} %copy-done.1, bf16[3,208,1152]{2,1,0:T(8,128)(2,1)S(1)} %collective-permute-done.8.got, ...), custom_call_target="tpu_custom_call" | custom-call | tf_op jit(solution)/shard_map/pallas_call | solution.py:231
  113.3 0.6 slice.3
Async XLA Ops:
  0.6 1.0 copy-start.2
  1.6 1.0 copy-start.4
  3.0 19.7 %collective-permute-start.2 = (bf16[192,1152]{1,0:T(8,128)(2,1)S(1)}, bf16[192,1152]{1,0:T(8,128)(2,1)S(1)}, u32[]{:S(2)}, u32[]{:S(2)}) collective-permute-start(bf16[192,1152]{1,0:T(8,128)(2,1)S(1)} %get-tuple-element.16.i0), channel_id=1, source_target_pairs={{0,6},{1,7},{2,4},{3,5},{4,2},{5,3},{6,0},{7,1},{8,14},{9,15},{10,... | collective-permute-start | bytes 1327112 | tf_op jit(solution)/shard_map/ppermute | solution.py:29
  8.2 27.9 %collective-permute-start.6 = (bf16[192,1152]{1,0:T(8,128)(2,1)S(1)}, bf16[192,1152]{1,0:T(8,128)(2,1)S(1)}, u32[]{:S(2)}, u32[]{:S(2)}) collective-permute-start(bf16[192,1152]{1,0:T(8,128)(2,1)S(1)} %get-tuple-element.17.ao), channel_id=1, source_target_pairs={{4,20},{5,21},{6,22},{7,23},{12,28},{13,29},{14,30},{15,31},{20,36... | collective-permute-start | bytes 1327112 | tf_op jit(solution)/shard_map/ppermute | solution.py:29
  8.9 29.2 %collective-permute-start.4 = (bf16[192,1152]{1,0:T(8,128)(2,1)S(1)}, bf16[192,1152]{1,0:T(8,128)(2,1)S(1)}, u32[]{:S(2)}, u32[]{:S(2)}) collective-permute-start(bf16[192,1152]{1,0:T(8,128)(2,1)S(1)} %get-tuple-element.17.ao), channel_id=1, source_target_pairs={{0,8},{1,9},{2,10},{3,11},{4,12},{5,13},{6,14},{7,15},{8,16},{9,17... | collective-permute-start | bytes 1327112 | tf_op jit(solution)/shard_map/ppermute | solution.py:29
  12.9 29.0 %collective-permute-start.1 = (bf16[192,1152]{1,0:T(8,128)(2,1)S(1)}, bf16[192,1152]{1,0:T(8,128)(2,1)S(1)}, u32[]{:S(2)}, u32[]{:S(2)}) collective-permute-start(bf16[192,1152]{1,0:T(8,128)(2,1)S(1)} %get-tuple-element.16.i0), channel_id=1, source_target_pairs={{0,4},{1,5},{2,6},{3,7},{4,0},{5,1},{6,2},{7,3},{8,12},{9,13},{10,... | collective-permute-start | bytes 1327112 | tf_op jit(solution)/shard_map/ppermute | solution.py:29
  20.5 21.4 %collective-permute-start = (bf16[192,1152]{1,0:T(8,128)(2,1)S(1)}, bf16[192,1152]{1,0:T(8,128)(2,1)S(1)}, u32[]{:S(2)}, u32[]{:S(2)}) collective-permute-start(bf16[192,1152]{1,0:T(8,128)(2,1)S(1)} %get-tuple-element.16.i0), channel_id=1, source_target_pairs={{0,2},{1,3},{2,0},{3,1},{4,6},{5,7},{6,4},{7,5},{8,10},{9,11},{10,... | collective-permute-start | bytes 1327112 | tf_op jit(solution)/shard_map/ppermute | solution.py:29
  22.7 19.3 %collective-permute-start.3 = (bf16[192,1152]{1,0:T(8,128)(2,1)S(1)}, bf16[192,1152]{1,0:T(8,128)(2,1)S(1)}, u32[]{:S(2)}, u32[]{:S(2)}) collective-permute-start(bf16[192,1152]{1,0:T(8,128)(2,1)S(1)} %get-tuple-element.17.ao), channel_id=1, source_target_pairs={{0,1},{1,0},{2,3},{3,2},{4,5},{5,4},{6,7},{7,6},{8,9},{9,8},{10,11... | collective-permute-start | bytes 1327112 | tf_op jit(solution)/shard_map/ppermute | solution.py:29
  36.1 5.8 %collective-permute-start.7 = (bf16[192,1152]{1,0:T(8,128)(2,1)S(1)}, bf16[192,1152]{1,0:T(8,128)(2,1)}, u32[]{:S(2)}, u32[]{:S(2)}) collective-permute-start(bf16[192,1152]{1,0:T(8,128)(2,1)S(1)} %collective-permute-done.6.co), channel_id=1, source_target_pairs={{0,1},{1,0},{2,3},{3,2},{4,5},{5,4},{6,7},{7,6},{8,9},{9,8},{10,11... | collective-permute-start | bytes 1327112 | tf_op jit(solution)/shard_map/ppermute | solution.py:29
  38.1 3.9 %collective-permute-start.5 = (bf16[192,1152]{1,0:T(8,128)(2,1)S(1)}, bf16[192,1152]{1,0:T(8,128)(2,1)}, u32[]{:S(2)}, u32[]{:S(2)}) collective-permute-start(bf16[192,1152]{1,0:T(8,128)(2,1)S(1)} %collective-permute-done.4.bo), channel_id=1, source_target_pairs={{0,1},{1,0},{2,3},{3,2},{4,5},{5,4},{6,7},{7,6},{8,9},{9,8},{10,11... | collective-permute-start | bytes 1327112 | tf_op jit(solution)/shard_map/ppermute | solution.py:29
  50.3 5.3 %collective-permute-start.8 = (bf16[3,208,1152]{2,1,0:T(8,128)(2,1)}, bf16[3,208,1152]{2,1,0:T(8,128)(2,1)S(1)}, u32[]{:S(2)}, u32[]{:S(2)}) collective-permute-start(bf16[3,208,1152]{2,1,0:T(8,128)(2,1)} %get-tuple-element.19), channel_id=1, source_target_pairs={{0,1},{1,0},{2,3},{3,2},{4,5},{5,4},{6,7},{7,6},{8,9},{9,8},{10,11... | collective-permute-start | bytes 4313096 | tf_op jit(solution)/shard_map/ppermute | solution.py:29
  55.6 1.8 %copy-start = (f32[3,192,1152]{2,1,0:T(8,128)S(1)}, f32[3,192,1152]{2,1,0:T(8,128)}, u32[]{:S(2)}) copy-start(f32[3,192,1152]{2,1,0:T(8,128)} %get-tuple-element.18.text_own.own) | copy-start | bytes 7962628
  57.4 51.9 %copy-start.5 = (bf16[192,1152]{1,0:T(8,128)(2,1)S(1)}, bf16[192,1152]{1,0:T(8,128)(2,1)}, u32[]{:S(2)}) copy-start(bf16[192,1152]{1,0:T(8,128)(2,1)} %images.3) | copy-start | bytes 1327108
  57.4 51.9 %copy-start.6 = (f32[192,1152]{1,0:T(8,128)S(1)}, f32[192,1152]{1,0:T(8,128)}, u32[]{:S(2)}) copy-start(f32[192,1152]{1,0:T(8,128)} %get-tuple-element.24.own) | copy-start | bytes 2654212
  57.6 53.7 %collective-permute-start.9 = (bf16[208,1152]{1,0:T(8,128)(2,1)S(1)}, bf16[208,1152]{1,0:T(8,128)(2,1)S(1)}, u32[]{:S(2)}, u32[]{:S(2)}) collective-permute-start(bf16[208,1152]{1,0:T(8,128)(2,1)S(1)} %get-tuple-element.21), channel_id=1, source_target_pairs={{0,760},{1,761},{2,762},{3,763},{4,764},{5,765},{6,766},{7,767},{8... | collective-permute-start | bytes 1437704 | tf_op jit(solution)/shard_map/ppermute | solution.py:29
  69.7 41.6 %collective-permute-start.10 = (bf16[208,1152]{1,0:T(8,128)(2,1)S(1)}, bf16[208,1152]{1,0:T(8,128)(2,1)S(1)}, u32[]{:S(2)}, u32[]{:S(2)}) collective-permute-start(bf16[208,1152]{1,0:T(8,128)(2,1)S(1)} %get-tuple-element.22), channel_id=1, source_target_pairs={{4,756},{5,757},{6,758},{7,759},{12,764},{13,765},{14,766},{15,767... | collective-permute-start | bytes 1437704 | tf_op jit(solution)/shard_map/ppermute | solution.py:29
  70.4 17.8 %collective-permute-start.11 = (bf16[192,1152]{1,0:T(8,128)(2,1)S(1)}, bf16[192,1152]{1,0:T(8,128)(2,1)S(1)}, u32[]{:S(2)}, u32[]{:S(2)}) collective-permute-start(bf16[192,1152]{1,0:T(8,128)(2,1)S(1)} %get-tuple-element.25), channel_id=1, source_target_pairs={{0,2},{1,3},{2,0},{3,1},{4,6},{5,7},{6,4},{7,5},{8,10},{9,11},{10,... | collective-permute-start | bytes 1327112 | tf_op jit(solution)/shard_map/ppermute | solution.py:29
  72.3 30.9 %collective-permute-start.12 = (bf16[192,1152]{1,0:T(8,128)(2,1)S(1)}, bf16[192,1152]{1,0:T(8,128)(2,1)S(1)}, u32[]{:S(2)}, u32[]{:S(2)}) collective-permute-start(bf16[192,1152]{1,0:T(8,128)(2,1)S(1)} %get-tuple-element.26), channel_id=1, source_target_pairs={{0,4},{1,5},{2,6},{3,7},{4,0},{5,1},{6,2},{7,3},{8,12},{9,13},{10,... | collective-permute-start | bytes 1327112 | tf_op jit(solution)/shard_map/ppermute | solution.py:29
  86.3 23.0 %collective-permute-start.13 = (bf16[192,1152]{1,0:T(8,128)(2,1)S(1)}, bf16[192,1152]{1,0:T(8,128)(2,1)S(1)}, u32[]{:S(2)}, u32[]{:S(2)}) collective-permute-start(bf16[192,1152]{1,0:T(8,128)(2,1)S(1)} %get-tuple-element.27), channel_id=1, source_target_pairs={{0,6},{1,7},{2,4},{3,5},{4,2},{5,3},{6,0},{7,1},{8,14},{9,15},{10,... | collective-permute-start | bytes 1327112 | tf_op jit(solution)/shard_map/ppermute | solution.py:29
  109.3 2.0 %copy-start.1 = (f32[3,192,1152]{2,1,0:T(8,128)S(1)}, f32[3,192,1152]{2,1,0:T(8,128)}, u32[]{:S(2)}) copy-start(f32[3,192,1152]{2,1,0:T(8,128)} %get-tuple-element.18.text_own.own) | copy-start | bytes 7962628
  109.3 2.0 %copy-start.3 = (bf16[192,1152]{1,0:T(8,128)(2,1)S(1)}, bf16[192,1152]{1,0:T(8,128)(2,1)}, u32[]{:S(2)}) copy-start(bf16[192,1152]{1,0:T(8,128)(2,1)} %texts.3) | copy-start | bytes 1327108

commit v2 on v0

v2 whole, which is shorter than its diff:
```python
import functools

import jax
import jax.numpy as jnp
from jax import lax
from jax.experimental import pallas as pl
from jax.experimental.pallas import tpu as pltpu

EPSILON = 1e-06
VISITS = 4
TAIL = 16
AXES = ("img", "txt")
F32, BF16 = jnp.float32, jnp.bfloat16
NT = (((1,), (1,)), ((), ()))
NN = (((1,), (0,)), ((), ()))
TN = (((0,), (0,)), ((), ()))
HBM = pl.BlockSpec(memory_space=pltpu.HBM)
VMEM = pl.BlockSpec(memory_space=pltpu.VMEM)
SMEM = pl.BlockSpec(memory_space=pltpu.SMEM)
PARAMS = pltpu.CompilerParams(vmem_limit_bytes=48 * 1024 * 1024)


def moved(value, lines, up=0, flip=0, other=0, odd_only=False):
    route = []
    for line in range(lines):
        for x in range(4):
            if odd_only and x < 2:
                continue
            for c in range(2):
                here = line * 8 + x * 2 + c
                there = (line + up) % lines * 8 + (x ^ flip) * 2 + (c ^ other)
                route.append((here, there))
    return lax.ppermute(value, AXES, route)


def unit_of(ref):
    wide = ref[...].astype(F32)
    square = jnp.sum(wide * wide, axis=-1, keepdims=True) + EPSILON
    scale = 1.0 / jnp.sqrt(square)
    return wide * scale, scale


def half_of(ref):
    return unit_of(ref)[0].astype(BF16)


def tail_of(loss):
    rows = lax.broadcasted_iota(jnp.int32, (TAIL, loss.shape[1]), 0)
    wide = jnp.broadcast_to(loss, rows.shape)
    high = wide.astype(BF16).astype(F32)
    return jnp.where(rows == 0, high, jnp.where(rows == 1, wide - high, 0.0)).astype(BF16)


def tail_sum(tail, n):
    tail = tail.astype(F32)
    return tail[0:1, :n] + tail[1:2, :n]


def halves_kernel(spot, c, i2, i1, i3, b, a, i0, ih, th, raw, arrived):
    r = a.shape[0]
    sources = (a, b, c, i0, i1, i2, i3)
    copies = [
        pltpu.make_async_copy(source, raw.at[k], arrived.at[k]) for k, source in enumerate(sources)
    ]
    for copy in copies:
        copy.start()
    copies[0].wait()
    own = half_of(raw.at[0])
    th[pl.ds(0, r), :] = own
    copies[1].wait()
    th[pl.ds(r, r), :] = half_of(raw.at[1])
    copies[2].wait()

    @pl.when(spot[0] < 2)
    def _():
        th[pl.ds(2 * r, r), :] = own

    @pl.when(spot[0] >= 2)
    def _():
        th[pl.ds(2 * r, r), :] = half_of(raw.at[2])

    for k in range(4):
        copies[3 + k].wait()
        ih[pl.ds(k * r, r), :] = half_of(raw.at[3 + k])


def band(scalars, ih, th, p, diagonal):
    r = th.shape[0] // 3
    n = 2 * r
    temper, bias = scalars[0], scalars[1]
    sums, parts = [], []
    for half in range(2):
        logits = bias + temper * lax.dot_general(
            ih[pl.ds(half * n, n), :], th[pl.ds(half * r, n), :], NT, preferred_element_type=F32
        )
        margin = logits
        if diagonal and half == 0:
            rows = lax.broadcasted_iota(jnp.int32, logits.shape, 0)
            cols = lax.broadcasted_iota(jnp.int32, logits.shape, 1)
            positive = (rows == cols) & (cols < r)
            margin = jnp.where(positive, -logits, logits)
        grown = jnp.exp(margin)
        whole = 1.0 + grown
        slope = grown / whole
        losses = jnp.where(
            grown < 0.00390625,
            grown * (1.0 - grown * (0.5 - grown * (1.0 / 3.0))),
            jnp.log(whole),
        )
        if diagonal and half == 0:
            slope = jnp.where(positive, -slope, slope)
        p[pl.ds(half * n, n), :] = slope.astype(BF16)
        losses = jnp.sum(losses.reshape(n // 8, 8, n), axis=0)
        sums.append(jnp.broadcast_to(jnp.sum(losses, axis=0, keepdims=True), (8, n)))
    for half in range(2):
        parts.append(
            lax.dot_general(
                p[pl.ds(half * n, n), :], ih[pl.ds(half * n, n), :], TN, preferred_element_type=F32
            )
        )
    near, far = parts
    return (
        (near[:r], near[r:] + far[:r], far[r:]),
        (sums[0], pltpu.roll(sums[0], r, 1) + sums[1], pltpu.roll(sums[1], r, 1)),
    )


def own_pairs_kernel(scalars, ih, th, p, own, sums):
    parts, losses = band(scalars, ih, th, p, True)
    for place in range(3):
        own[place] = parts[place]
        sums[place] = losses[place]


def sibling_pairs_kernel(scalars, ih, th, after, p, send):
    del after
    parts, losses = band(scalars, ih, th, p, False)
    r, width = parts[0].shape
    for place in range(3):
        send[place, pl.ds(0, r), :] = parts[place].astype(BF16)
        send[place, pl.ds(r, TAIL), :] = jnp.zeros((TAIL, width), BF16)
        send[place, pl.ds(r, TAIL), pl.ds(0, 2 * r)] = tail_of(losses[place][:1])


def spread_kernel(p_own, p_sib, t_own, t_sib, image_own, image_1, image_2, image_3):
    r = image_own.shape[0]
    n = 2 * r
    for half, (first, second) in ((1, (image_2, image_3)), (0, (image_own, image_1))):
        total = 0.0
        for p, t in ((p_own, t_own), (p_sib, t_sib)):
            total = total + lax.dot_general(
                p[pl.ds(half * n, n), :], t[pl.ds(half * r, n), :], NN, preferred_element_type=F32
            )
        first[...] = total[:r].astype(first.dtype)
        second[...] = total[r:].astype(second.dtype)


def join_kernel(own, got, sums, after, b_back, c_back):
    del after
    r = own.shape[1]
    n = sums.shape[2]
    for place, out in ((1, b_back), (2, c_back)):
        out[pl.ds(0, r), :] = (own[place] + got[place, pl.ds(0, r), :].astype(F32)).astype(BF16)
        loss = sums[place][:1] + tail_sum(got[place, pl.ds(r, TAIL), :], n)
        out[pl.ds(r, TAIL), :] = jnp.zeros((TAIL, out.shape[1]), BF16)
        out[pl.ds(r, TAIL), pl.ds(0, n)] = tail_of(loss)


def tangent(total, ref, temper):
    unit, scale = unit_of(ref)
    total = temper * total
    return (total - unit * jnp.sum(unit * total, axis=-1, keepdims=True)) * scale


def image_end_kernel(scalars, images, own, a, b, c, grad):
    total = own[...] + a[...].astype(F32) + b[...].astype(F32) + c[...].astype(F32)
    grad[...] = tangent(total, images, scalars[0])


def text_end_kernel(scalars, spot, texts, own, got, sums, b_got, c_got, grad, loss):
    r = texts.shape[0]
    n = sums.shape[2]

    def here(place):
        rows = own[place] + got[place, pl.ds(0, r), :].astype(F32)
        return rows, sums[place][:1] + tail_sum(got[place, pl.ds(r, TAIL), :], n)

    total, losses = here(0)
    more, more_losses = here(2)
    even = spot[0] < 2
    total = total + jnp.where(even, more, 0.0)
    losses = losses + jnp.where(even, more_losses, 0.0)
    for ref in (b_got, c_got):
        total = total + ref[pl.ds(0, r), :].astype(F32)
        losses = losses + tail_sum(ref[pl.ds(r, TAIL), :], n)
    grad[...] = tangent(total, texts, scalars[0])
    loss[...] = jnp.broadcast_to(losses / (VISITS * 4 * r), loss.shape)


def call(kernel, outs, name, smem, vmem, hbm=(), scratch=()):
    return pl.pallas_call(
        kernel,
        out_shape=outs,
        in_specs=[SMEM] * len(smem) + [VMEM] * len(vmem) + [HBM] * len(hbm),
        out_specs=tuple(VMEM for _ in outs),
        scratch_shapes=scratch,
        compiler_params=PARAMS,
        name=name,
    )(*smem, *vmem, *(pltpu.with_memory_space_constraint(value, pltpu.HBM) for value in hbm))


def on_device(lines, images, texts, log_temp, bias):
    r, width = images.shape
    n = 2 * r
    shape = jax.ShapeDtypeStruct
    half, long = shape((r, width), BF16), shape((r, width), F32)

    def send(value, name, **way):
        with jax.named_scope(name):
            return moved(value, lines, **way)

    scalars = jnp.stack([jnp.exp(log_temp), bias])
    spot = lax.axis_index("img") % 2 * 2 + lax.axis_index("txt") // 2
    spot = jnp.reshape(spot, (1,)).astype(jnp.int32)
    c_own = send(texts, "texts_two_up", up=2, odd_only=True)
    b_own = send(texts, "texts_one_up", up=1)
    image_2 = send(images, "images_across", flip=2)
    image_3 = send(images, "images_beside_far", flip=3)
    image_1 = send(images, "images_beside", flip=1)
    ih, t_own = call(
        halves_kernel,
        (shape((4 * r, width), BF16), shape((3 * r, width), BF16)),
        "halves",
        [spot],
        [],
        [c_own, image_2, image_1, image_3, b_own, texts, images],
        scratch=(pltpu.VMEM((7, r, width), BF16), pltpu.SemaphoreType.DMA((7,))),
    )
    t_sib = send(t_own, "texts_sibling", other=1)
    slopes = shape((4 * r, n), BF16)
    p_own, own, sums = call(
        own_pairs_kernel,
        (slopes, shape((3, r, width), F32), shape((3, 8, n), F32)),
        "own_pairs",
        [scalars],
        [ih, t_own],
    )
    p_sib, text_send = call(
        sibling_pairs_kernel,
        (slopes, shape((3, r + TAIL, width), BF16)),
        "sibling_pairs",
        [scalars],
        [ih, t_sib, sums],
    )
    got = send(text_send, "text_parts_sibling", other=1)
    image_own, out_1, out_2, out_3 = call(
        spread_kernel, (long, half, half, half), "spread", [], [p_own, p_sib, t_own, t_sib]
    )
    back_2 = send(out_2, "image_parts_across", flip=2)
    back_3 = send(out_3, "image_parts_beside_far", flip=3)
    back_1 = send(out_1, "image_parts_beside", flip=1)
    back = shape((r + TAIL, width), BF16)
    b_back, c_back = call(join_kernel, (back, back), "join", [], [own, got, sums, out_2])
    c_got = send(c_back, "text_parts_two_down", up=-2, odd_only=True)
    b_got = send(b_back, "text_parts_one_down", up=-1)
    (image_grad,) = call(
        image_end_kernel, (long,), "image_end", [scalars], [images, image_own, back_1, back_2, back_3]
    )
    text_grad, loss = call(
        text_end_kernel,
        (long, shape((8, n), F32)),
        "text_end",
        [scalars, spot],
        [texts, own, got, sums, b_got, c_got],
    )
    return loss[0, :r], image_grad, text_grad


def solution(mesh):
    from jax.sharding import PartitionSpec as P

    lines = mesh.shape["img"] // 2
    rows = P(AXES, None)
    return jax.shard_map(
        functools.partial(on_device, lines),
        mesh=mesh,
        in_specs=(rows, rows, P(), P()),
        out_specs=(P(AXES), rows, rows),
        check_vma=False,
    )
```

time: 248 us -> 106 us (0.43)
  the two profiles are of different devices: /device:TPU:32 before, /device:TPU:1 now
where the time goes in v2:
time: 106 us; the launch traced here: 105 us
  starting transfers between devices  48.8 us (46%)
  waiting for transfers between devices  34.4 us (32%)
  Pallas kernels  18.3 us (17%)
  between operations  2.19 us (2%)
  local copies, waits for them, and re-layouts  1.38 us (1%)
    ppermute x12, starting transfers between devices, moved(): return lax.ppermute(value, AXES, route)  48.8 us
    ppermute x12, waiting for transfers between devices, moved(): return lax.ppermute(value, AXES, route)  34.4 us
    pallas_call x7, Pallas kernels, call(): pl.pallas_call(kernel, out_shape=outs, in_specs=[SMEM] * len(smem) + [VME...  18.3 us
  transfers between devices with their start and end apart: 12, of which 5 were waited for; matrix products, arithmetic and copies ran while one was open for 0% of the time, Pallas kernels for 10%

profile of v2, /device:TPU:1, one launch (start us, length us, event | category | flops | bytes accessed | tf_op | source)
XLA Modules:
  0.0 105.2 jit_solution(9702630802379248613)
XLA Ops:
  0.6 0.7 collective-permute-start
  1.3 10.6 %collective-permute-start.1 = (bf16[192,1152]{1,0:T(8,128)(2,1)}, bf16[192,1152]{1,0:T(8,128)(2,1)S(1)}, u32[]{:S(2)}, u32[]{:S(2)}) collective-permute-start(bf16[192,1152]{1,0:T(8,128)(2,1)} %images.1), channel_id=1, source_target_pairs={{0,4},{1,5},{2,6},{3,7},{4,0},{5,1},{6,2},{7,3},{8,12},{9,13},{10,... | collective-permute-start | bytes 1327112 | tf_op jit(solution)/shard_map/images_across/ppermute | solution.py:33
  11.9 2.2 %collective-permute-start.2 = (bf16[192,1152]{1,0:T(8,128)(2,1)}, bf16[192,1152]{1,0:T(8,128)(2,1)S(1)}, u32[]{:S(2)}, u32[]{:S(2)}) collective-permute-start(bf16[192,1152]{1,0:T(8,128)(2,1)} %images.1), channel_id=1, source_target_pairs={{0,2},{1,3},{2,0},{3,1},{4,6},{5,7},{6,4},{7,5},{8,10},{9,11},{10,... | collective-permute-start | bytes 1327112 | tf_op jit(solution)/shard_map/images_beside/ppermute | solution.py:33
  14.2 1.9 %collective-permute-start.3 = (bf16[192,1152]{1,0:T(8,128)(2,1)}, bf16[192,1152]{1,0:T(8,128)(2,1)S(1)}, u32[]{:S(2)}, u32[]{:S(2)}) collective-permute-start(bf16[192,1152]{1,0:T(8,128)(2,1)} %images.1), channel_id=1, source_target_pairs={{0,6},{1,7},{2,4},{3,5},{4,2},{5,3},{6,0},{7,1},{8,14},{9,15},{10,... | collective-permute-start | bytes 1327112 | tf_op jit(solution)/shard_map/images_beside_far/ppermute | solution.py:33
  16.1 4.0 %collective-permute-start.4 = (bf16[192,1152]{1,0:T(8,128)(2,1)}, bf16[192,1152]{1,0:T(8,128)(2,1)S(1)}, u32[]{:S(2)}, u32[]{:S(2)}) collective-permute-start(bf16[192,1152]{1,0:T(8,128)(2,1)} %texts.1), channel_id=1, source_target_pairs={{0,8},{1,9},{2,10},{3,11},{4,12},{5,13},{6,14},{7,15},{8,16},{9,17... | collective-permute-start | bytes 1327112 | tf_op jit(solution)/shard_map/texts_one_up/ppermute | solution.py:33
  20.1 0.0 collective-permute-done.c
  20.1 0.0 copy-start.3
  20.2 0.0 collective-permute-done.1.i2
  20.2 0.0 copy-start.4
  20.2 11.0 %collective-permute-done.2.i1 = bf16[192,1152]{1,0:T(8,128)(2,1)S(1)} collective-permute-done((bf16[192,1152]{1,0:T(8,128)(2,1)}, bf16[192,1152]{1,0:T(8,128)(2,1)S(1)}, u32[]{:S(2)}, u32[]{:S(2)}) %collective-permute-start.2) | collective-permute-done | bytes 442400 | tf_op jit(solution)/shard_map/images_beside/ppermute | solution.py:33
  31.2 0.0 copy-start.5
  31.2 1.0 collective-permute-done.3.i3
  32.2 0.0 copy-start.6
  32.2 6.7 %collective-permute-done.4.b = bf16[192,1152]{1,0:T(8,128)(2,1)S(1)} collective-permute-done((bf16[192,1152]{1,0:T(8,128)(2,1)}, bf16[192,1152]{1,0:T(8,128)(2,1)S(1)}, u32[]{:S(2)}, u32[]{:S(2)}) %collective-permute-start.4) | collective-permute-done | bytes 442400 | tf_op jit(solution)/shard_map/texts_one_up/ppermute | solution.py:33
  38.9 0.0 copy-done.4
  38.9 0.0 copy-done.5
  38.9 0.0 copy-done.6
  38.9 0.0 copy-start.7
  38.9 0.8 copy-done.7
  39.7 0.0 copy-done.3
  39.7 2.3 %halves.1 = (bf16[768,1152]{1,0:T(8,128)(2,1)S(1)}, bf16[576,1152]{1,0:T(8,128)(2,1)S(1)}) custom-call(s32[1]{0:T(128)} %bitcast.2.spot, bf16[192,1152]{1,0:T(8,128)(2,1)} %copy-done.3, bf16[192,1152]{1,0:T(8,128)(2,1)} %copy-done.4, bf16[192,1152]{1,0:T(8,128)(2,1)} %copy-done.5, bf16[192,1152]{1,0:T(8,128)(2,1)} %copy-done.6, bf16[192,1152]{1,0:T(8,128)(2,1)} %copy-done.7, ...), custom_call_target="tpu_custom_call" | custom-call | tf_op jit(solution)/shard_map/halves/pallas_call | solution.py:201
  42.0 3.8 %collective-permute-start.5 = (bf16[576,1152]{1,0:T(8,128)(2,1)S(1)}, bf16[576,1152]{1,0:T(8,128)(2,1)}, u32[]{:S(2)}, u32[]{:S(2)}) collective-permute-start(bf16[576,1152]{1,0:T(8,128)(2,1)S(1)} %get-tuple-element.19.th.t_own), channel_id=1, source_target_pairs={{0,1},{1,0},{2,3},{3,2},{4,5},{5,4},{6,7},{7,6},{8,9},{9,8},{10,11... | collective-permute-start | bytes 3981320 | tf_op jit(solution)/shard_map/texts_sibling/ppermute | solution.py:33
  47.1 0.1 pad_maximum_fusion.scalars
  47.2 4.5 %own_pairs.1 = (bf16[768,384]{1,0:T(8,128)(2,1)S(1)}, f32[3,192,1152]{2,1,0:T(8,128)}, f32[3,8,384]{2,1,0:T(8,128)S(1)}) custom-call(f32[2]{0:T(128)S(1)} %pad_maximum_fusion.scalars, bf16[768,1152]{1,0:T(8,128)(2,1)S(1)} %get-tuple-element.18.ih, bf16[576,1152]{1,0:T(8,128)(2,1)S(1)} %get-tuple-element.19.th.t_own), custom_call_target="tpu_custom_call" | custom-call | tf_op jit(solution)/shard_map/own_pairs/pallas_call | solution.py:201
  51.7 0.0 collective-permute-done.5.th.t_sib
  51.7 3.8 %sibling_pairs.1 = (bf16[768,384]{1,0:T(8,128)(2,1)S(1)}, bf16[3,208,1152]{2,1,0:T(8,128)(2,1)S(1)}) custom-call(f32[2]{0:T(128)S(1)} %pad_maximum_fusion.scalars, bf16[768,1152]{1,0:T(8,128)(2,1)S(1)} %get-tuple-element.18.ih, bf16[576,1152]{1,0:T(8,128)(2,1)} %collective-permute-done.5.th.t_sib, f32[3,8,384]{2,1,0:T(8,128)S(1)} %get-tuple-element.21.after.sums), custom_call_target="tpu_custom_call" | custom-call | tf_op jit(solution)/shard_map/sibling_pairs/pallas_call | solution.py:201
  55.4 1.9 %collective-permute-start.6 = (bf16[3,208,1152]{2,1,0:T(8,128)(2,1)S(1)}, bf16[3,208,1152]{2,1,0:T(8,128)(2,1)S(1)}, u32[]{:S(2)}, u32[]{:S(2)}) collective-permute-start(bf16[3,208,1152]{2,1,0:T(8,128)(2,1)S(1)} %get-tuple-element.22), channel_id=1, source_target_pairs={{0,1},{1,0},{2,3},{3,2},{4,5},{5,4},{6,7},{7,6},{8,9},{9,8},{10,11... | collective-permute-start | bytes 4313096 | tf_op jit(solution)/shard_map/text_parts_sibling/ppermute | solution.py:33
  57.4 0.0 copy-start
  57.4 3.6 %spread.1 = (f32[192,1152]{1,0:T(8,128)S(1)}, bf16[192,1152]{1,0:T(8,128)(2,1)S(1)}, bf16[192,1152]{1,0:T(8,128)(2,1)S(1)}, bf16[192,1152]{1,0:T(8,128)(2,1)S(1)}) custom-call(bf16[768,384]{1,0:T(8,128)(2,1)S(1)} %get-tuple-element.23.p_own, bf16[768,384]{1,0:T(8,128)(2,1)S(1)} %get-tuple-element.24.p_sib, bf16[576,1152]{1,0:T(8,128)(2,1)S(1)} %get-tuple-element.19.th.t_own, ...), custom_call_target="tpu_custom_call" | custom-call | tf_op jit(solution)/shard_map/spread/pallas_call | solution.py:201
  61.0 0.0 collective-permute-done.6.got
  61.0 0.0 copy-done
  61.0 0.0 copy-start.2
  61.0 0.2 join.1
  61.2 6.6 %collective-permute-start.7 = (bf16[208,1152]{1,0:T(8,128)(2,1)S(1)}, bf16[208,1152]{1,0:T(8,128)(2,1)S(1)}, u32[]{:S(2)}, u32[]{:S(2)}) collective-permute-start(bf16[208,1152]{1,0:T(8,128)(2,1)S(1)} %get-tuple-element.26), channel_id=1, source_target_pairs={{0,760},{1,761},{2,762},{3,763},{4,764},{5,765},{6,766},{7,767},{8... | collective-permute-start | bytes 1437704 | tf_op jit(solution)/shard_map/text_parts_one_down/ppermute | solution.py:33
  67.8 0.7 collective-permute-start.8
  68.5 12.2 %collective-permute-start.10 = (bf16[192,1152]{1,0:T(8,128)(2,1)S(1)}, bf16[192,1152]{1,0:T(8,128)(2,1)S(1)}, u32[]{:S(2)}, u32[]{:S(2)}) collective-permute-start(bf16[192,1152]{1,0:T(8,128)(2,1)S(1)} %get-tuple-element.25.after), channel_id=1, source_target_pairs={{0,4},{1,5},{2,6},{3,7},{4,0},{5,1},{6,2},{7,3},{8,12},{9,13},{10,... | collective-permute-start | bytes 1327112 | tf_op jit(solution)/shard_map/image_parts_across/ppermute | solution.py:33
  80.7 2.2 %collective-permute-start.9 = (bf16[192,1152]{1,0:T(8,128)(2,1)S(1)}, bf16[192,1152]{1,0:T(8,128)(2,1)S(1)}, u32[]{:S(2)}, u32[]{:S(2)}) collective-permute-start(bf16[192,1152]{1,0:T(8,128)(2,1)S(1)} %get-tuple-element.30), channel_id=1, source_target_pairs={{0,2},{1,3},{2,0},{3,1},{4,6},{5,7},{6,4},{7,5},{8,10},{9,11},{10,... | collective-permute-start | bytes 1327112 | tf_op jit(solution)/shard_map/image_parts_beside/ppermute | solution.py:33
  82.9 1.9 %collective-permute-start.11 = (bf16[192,1152]{1,0:T(8,128)(2,1)S(1)}, bf16[192,1152]{1,0:T(8,128)(2,1)S(1)}, u32[]{:S(2)}, u32[]{:S(2)}) collective-permute-start(bf16[192,1152]{1,0:T(8,128)(2,1)S(1)} %get-tuple-element.31), channel_id=1, source_target_pairs={{0,6},{1,7},{2,4},{3,5},{4,2},{5,3},{6,0},{7,1},{8,14},{9,15},{10,... | collective-permute-start | bytes 1327112 | tf_op jit(solution)/shard_map/image_parts_beside_far/ppermute | solution.py:33
  84.9 14.8 %collective-permute-done.9.a = bf16[192,1152]{1,0:T(8,128)(2,1)S(1)} collective-permute-done((bf16[192,1152]{1,0:T(8,128)(2,1)S(1)}, bf16[192,1152]{1,0:T(8,128)(2,1)S(1)}, u32[]{:S(2)}, u32[]{:S(2)}) %collective-permute-start.9) | collective-permute-done | bytes 442400 | tf_op jit(solution)/shard_map/image_parts_beside/ppermute | solution.py:33
  99.7 0.0 collective-permute-done.10.b
  99.7 0.9 collective-permute-done.11.c
  100.5 0.0 copy-done.2
  100.6 0.0 copy-start.1
  100.6 2.0 %image_end.1 = f32[192,1152]{1,0:T(8,128)} custom-call(f32[2]{0:T(128)S(1)} %pad_maximum_fusion.scalars, bf16[192,1152]{1,0:T(8,128)(2,1)S(1)} %copy-done.2, f32[192,1152]{1,0:T(8,128)S(1)} %get-tuple-element.29.own, bf16[192,1152]{1,0:T(8,128)(2,1)S(1)} %collective-permute-done.9.a, bf16[192,1152]{1,0:T(8,128)(2,1)S(1)} %collective-permute-done.10.b, ...), custom_call_target="tpu_custom_call" | custom-call | tf_op jit(solution)/shard_map/image_end/pallas_call | solution.py:201
  102.5 0.0 collective-permute-done.7.b_got
  102.5 0.0 collective-permute-done.8.c_got
  102.5 0.0 copy-done.1
  102.5 2.1 %text_end.1 = (f32[192,1152]{1,0:T(8,128)}, f32[8,384]{1,0:T(8,128)S(1)}) custom-call(f32[2]{0:T(128)S(1)} %pad_maximum_fusion.scalars, s32[1]{0:T(128)} %bitcast.2.spot, bf16[192,1152]{1,0:T(8,128)(2,1)S(1)} %copy-done.1, f32[3,192,1152]{2,1,0:T(8,128)S(1)} %copy-done, bf16[3,208,1152]{2,1,0:T(8,128)(2,1)S(1)} %collective-permute-done.6.got, ...), custom_call_target="tpu_custom_call" | custom-call | tf_op jit(solution)/shard_map/text_end/pallas_call | solution.py:201
  104.6 0.6 slice.3
Async XLA Ops:
  0.6 19.5 %collective-permute-start = (bf16[192,1152]{1,0:T(8,128)(2,1)}, bf16[192,1152]{1,0:T(8,128)(2,1)S(1)}, u32[]{:S(2)}, u32[]{:S(2)}) collective-permute-start(bf16[192,1152]{1,0:T(8,128)(2,1)} %texts.1), channel_id=1, source_target_pairs={{4,20},{5,21},{6,22},{7,23},{12,28},{13,29},{14,30},{15,31},{20,36... | collective-permute-start | bytes 1327112 | tf_op jit(solution)/shard_map/texts_two_up/ppermute | solution.py:33
  1.3 18.9 %collective-permute-start.1 = (bf16[192,1152]{1,0:T(8,128)(2,1)}, bf16[192,1152]{1,0:T(8,128)(2,1)S(1)}, u32[]{:S(2)}, u32[]{:S(2)}) collective-permute-start(bf16[192,1152]{1,0:T(8,128)(2,1)} %images.1), channel_id=1, source_target_pairs={{0,4},{1,5},{2,6},{3,7},{4,0},{5,1},{6,2},{7,3},{8,12},{9,13},{10,... | collective-permute-start | bytes 1327112 | tf_op jit(solution)/shard_map/images_across/ppermute | solution.py:33
  11.9 19.3 %collective-permute-start.2 = (bf16[192,1152]{1,0:T(8,128)(2,1)}, bf16[192,1152]{1,0:T(8,128)(2,1)S(1)}, u32[]{:S(2)}, u32[]{:S(2)}) collective-permute-start(bf16[192,1152]{1,0:T(8,128)(2,1)} %images.1), channel_id=1, source_target_pairs={{0,2},{1,3},{2,0},{3,1},{4,6},{5,7},{6,4},{7,5},{8,10},{9,11},{10,... | collective-permute-start | bytes 1327112 | tf_op jit(solution)/shard_map/images_beside/ppermute | solution.py:33
  14.2 18.0 %collective-permute-start.3 = (bf16[192,1152]{1,0:T(8,128)(2,1)}, bf16[192,1152]{1,0:T(8,128)(2,1)S(1)}, u32[]{:S(2)}, u32[]{:S(2)}) collective-permute-start(bf16[192,1152]{1,0:T(8,128)(2,1)} %images.1), channel_id=1, source_target_pairs={{0,6},{1,7},{2,4},{3,5},{4,2},{5,3},{6,0},{7,1},{8,14},{9,15},{10,... | collective-permute-start | bytes 1327112 | tf_op jit(solution)/shard_map/images_beside_far/ppermute | solution.py:33
  16.1 22.8 %collective-permute-start.4 = (bf16[192,1152]{1,0:T(8,128)(2,1)}, bf16[192,1152]{1,0:T(8,128)(2,1)S(1)}, u32[]{:S(2)}, u32[]{:S(2)}) collective-permute-start(bf16[192,1152]{1,0:T(8,128)(2,1)} %texts.1), channel_id=1, source_target_pairs={{0,8},{1,9},{2,10},{3,11},{4,12},{5,13},{6,14},{7,15},{8,16},{9,17... | collective-permute-start | bytes 1327112 | tf_op jit(solution)/shard_map/texts_one_up/ppermute | solution.py:33
  20.1 19.5 %copy-start.3 = (bf16[192,1152]{1,0:T(8,128)(2,1)}, bf16[192,1152]{1,0:T(8,128)(2,1)S(1)}, u32[]{:S(2)}) copy-start(bf16[192,1152]{1,0:T(8,128)(2,1)S(1)} %collective-permute-done.c) | copy-start | bytes 1327108
  20.2 18.7 %copy-start.4 = (bf16[192,1152]{1,0:T(8,128)(2,1)}, bf16[192,1152]{1,0:T(8,128)(2,1)S(1)}, u32[]{:S(2)}) copy-start(bf16[192,1152]{1,0:T(8,128)(2,1)S(1)} %collective-permute-done.1.i2) | copy-start | bytes 1327108
  31.2 7.7 %copy-start.5 = (bf16[192,1152]{1,0:T(8,128)(2,1)}, bf16[192,1152]{1,0:T(8,128)(2,1)S(1)}, u32[]{:S(2)}) copy-start(bf16[192,1152]{1,0:T(8,128)(2,1)S(1)} %collective-permute-done.2.i1) | copy-start | bytes 1327108
  32.2 6.7 %copy-start.6 = (bf16[192,1152]{1,0:T(8,128)(2,1)}, bf16[192,1152]{1,0:T(8,128)(2,1)S(1)}, u32[]{:S(2)}) copy-start(bf16[192,1152]{1,0:T(8,128)(2,1)S(1)} %collective-permute-done.3.i3) | copy-start | bytes 1327108
  38.9 0.8 copy-start.7
  42.0 9.7 %collective-permute-start.5 = (bf16[576,1152]{1,0:T(8,128)(2,1)S(1)}, bf16[576,1152]{1,0:T(8,128)(2,1)}, u32[]{:S(2)}, u32[]{:S(2)}) collective-permute-start(bf16[576,1152]{1,0:T(8,128)(2,1)S(1)} %get-tuple-element.19.th.t_own), channel_id=1, source_target_pairs={{0,1},{1,0},{2,3},{3,2},{4,5},{5,4},{6,7},{7,6},{8,9},{9,8},{10,11... | collective-permute-start | bytes 3981320 | tf_op jit(solution)/shard_map/texts_sibling/ppermute | solution.py:33
  55.4 5.5 %collective-permute-start.6 = (bf16[3,208,1152]{2,1,0:T(8,128)(2,1)S(1)}, bf16[3,208,1152]{2,1,0:T(8,128)(2,1)S(1)}, u32[]{:S(2)}, u32[]{:S(2)}) collective-permute-start(bf16[3,208,1152]{2,1,0:T(8,128)(2,1)S(1)} %get-tuple-element.22), channel_id=1, source_target_pairs={{0,1},{1,0},{2,3},{3,2},{4,5},{5,4},{6,7},{7,6},{8,9},{9,8},{10,11... | collective-permute-start | bytes 4313096 | tf_op jit(solution)/shard_map/text_parts_sibling/ppermute | solution.py:33
  57.4 3.6 %copy-start = (f32[3,192,1152]{2,1,0:T(8,128)S(1)}, f32[3,192,1152]{2,1,0:T(8,128)}, u32[]{:S(2)}) copy-start(f32[3,192,1152]{2,1,0:T(8,128)} %get-tuple-element.20.own) | copy-start | bytes 7962628
  61.0 39.6 %copy-start.2 = (bf16[192,1152]{1,0:T(8,128)(2,1)S(1)}, bf16[192,1152]{1,0:T(8,128)(2,1)}, u32[]{:S(2)}) copy-start(bf16[192,1152]{1,0:T(8,128)(2,1)} %images.1) | copy-start | bytes 1327108
  61.2 41.4 %collective-permute-start.7 = (bf16[208,1152]{1,0:T(8,128)(2,1)S(1)}, bf16[208,1152]{1,0:T(8,128)(2,1)S(1)}, u32[]{:S(2)}, u32[]{:S(2)}) collective-permute-start(bf16[208,1152]{1,0:T(8,128)(2,1)S(1)} %get-tuple-element.26), channel_id=1, source_target_pairs={{0,760},{1,761},{2,762},{3,763},{4,764},{5,765},{6,766},{7,767},{8... | collective-permute-start | bytes 1437704 | tf_op jit(solution)/shard_map/text_parts_one_down/ppermute | solution.py:33
  67.8 34.8 %collective-permute-start.8 = (bf16[208,1152]{1,0:T(8,128)(2,1)S(1)}, bf16[208,1152]{1,0:T(8,128)(2,1)S(1)}, u32[]{:S(2)}, u32[]{:S(2)}) collective-permute-start(bf16[208,1152]{1,0:T(8,128)(2,1)S(1)} %get-tuple-element.27), channel_id=1, source_target_pairs={{4,756},{5,757},{6,758},{7,759},{12,764},{13,765},{14,766},{15,767... | collective-permute-start | bytes 1437704 | tf_op jit(solution)/shard_map/text_parts_two_down/ppermute | solution.py:33
  68.5 31.2 %collective-permute-start.10 = (bf16[192,1152]{1,0:T(8,128)(2,1)S(1)}, bf16[192,1152]{1,0:T(8,128)(2,1)S(1)}, u32[]{:S(2)}, u32[]{:S(2)}) collective-permute-start(bf16[192,1152]{1,0:T(8,128)(2,1)S(1)} %get-tuple-element.25.after), channel_id=1, source_target_pairs={{0,4},{1,5},{2,6},{3,7},{4,0},{5,1},{6,2},{7,3},{8,12},{9,13},{10,... | collective-permute-start | bytes 1327112 | tf_op jit(solution)/shard_map/image_parts_across/ppermute | solution.py:33
  80.7 19.0 %collective-permute-start.9 = (bf16[192,1152]{1,0:T(8,128)(2,1)S(1)}, bf16[192,1152]{1,0:T(8,128)(2,1)S(1)}, u32[]{:S(2)}, u32[]{:S(2)}) collective-permute-start(bf16[192,1152]{1,0:T(8,128)(2,1)S(1)} %get-tuple-element.30), channel_id=1, source_target_pairs={{0,2},{1,3},{2,0},{3,1},{4,6},{5,7},{6,4},{7,5},{8,10},{9,11},{10,... | collective-permute-start | bytes 1327112 | tf_op jit(solution)/shard_map/image_parts_beside/ppermute | solution.py:33
  82.9 17.6 %collective-permute-start.11 = (bf16[192,1152]{1,0:T(8,128)(2,1)S(1)}, bf16[192,1152]{1,0:T(8,128)(2,1)S(1)}, u32[]{:S(2)}, u32[]{:S(2)}) collective-permute-start(bf16[192,1152]{1,0:T(8,128)(2,1)S(1)} %get-tuple-element.31), channel_id=1, source_target_pairs={{0,6},{1,7},{2,4},{3,5},{4,2},{5,3},{6,0},{7,1},{8,14},{9,15},{10,... | collective-permute-start | bytes 1327112 | tf_op jit(solution)/shard_map/image_parts_beside_far/ppermute | solution.py:33
  100.6 2.0 %copy-start.1 = (bf16[192,1152]{1,0:T(8,128)(2,1)S(1)}, bf16[192,1152]{1,0:T(8,128)(2,1)}, u32[]{:S(2)}) copy-start(bf16[192,1152]{1,0:T(8,128)(2,1)} %texts.1) | copy-start | bytes 1327108

commit v3 on v2

v3 whole, which is shorter than its diff:
```python
import functools

import jax
import jax.numpy as jnp
from jax import lax
from jax.experimental import pallas as pl
from jax.experimental.pallas import tpu as pltpu

EPSILON = 1e-06
VISITS = 4
TAIL = 16
AXES = ("img", "txt")
F32, BF16 = jnp.float32, jnp.bfloat16
NT = (((1,), (1,)), ((), ()))
NN = (((1,), (0,)), ((), ()))
TN = (((0,), (0,)), ((), ()))
HBM = pl.BlockSpec(memory_space=pltpu.HBM)
VMEM = pl.BlockSpec(memory_space=pltpu.VMEM)
SMEM = pl.BlockSpec(memory_space=pltpu.SMEM)
PARAMS = pltpu.CompilerParams(vmem_limit_bytes=48 * 1024 * 1024)


def moved(value, lines, up=0, flip=0, other=0, odd_only=False):
    route = []
    for line in range(lines):
        for x in range(4):
            if odd_only and x < 2:
                continue
            for c in range(2):
                here = line * 8 + x * 2 + c
                there = (line + up) % lines * 8 + (x ^ flip) * 2 + (c ^ other)
                route.append((here, there))
    return lax.ppermute(value, AXES, route)


def unit_of(ref):
    wide = ref[...].astype(F32)
    square = jnp.sum(wide * wide, axis=-1, keepdims=True) + EPSILON
    scale = 1.0 / jnp.sqrt(square)
    return wide * scale, scale


def half_of(ref):
    return unit_of(ref)[0].astype(BF16)


def tail_of(loss):
    rows = lax.broadcasted_iota(jnp.int32, (TAIL, loss.shape[1]), 0)
    wide = jnp.broadcast_to(loss, rows.shape)
    high = wide.astype(BF16).astype(F32)
    return jnp.where(rows == 0, high, jnp.where(rows == 1, wide - high, 0.0)).astype(BF16)


def tail_sum(tail, n):
    tail = tail.astype(F32)
    return tail[0:1, :n] + tail[1:2, :n]


def halves_kernel(b, a, i2, i1, i3, i0, ih, ah, bh, raw, arrived):
    r = i0.shape[0]
    places = ((b, bh, 0), (a, ah, 0), (i0, ih, 0), (i2, ih, 2), (i1, ih, 1), (i3, ih, 3))
    copies, at = [], 0
    for k, (ref, _, _) in enumerate(places):
        rows = ref.shape[0]
        copies.append(pltpu.make_async_copy(ref, raw.at[pl.ds(at, rows), :], arrived.at[k]))
        copies[-1].start()
        at += rows
    at = 0
    for copy, (ref, out, place) in zip(copies, places):
        rows = ref.shape[0]
        copy.wait()
        out[pl.ds(place * r, rows), :] = half_of(raw.at[pl.ds(at, rows), :])
        at += rows


def late_halves_kernel(after, c, out):
    del after
    out[...] = half_of(c)


def temper_of(log_temp, lanes):
    return jnp.exp(jnp.full((1, lanes), log_temp[0], F32))


def tile(log_temp, bias, images, texts, diagonal=False):
    rows, cols = images.shape[0], texts.shape[0]
    logits = bias[0] + temper_of(log_temp, cols) * dot(images, texts, NT)
    margin = logits
    if diagonal:
        row = lax.broadcasted_iota(jnp.int32, logits.shape, 0)
        col = lax.broadcasted_iota(jnp.int32, logits.shape, 1)
        positive = (row == col) & (col < cols // 2)
        margin = jnp.where(positive, -logits, logits)
    grown = jnp.exp(margin)
    whole = 1.0 + grown
    inverse = pl.reciprocal(whole, approx=True)
    inverse = inverse * (2.0 - whole * inverse)
    slope = grown * inverse
    left = (grown - (whole - 1.0)) * inverse
    if diagonal:
        slope = jnp.where(positive, -slope, slope)
    q = rows // 4
    product = (whole[:q] * whole[q : 2 * q]) * (whole[2 * q : 3 * q] * whole[3 * q :])
    left = (left[:q] + left[q : 2 * q]) + (left[2 * q : 3 * q] + left[3 * q :])
    losses = jnp.sum((jnp.log(product) + left).reshape(q // 8, 8, cols), axis=0)
    return slope.astype(BF16), jnp.sum(losses, axis=0, keepdims=True)


def halved(sums, r):
    sums = jnp.broadcast_to(sums, (8, 2 * r))
    return sums[:1, :r], pltpu.roll(sums, r, 1)[:1, :r]


def dot(left, right, dims):
    return lax.dot_general(left, right, dims, preferred_element_type=F32)


def band(log_temp, bias, spot, ih, th, near, far, extra, part, losses, diagonal):
    r = th.shape[0] // 2
    n = 2 * r
    slope, sums = tile(log_temp, bias, ih[:n], th[...], diagonal)
    near[...] = slope
    sums_a, sums_b = halved(sums, r)
    slope, sums = tile(log_temp, bias, ih[n:], th[r:])
    far[...] = slope
    losses[1] = jnp.broadcast_to(sums_b + sums, losses.shape[1:])
    losses[0] = jnp.broadcast_to(sums_a, losses.shape[1:])
    extra[...] = jnp.zeros_like(extra)
    both = dot(near[...], ih[:n], TN)
    part[0] = both[:r]
    part[1] = both[r:] + dot(far[...], ih[n:], TN)

    @pl.when(spot[0] < 2)
    def _():
        slope, sums = tile(log_temp, bias, ih[n:], th[:r])
        extra[...] = slope
        losses[0] += jnp.broadcast_to(sums, losses.shape[1:])
        part[0] += dot(extra[...], ih[n:], TN)


def put_rows(out, rows):
    out[pl.ds(0, rows.shape[0]), :] = rows.astype(BF16)
    out[pl.ds(rows.shape[0], TAIL), :] = jnp.zeros((TAIL, rows.shape[1]), BF16)


def put_send(send, place, part, sums):
    r, width = part.shape
    send[place, pl.ds(0, r), :] = part.astype(BF16)
    send[place, pl.ds(r, TAIL), :] = jnp.zeros((TAIL, width), BF16)
    send[place, pl.ds(r, TAIL), pl.ds(0, r)] = tail_of(sums)


def own_pairs_kernel(log_temp, bias, spot, ih, a, b, near, far, extra, part, losses, th):
    r = th.shape[0] // 2
    th[pl.ds(0, r), :] = of_core(a, spot[1])
    th[pl.ds(r, r), :] = of_core(b, spot[1])
    band(log_temp, bias, spot, ih, th, near, far, extra, part, losses, True)


def of_core(ref, core):
    r = ref.shape[0] // 2
    return ref[pl.ds(pl.multiple_of(core * r, r), r), :]


def sibling_pairs_kernel(log_temp, bias, spot, ih, a, b, after, near, far, extra, send, th, part, losses):
    del after
    r = th.shape[0] // 2
    th[pl.ds(0, r), :] = of_core(a, 1 - spot[1])
    th[pl.ds(r, r), :] = of_core(b, 1 - spot[1])
    band(log_temp, bias, spot, ih, th, near, far, extra, part, losses, False)
    for place in range(2):
        put_send(send, place, part[place], losses[place][:1])


def spread_kernel(
    spot, near_o, far_o, extra_o, a, b, near_s, far_s, extra_s, image_own, image_1, rest, t_o, t_s
):
    r = image_own.shape[0]
    for core, th in ((spot[1], t_o), (1 - spot[1], t_s)):
        th[pl.ds(0, r), :] = of_core(a, core)
        th[pl.ds(r, r), :] = of_core(b, core)
    rest[...] = dot(far_o[...], t_o[r:], NN) + dot(far_s[...], t_s[r:], NN)

    @pl.when(spot[0] < 2)
    def _():
        rest[...] += dot(extra_o[...], t_o[:r], NN) + dot(extra_s[...], t_s[:r], NN)

    total = dot(near_o[...], t_o[...], NN) + dot(near_s[...], t_s[...], NN)
    image_own[...] = total[:r]
    put_rows(image_1, total[r:])


def late_pairs_kernel(log_temp, bias, spot, ih, c, rest, image_2, image_3, own, sums, send, texts, slopes):
    r = own.shape[0]
    n = 2 * r

    @pl.when(spot[0] >= 2)
    def _():
        texts[pl.ds(0, r), :] = of_core(c, spot[1])
        texts[pl.ds(r, r), :] = of_core(c, 1 - spot[1])
        slope, losses = tile(log_temp, bias, ih[n:], texts[...])
        slopes[...] = slope
        both = dot(slopes[...], ih[n:], TN)
        sums_own, sums_sibling = halved(losses, r)
        own[...] = both[:r]
        sums[...] = jnp.broadcast_to(sums_own, sums.shape)
        put_send(send, 0, both[r:], sums_sibling)
        total = rest[...] + dot(slopes[...], texts[...], NN)
        put_rows(image_2, total[:r])
        put_rows(image_3, total[r:])

    @pl.when(spot[0] < 2)
    def _():
        own[...] = jnp.zeros_like(own)
        sums[...] = jnp.zeros_like(sums)
        send[...] = jnp.zeros_like(send)
        put_rows(image_2, rest[:r])
        put_rows(image_3, rest[r:])


def joined(part, sums, got):
    r = part.shape[0]
    return part + got[:r].astype(F32), sums + tail_sum(got[r:], r)


def join_kernel(part, losses, got, late_part, late_sums, late_got, b_back, c_back):
    put_send(b_back, 0, *joined(part[1], losses[1][:1], got[1]))
    put_send(c_back, 0, *joined(late_part[...], late_sums[:1], late_got[0]))


def tangent(total, ref, log_temp):
    unit, scale = unit_of(ref)
    total = temper_of(log_temp, ref.shape[1]) * total
    return (total - unit * jnp.sum(unit * total, axis=-1, keepdims=True)) * scale


def image_end_kernel(log_temp, images, own, a, b, c, grad):
    r = own.shape[0]
    total = own[...] + a[:r].astype(F32) + b[:r].astype(F32) + c[:r].astype(F32)
    grad[...] = tangent(total, images, log_temp)


def text_end_kernel(log_temp, texts, part, losses, got, c_got, b_got, grad, loss):
    r = texts.shape[0]
    total, sums = joined(part[0], losses[0][:1], got[0])
    for ref in (c_got, b_got):
        total, sums = joined(total, sums, ref[0])
    grad[...] = tangent(total, texts, log_temp)
    loss[...] = sums / (VISITS * 4 * r)


def call(kernel, outs, name, smem, vmem, hbm=(), scratch=()):
    return pl.pallas_call(
        kernel,
        out_shape=outs,
        in_specs=[SMEM] * len(smem) + [VMEM] * len(vmem) + [HBM] * len(hbm),
        out_specs=tuple(VMEM for _ in outs),
        scratch_shapes=scratch,
        compiler_params=PARAMS,
        name=name,
    )(*smem, *vmem, *(pltpu.with_memory_space_constraint(value, pltpu.HBM) for value in hbm))


def on_device(lines, images, texts, log_temp, bias):
    r, width = images.shape
    n = 2 * r
    shape = jax.ShapeDtypeStruct
    half, long = shape((r, width), BF16), shape((r, width), F32)
    loss_rows = shape((2, 8, r), F32)
    wide = shape((r + TAIL, width), BF16)

    def send(value, name, **way):
        with jax.named_scope(name):
            return moved(value, lines, **way)

    log_temp, bias = jnp.reshape(log_temp, (1,)), jnp.reshape(bias, (1,))
    txt = lax.axis_index("txt")
    spot = jnp.stack([lax.axis_index("img") % 2 * 2 + txt // 2, txt % 2]).astype(jnp.int32)
    pairs = [[2 * k, 2 * k + 1] for k in range(4 * lines)]

    def of_both(value, name):
        with jax.named_scope(name):
            return lax.all_gather(value, AXES, axis_index_groups=pairs, axis=0, tiled=True)

    b_own = send(texts, "texts_one_up", up=1)
    c_raw = send(texts, "texts_two_up", up=2, odd_only=True)
    image_2 = send(images, "images_across", flip=2)
    image_1 = send(images, "images_beside", flip=1)
    image_3 = send(images, "images_beside_far", flip=3)
    a_raw = of_both(texts, "texts_of_both_cores")
    b_raw = of_both(b_own, "moved_texts_of_both_cores")
    ih, a_both, b_both = call(
        halves_kernel,
        (shape((4 * r, width), BF16), shape((n, width), BF16), shape((n, width), BF16)),
        "halves",
        [],
        [],
        [b_raw, a_raw, image_2, image_1, image_3, images],
        scratch=(pltpu.VMEM((8 * r, width), BF16), pltpu.SemaphoreType.DMA((6,))),
    )
    slopes = (shape((n, n), BF16), shape((n, r), BF16), shape((n, r), BF16))
    pair = pltpu.VMEM((n, width), BF16)
    near_o, far_o, extra_o, part, losses = call(
        own_pairs_kernel,
        (*slopes, shape((2, r, width), F32), loss_rows),
        "own_pairs",
        [log_temp, bias, spot],
        [ih, a_both, b_both],
        scratch=(pair,),
    )
    near_s, far_s, extra_s, text_send = call(
        sibling_pairs_kernel,
        (*slopes, shape((2, r + TAIL, width), BF16)),
        "sibling_pairs",
        [log_temp, bias, spot],
        [ih, a_both, b_both, losses],
        scratch=(pair, pltpu.VMEM((2, r, width), F32), pltpu.VMEM((2, 8, r), F32)),
    )
    (c_own,) = call(late_halves_kernel, (half,), "late_halves", [], [extra_s, c_raw])
    c_both = of_both(c_own, "late_texts_of_both_cores")
    got = send(text_send, "text_parts_sibling", other=1)
    image_own, out_1, rest = call(
        spread_kernel,
        (long, wide, shape((n, width), F32)),
        "spread",
        [spot],
        [near_o, far_o, extra_o, a_both, b_both, near_s, far_s, extra_s],
        scratch=(pair, pair),
    )
    back = shape((1, r + TAIL, width), BF16)
    out_2, out_3, late_part, late_sums, late_send = call(
        late_pairs_kernel,
        (wide, wide, long, shape((8, r), F32), back),
        "late_pairs",
        [log_temp, bias, spot],
        [ih, c_both, rest],
        scratch=(pltpu.VMEM((n, width), BF16), pltpu.VMEM((n, n), BF16)),
    )
    late_got = send(late_send, "late_text_parts_sibling", other=1)
    back_2 = send(out_2, "image_parts_across", flip=2)
    back_3 = send(out_3, "image_parts_beside_far", flip=3)
    back_1 = send(out_1, "image_parts_beside", flip=1)
    b_back, c_back = call(
        join_kernel, (back, back), "join", [], [part, losses, got, late_part, late_sums, late_got]
    )
    c_got = send(c_back, "text_parts_two_down", up=-2, odd_only=True)
    b_got = send(b_back, "text_parts_one_down", up=-1)
    (image_grad,) = call(
        image_end_kernel, (long,), "image_end", [log_temp], [images, image_own, back_1, back_2, back_3]
    )
    text_grad, loss = call(
        text_end_kernel,
        (long, shape((1, r), F32)),
        "text_end",
        [log_temp],
        [texts, part, losses, got, c_got, b_got],
    )
    return jnp.reshape(loss, (r,)), image_grad, text_grad


def solution(mesh):
    from jax.sharding import PartitionSpec as P

    lines = mesh.shape["img"] // 2
    rows = P(AXES, None)
    return jax.shard_map(
        functools.partial(on_device, lines),
        mesh=mesh,
        in_specs=(rows, rows, P(), P()),
        out_specs=(P(AXES), rows, rows),
        check_vma=False,
    )
```

time: 106 us -> 112 us (1.057)
  the two profiles are of different devices: /device:TPU:1 before, /device:TPU:4 now
where the time goes in v3:
time: 112 us; the launch traced here: 111 us
  starting transfers between devices  47.8 us (43%)
  waiting for transfers between devices  32.7 us (29%)
  Pallas kernels  17.8 us (16%)
  blocking collectives  9.15 us (8%)
  between operations  2.15 us (2%)
  local copies, waits for them, and re-layouts  1.66 us (1%)
    ppermute x12, starting transfers between devices, moved(): return lax.ppermute(value, AXES, route)  47.8 us
    ppermute x12, waiting for transfers between devices, moved(): return lax.ppermute(value, AXES, route)  32.7 us
    pallas_call x9, Pallas kernels, call(): pl.pallas_call(kernel, out_shape=outs, in_specs=[SMEM] * len(smem) + [VME...  17.8 us
    all_gather x3, blocking collectives, of_both(): lax.all_gather(value, AXES, axis_index_groups=pairs, axis=0, tiled=True)  9.15 us
  transfers between devices with their start and end apart: 12, of which 5 were waited for; matrix products, arithmetic and copies ran while one was open for 0% of the time, Pallas kernels for 15%

profile of v3, /device:TPU:4, one launch (start us, length us, event | category | flops | bytes accessed | tf_op | source)
XLA Modules:
  0.0 111.3 jit_solution(16907692189018244767)
XLA Ops:
  0.6 4.3 %collective-permute-start = (bf16[192,1152]{1,0:T(8,128)(2,1)}, bf16[192,1152]{1,0:T(8,128)(2,1)S(1)}, u32[]{:S(2)}, u32[]{:S(2)}) collective-permute-start(bf16[192,1152]{1,0:T(8,128)(2,1)} %texts.1), channel_id=1, source_target_pairs={{0,8},{1,9},{2,10},{3,11},{4,12},{5,13},{6,14},{7,15},{8,16},{9,17... | collective-permute-start | bytes 1327112 | tf_op jit(solution)/shard_map/texts_one_up/ppermute | solution.py:33
  4.9 9.1 %collective-permute-start.1 = (bf16[192,1152]{1,0:T(8,128)(2,1)}, bf16[192,1152]{1,0:T(8,128)(2,1)S(1)}, u32[]{:S(2)}, u32[]{:S(2)}) collective-permute-start(bf16[192,1152]{1,0:T(8,128)(2,1)} %images.1), channel_id=1, source_target_pairs={{0,4},{1,5},{2,6},{3,7},{4,0},{5,1},{6,2},{7,3},{8,12},{9,13},{10,... | collective-permute-start | bytes 1327112 | tf_op jit(solution)/shard_map/images_across/ppermute | solution.py:33
  14.0 1.9 %collective-permute-start.2 = (bf16[192,1152]{1,0:T(8,128)(2,1)}, bf16[192,1152]{1,0:T(8,128)(2,1)S(1)}, u32[]{:S(2)}, u32[]{:S(2)}) collective-permute-start(bf16[192,1152]{1,0:T(8,128)(2,1)} %images.1), channel_id=1, source_target_pairs={{0,2},{1,3},{2,0},{3,1},{4,6},{5,7},{6,4},{7,5},{8,10},{9,11},{10,... | collective-permute-start | bytes 1327112 | tf_op jit(solution)/shard_map/images_beside/ppermute | solution.py:33
  15.9 2.5 %collective-permute-start.3 = (bf16[192,1152]{1,0:T(8,128)(2,1)}, bf16[192,1152]{1,0:T(8,128)(2,1)S(1)}, u32[]{:S(2)}, u32[]{:S(2)}) collective-permute-start(bf16[192,1152]{1,0:T(8,128)(2,1)} %images.1), channel_id=1, source_target_pairs={{0,6},{1,7},{2,4},{3,5},{4,2},{5,3},{6,0},{7,1},{8,14},{9,15},{10,... | collective-permute-start | bytes 1327112 | tf_op jit(solution)/shard_map/images_beside_far/ppermute | solution.py:33
  18.4 2.5 %collective-permute-start.5 = (bf16[192,1152]{1,0:T(8,128)(2,1)}, bf16[192,1152]{1,0:T(8,128)(2,1)S(1)}, u32[]{:S(2)}, u32[]{:S(2)}) collective-permute-start(bf16[192,1152]{1,0:T(8,128)(2,1)} %texts.1), channel_id=1, source_target_pairs={{4,20},{5,21},{6,22},{7,23},{12,28},{13,29},{14,30},{15,31},{20,36... | collective-permute-start | bytes 1327112 | tf_op jit(solution)/shard_map/texts_two_up/ppermute | solution.py:33
  22.2 0.1 pad_add_fusion.spot
  22.3 4.1 %all_gather.10.a = bf16[384,1152]{1,0:T(8,128)(2,1)} all-gather(bf16[192,1152]{1,0:T(8,128)(2,1)} %texts.1), channel_id=1, replica_groups={{0,1},{2,3},{4,5},{6,7},{8,9},{10,11},{12,13},{14,15},{16,17},{18,19},{..., dimensions={0}, use_global_device_ids=true | all-gather | bytes 1327104 | tf_op jit(solution)/shard_map/texts_of_both_cores/all_gather | solution.py:283
  26.4 2.1 %collective-permute-done = bf16[192,1152]{1,0:T(8,128)(2,1)S(1)} collective-permute-done((bf16[192,1152]{1,0:T(8,128)(2,1)}, bf16[192,1152]{1,0:T(8,128)(2,1)S(1)}, u32[]{:S(2)}, u32[]{:S(2)}) %collective-permute-start) | collective-permute-done | bytes 442400 | tf_op jit(solution)/shard_map/texts_one_up/ppermute | solution.py:33
  28.5 2.6 %all_gather.9.b = bf16[384,1152]{1,0:T(8,128)(2,1)} all-gather(bf16[192,1152]{1,0:T(8,128)(2,1)S(1)} %collective-permute-done), channel_id=1, replica_groups={{0,1},{2,3},{4,5},{6,7},{8,9},{10,11},{12,13},{14,15},{16,17},{18,19},{..., dimensions={0}, use_global_device_ids=true | all-gather | bytes 1327104 | tf_op jit(solution)/shard_map/moved_texts_of_both_cores/all_gather | solution.py:283
  31.1 0.0 collective-permute-done.1.i2
  31.1 0.0 copy-start.2
  31.1 0.0 collective-permute-done.2.i1
  31.1 0.0 copy-start.3
  31.1 0.0 collective-permute-done.3.i3
  31.1 0.7 copy-done.2
  31.8 0.1 copy-done.3
  32.0 0.0 copy-start.4
  32.0 0.8 copy-done.4
  32.7 2.7 %halves.1 = (bf16[768,1152]{1,0:T(8,128)(2,1)S(1)}, bf16[384,1152]{1,0:T(8,128)(2,1)S(1)}, bf16[384,1152]{1,0:T(8,128)(2,1)S(1)}) custom-call(bf16[384,1152]{1,0:T(8,128)(2,1)} %all_gather.9.b, bf16[384,1152]{1,0:T(8,128)(2,1)} %all_gather.10.a, bf16[192,1152]{1,0:T(8,128)(2,1)} %copy-done.2, bf16[192,1152]{1,0:T(8,128)(2,1)} %copy-done.3, ...), custom_call_target="tpu_custom_call" | custom-call | tf_op jit(solution)/shard_map/halves/pallas_call | solution.py:253
  35.4 2.7 %own_pairs.1 = (bf16[384,384]{1,0:T(8,128)(2,1)S(1)}, bf16[384,192]{1,0:T(8,128)(2,1)S(1)}, bf16[384,192]{1,0:T(8,128)(2,1)S(1)}, f32[2,192,1152]{2,1,0:T(8,128)S(1)}, f32[2,8,192]{2,1,0:T(8,128)S(1)}) custom-call(f32[1]{0:T(128)} %bitcast.5.log_temp, f32[1]{0:T(128)} %bitcast.10.bias, s32[2]{0:T(128)S(1)} %pad_add_fusion.spot, ...), custom_call_target="tpu_custom_call" | custom-call | tf_op jit(solution)/shard_map/own_pairs/pallas_call | solution.py:253
  38.1 2.7 %sibling_pairs.1 = (bf16[384,384]{1,0:T(8,128)(2,1)S(1)}, bf16[384,192]{1,0:T(8,128)(2,1)S(1)}, bf16[384,192]{1,0:T(8,128)(2,1)S(1)}, bf16[2,208,1152]{2,1,0:T(8,128)(2,1)S(1)}) custom-call(f32[1]{0:T(128)} %bitcast.6.log_temp, f32[1]{0:T(128)} %bitcast.11.bias, s32[2]{0:T(128)S(1)} %pad_add_fusion.spot, bf16[768,1152]{1,0:T(8,128)(2,1)S(1)} %get-tuple-element.27.ih, ...), custom_call_target="tpu_custom_call" | custom-call | tf_op jit(solution)/shard_map/sibling_pairs/pallas_call | solution.py:253
  40.8 2.0 %collective-permute-start.4 = (bf16[2,208,1152]{2,1,0:T(8,128)(2,1)S(1)}, bf16[2,208,1152]{2,1,0:T(8,128)(2,1)S(1)}, u32[]{:S(2)}, u32[]{:S(2)}) collective-permute-start(bf16[2,208,1152]{2,1,0:T(8,128)(2,1)S(1)} %get-tuple-element.32), channel_id=1, source_target_pairs={{0,1},{1,0},{2,3},{3,2},{4,5},{5,4},{6,7},{7,6},{8,9},{9,8},{10,11... | collective-permute-start | bytes 2875400 | tf_op jit(solution)/shard_map/text_parts_sibling/ppermute | solution.py:33
  42.8 3.0 %spread.1 = (f32[192,1152]{1,0:T(8,128)S(1)}, bf16[208,1152]{1,0:T(8,128)(2,1)S(1)}, f32[384,1152]{1,0:T(8,128)}) custom-call(s32[2]{0:T(128)S(1)} %pad_add_fusion.spot, bf16[384,384]{1,0:T(8,128)(2,1)S(1)} %get-tuple-element.34.near_o, bf16[384,192]{1,0:T(8,128)(2,1)S(1)} %get-tuple-element.35.far_o, bf16[384,192]{1,0:T(8,128)(2,1)S(1)} %get-tuple-element.36.extra_o, ...), custom_call_target="tpu_custom_call" | custom-call | tf_op jit(solution)/shard_map/spread/pallas_call | solution.py:253
  45.8 4.3 %collective-permute-done.5.c = bf16[192,1152]{1,0:T(8,128)(2,1)S(1)} collective-permute-done((bf16[192,1152]{1,0:T(8,128)(2,1)}, bf16[192,1152]{1,0:T(8,128)(2,1)S(1)}, u32[]{:S(2)}, u32[]{:S(2)}) %collective-permute-start.5) | collective-permute-done | bytes 442400 | tf_op jit(solution)/shard_map/texts_two_up/ppermute | solution.py:33
  50.1 0.2 late_halves.1
  50.3 2.4 %all_gather.11.c = bf16[384,1152]{1,0:T(8,128)(2,1)S(1)} all-gather(bf16[192,1152]{1,0:T(8,128)(2,1)S(1)} %late_halves.1), channel_id=1, replica_groups={{0,1},{2,3},{4,5},{6,7},{8,9},{10,11},{12,13},{14,15},{16,17},{18,19},{..., dimensions={0}, use_global_device_ids=true | all-gather | bytes 1327104 | tf_op jit(solution)/shard_map/late_texts_of_both_cores/all_gather | solution.py:283
  52.8 3.6 %late_pairs.1 = (bf16[208,1152]{1,0:T(8,128)(2,1)S(1)}, bf16[208,1152]{1,0:T(8,128)(2,1)S(1)}, f32[192,1152]{1,0:T(8,128)S(1)}, f32[8,192]{1,0:T(8,128)S(1)}, bf16[1,208,1152]{2,1,0:T(8,128)(2,1)S(1)}) custom-call(f32[1]{0:T(128)} %bitcast.7.log_temp, f32[1]{0:T(128)} %bitcast.12.bias, s32[2]{0:T(128)S(1)} %pad_add_fusion.spot, ...), custom_call_target="tpu_custom_call" | custom-call | tf_op jit(solution)/shard_map/late_pairs/pallas_call | solution.py:253
  56.3 2.0 %collective-permute-start.6 = (bf16[1,208,1152]{2,1,0:T(8,128)(2,1)S(1)}, bf16[1,208,1152]{2,1,0:T(8,128)(2,1)S(1)}, u32[]{:S(2)}, u32[]{:S(2)}) collective-permute-start(bf16[1,208,1152]{2,1,0:T(8,128)(2,1)S(1)} %get-tuple-element.42), channel_id=1, source_target_pairs={{0,1},{1,0},{2,3},{3,2},{4,5},{5,4},{6,7},{7,6},{8,9},{9,8},{10,11... | collective-permute-start | bytes 1437704 | tf_op jit(solution)/shard_map/late_text_parts_sibling/ppermute | solution.py:33
  58.4 1.9 %collective-permute-start.10 = (bf16[208,1152]{1,0:T(8,128)(2,1)S(1)}, bf16[208,1152]{1,0:T(8,128)(2,1)S(1)}, u32[]{:S(2)}, u32[]{:S(2)}) collective-permute-start(bf16[208,1152]{1,0:T(8,128)(2,1)S(1)} %get-tuple-element.48), channel_id=1, source_target_pairs={{0,4},{1,5},{2,6},{3,7},{4,0},{5,1},{6,2},{7,3},{8,12},{9,13},{10,... | collective-permute-start | bytes 1437704 | tf_op jit(solution)/shard_map/image_parts_across/ppermute | solution.py:33
  60.3 4.6 %collective-permute-start.11 = (bf16[208,1152]{1,0:T(8,128)(2,1)S(1)}, bf16[208,1152]{1,0:T(8,128)(2,1)S(1)}, u32[]{:S(2)}, u32[]{:S(2)}) collective-permute-start(bf16[208,1152]{1,0:T(8,128)(2,1)S(1)} %get-tuple-element.49), channel_id=1, source_target_pairs={{0,6},{1,7},{2,4},{3,5},{4,2},{5,3},{6,0},{7,1},{8,14},{9,15},{10,... | collective-permute-start | bytes 1437704 | tf_op jit(solution)/shard_map/image_parts_beside_far/ppermute | solution.py:33
  64.9 3.9 %collective-permute-start.9 = (bf16[208,1152]{1,0:T(8,128)(2,1)S(1)}, bf16[208,1152]{1,0:T(8,128)(2,1)S(1)}, u32[]{:S(2)}, u32[]{:S(2)}) collective-permute-start(bf16[208,1152]{1,0:T(8,128)(2,1)S(1)} %get-tuple-element.47), channel_id=1, source_target_pairs={{0,2},{1,3},{2,0},{3,1},{4,6},{5,7},{6,4},{7,5},{8,10},{9,11},{10,... | collective-permute-start | bytes 1437704 | tf_op jit(solution)/shard_map/image_parts_beside/ppermute | solution.py:33
  68.9 0.0 collective-permute-done.6.late_got
  68.9 0.0 collective-permute-done.4.got
  68.9 0.0 copy-start.1
  68.9 0.2 join.1
  69.1 10.6 %collective-permute-start.7 = (bf16[1,208,1152]{2,1,0:T(8,128)(2,1)S(1)}, bf16[1,208,1152]{2,1,0:T(8,128)(2,1)S(1)}, u32[]{:S(2)}, u32[]{:S(2)}) collective-permute-start(bf16[1,208,1152]{2,1,0:T(8,128)(2,1)S(1)} %get-tuple-element.43), channel_id=1, source_target_pairs={{4,756},{5,757},{6,758},{7,759},{12,764},{13,765},{14,766},{15,767... | collective-permute-start | bytes 1437704 | tf_op jit(solution)/shard_map/text_parts_two_down/ppermute | solution.py:33
  79.7 2.5 %collective-permute-start.8 = (bf16[1,208,1152]{2,1,0:T(8,128)(2,1)S(1)}, bf16[1,208,1152]{2,1,0:T(8,128)(2,1)S(1)}, u32[]{:S(2)}, u32[]{:S(2)}) collective-permute-start(bf16[1,208,1152]{2,1,0:T(8,128)(2,1)S(1)} %get-tuple-element.44), channel_id=1, source_target_pairs={{0,760},{1,761},{2,762},{3,763},{4,764},{5,765},{6,766},{7,767},{8... | collective-permute-start | bytes 1437704 | tf_op jit(solution)/shard_map/text_parts_one_down/ppermute | solution.py:33
  82.2 0.0 collective-permute-done.10.b
  82.2 3.1 %collective-permute-done.11.c = bf16[208,1152]{1,0:T(8,128)(2,1)S(1)} collective-permute-done((bf16[208,1152]{1,0:T(8,128)(2,1)S(1)}, bf16[208,1152]{1,0:T(8,128)(2,1)S(1)}, u32[]{:S(2)}, u32[]{:S(2)}) %collective-permute-start.11) | collective-permute-done | bytes 479264 | tf_op jit(solution)/shard_map/image_parts_beside_far/ppermute | solution.py:33
  85.3 0.0 collective-permute-done.9.a
  85.3 0.0 copy-done.1
  85.3 0.0 copy-start
  85.3 1.4 %image_end.1 = f32[192,1152]{1,0:T(8,128)} custom-call(f32[1]{0:T(128)} %bitcast.9.log_temp, bf16[192,1152]{1,0:T(8,128)(2,1)S(1)} %copy-done.1, f32[192,1152]{1,0:T(8,128)S(1)} %get-tuple-element.46.own, bf16[208,1152]{1,0:T(8,128)(2,1)S(1)} %collective-permute-done.9.a, bf16[208,1152]{1,0:T(8,128)(2,1)S(1)} %collective-permute-done.10.b, ...), custom_call_target="tpu_custom_call" | custom-call | tf_op jit(solution)/shard_map/image_end/pallas_call | solution.py:253
  86.7 13.2 %collective-permute-done.7.c_got = bf16[1,208,1152]{2,1,0:T(8,128)(2,1)S(1)} collective-permute-done((bf16[1,208,1152]{2,1,0:T(8,128)(2,1)S(1)}, bf16[1,208,1152]{2,1,0:T(8,128)(2,1)S(1)}, u32[]{:S(2)}, u32[]{:S(2)}) %collective-permute-start.7) | collective-permute-done | bytes 479264 | tf_op jit(solution)/shard_map/text_parts_two_down/ppermute | solution.py:33
  99.9 10.0 %collective-permute-done.8.b_got = bf16[1,208,1152]{2,1,0:T(8,128)(2,1)S(1)} collective-permute-done((bf16[1,208,1152]{2,1,0:T(8,128)(2,1)S(1)}, bf16[1,208,1152]{2,1,0:T(8,128)(2,1)S(1)}, u32[]{:S(2)}, u32[]{:S(2)}) %collective-permute-start.8) | collective-permute-done | bytes 479264 | tf_op jit(solution)/shard_map/text_parts_one_down/ppermute | solution.py:33
  109.9 0.0 copy-done
  109.9 1.4 %text_end.1 = (f32[192,1152]{1,0:T(8,128)}, f32[1,192]{1,0:T(1,128)}) custom-call(f32[1]{0:T(128)} %bitcast.8.log_temp, bf16[192,1152]{1,0:T(8,128)(2,1)S(1)} %copy-done, f32[2,192,1152]{2,1,0:T(8,128)S(1)} %get-tuple-element.30.part, f32[2,8,192]{2,1,0:T(8,128)S(1)} %get-tuple-element.31.after.losses, bf16[2,208,1152]{2,1,0:T(8,128)(2,1)S(1)} %collective-permute-done.4.got, ...), custom_call_target="tpu_custom_call" | custom-call | tf_op jit(solution)/shard_map/text_end/pallas_call | solution.py:253
Async XLA Ops:
  0.6 27.9 %collective-permute-start = (bf16[192,1152]{1,0:T(8,128)(2,1)}, bf16[192,1152]{1,0:T(8,128)(2,1)S(1)}, u32[]{:S(2)}, u32[]{:S(2)}) collective-permute-start(bf16[192,1152]{1,0:T(8,128)(2,1)} %texts.1), channel_id=1, source_target_pairs={{0,8},{1,9},{2,10},{3,11},{4,12},{5,13},{6,14},{7,15},{8,16},{9,17... | collective-permute-start | bytes 1327112 | tf_op jit(solution)/shard_map/texts_one_up/ppermute | solution.py:33
  4.9 26.1 %collective-permute-start.1 = (bf16[192,1152]{1,0:T(8,128)(2,1)}, bf16[192,1152]{1,0:T(8,128)(2,1)S(1)}, u32[]{:S(2)}, u32[]{:S(2)}) collective-permute-start(bf16[192,1152]{1,0:T(8,128)(2,1)} %images.1), channel_id=1, source_target_pairs={{0,4},{1,5},{2,6},{3,7},{4,0},{5,1},{6,2},{7,3},{8,12},{9,13},{10,... | collective-permute-start | bytes 1327112 | tf_op jit(solution)/shard_map/images_across/ppermute | solution.py:33
  14.0 17.1 %collective-permute-start.2 = (bf16[192,1152]{1,0:T(8,128)(2,1)}, bf16[192,1152]{1,0:T(8,128)(2,1)S(1)}, u32[]{:S(2)}, u32[]{:S(2)}) collective-permute-start(bf16[192,1152]{1,0:T(8,128)(2,1)} %images.1), channel_id=1, source_target_pairs={{0,2},{1,3},{2,0},{3,1},{4,6},{5,7},{6,4},{7,5},{8,10},{9,11},{10,... | collective-permute-start | bytes 1327112 | tf_op jit(solution)/shard_map/images_beside/ppermute | solution.py:33
  15.9 15.2 %collective-permute-start.3 = (bf16[192,1152]{1,0:T(8,128)(2,1)}, bf16[192,1152]{1,0:T(8,128)(2,1)S(1)}, u32[]{:S(2)}, u32[]{:S(2)}) collective-permute-start(bf16[192,1152]{1,0:T(8,128)(2,1)} %images.1), channel_id=1, source_target_pairs={{0,6},{1,7},{2,4},{3,5},{4,2},{5,3},{6,0},{7,1},{8,14},{9,15},{10,... | collective-permute-start | bytes 1327112 | tf_op jit(solution)/shard_map/images_beside_far/ppermute | solution.py:33
  18.4 31.7 %collective-permute-start.5 = (bf16[192,1152]{1,0:T(8,128)(2,1)}, bf16[192,1152]{1,0:T(8,128)(2,1)S(1)}, u32[]{:S(2)}, u32[]{:S(2)}) collective-permute-start(bf16[192,1152]{1,0:T(8,128)(2,1)} %texts.1), channel_id=1, source_target_pairs={{4,20},{5,21},{6,22},{7,23},{12,28},{13,29},{14,30},{15,31},{20,36... | collective-permute-start | bytes 1327112 | tf_op jit(solution)/shard_map/texts_two_up/ppermute | solution.py:33
  31.1 0.8 copy-start.2
  31.1 0.9 copy-start.3
  32.0 0.8 copy-start.4
  40.8 28.1 %collective-permute-start.4 = (bf16[2,208,1152]{2,1,0:T(8,128)(2,1)S(1)}, bf16[2,208,1152]{2,1,0:T(8,128)(2,1)S(1)}, u32[]{:S(2)}, u32[]{:S(2)}) collective-permute-start(bf16[2,208,1152]{2,1,0:T(8,128)(2,1)S(1)} %get-tuple-element.32), channel_id=1, source_target_pairs={{0,1},{1,0},{2,3},{3,2},{4,5},{5,4},{6,7},{7,6},{8,9},{9,8},{10,11... | collective-permute-start | bytes 2875400 | tf_op jit(solution)/shard_map/text_parts_sibling/ppermute | solution.py:33
  56.3 12.5 %collective-permute-start.6 = (bf16[1,208,1152]{2,1,0:T(8,128)(2,1)S(1)}, bf16[1,208,1152]{2,1,0:T(8,128)(2,1)S(1)}, u32[]{:S(2)}, u32[]{:S(2)}) collective-permute-start(bf16[1,208,1152]{2,1,0:T(8,128)(2,1)S(1)} %get-tuple-element.42), channel_id=1, source_target_pairs={{0,1},{1,0},{2,3},{3,2},{4,5},{5,4},{6,7},{7,6},{8,9},{9,8},{10,11... | collective-permute-start | bytes 1437704 | tf_op jit(solution)/shard_map/late_text_parts_sibling/ppermute | solution.py:33
  58.4 23.8 %collective-permute-start.10 = (bf16[208,1152]{1,0:T(8,128)(2,1)S(1)}, bf16[208,1152]{1,0:T(8,128)(2,1)S(1)}, u32[]{:S(2)}, u32[]{:S(2)}) collective-permute-start(bf16[208,1152]{1,0:T(8,128)(2,1)S(1)} %get-tuple-element.48), channel_id=1, source_target_pairs={{0,4},{1,5},{2,6},{3,7},{4,0},{5,1},{6,2},{7,3},{8,12},{9,13},{10,... | collective-permute-start | bytes 1437704 | tf_op jit(solution)/shard_map/image_parts_across/ppermute | solution.py:33
  60.3 25.0 %collective-permute-start.11 = (bf16[208,1152]{1,0:T(8,128)(2,1)S(1)}, bf16[208,1152]{1,0:T(8,128)(2,1)S(1)}, u32[]{:S(2)}, u32[]{:S(2)}) collective-permute-start(bf16[208,1152]{1,0:T(8,128)(2,1)S(1)} %get-tuple-element.49), channel_id=1, source_target_pairs={{0,6},{1,7},{2,4},{3,5},{4,2},{5,3},{6,0},{7,1},{8,14},{9,15},{10,... | collective-permute-start | bytes 1437704 | tf_op jit(solution)/shard_map/image_parts_beside_far/ppermute | solution.py:33
  64.9 20.4 %collective-permute-start.9 = (bf16[208,1152]{1,0:T(8,128)(2,1)S(1)}, bf16[208,1152]{1,0:T(8,128)(2,1)S(1)}, u32[]{:S(2)}, u32[]{:S(2)}) collective-permute-start(bf16[208,1152]{1,0:T(8,128)(2,1)S(1)} %get-tuple-element.47), channel_id=1, source_target_pairs={{0,2},{1,3},{2,0},{3,1},{4,6},{5,7},{6,4},{7,5},{8,10},{9,11},{10,... | collective-permute-start | bytes 1437704 | tf_op jit(solution)/shard_map/image_parts_beside/ppermute | solution.py:33
  68.9 16.4 %copy-start.1 = (bf16[192,1152]{1,0:T(8,128)(2,1)S(1)}, bf16[192,1152]{1,0:T(8,128)(2,1)}, u32[]{:S(2)}) copy-start(bf16[192,1152]{1,0:T(8,128)(2,1)} %images.1) | copy-start | bytes 1327108
  69.1 30.9 %collective-permute-start.7 = (bf16[1,208,1152]{2,1,0:T(8,128)(2,1)S(1)}, bf16[1,208,1152]{2,1,0:T(8,128)(2,1)S(1)}, u32[]{:S(2)}, u32[]{:S(2)}) collective-permute-start(bf16[1,208,1152]{2,1,0:T(8,128)(2,1)S(1)} %get-tuple-element.43), channel_id=1, source_target_pairs={{4,756},{5,757},{6,758},{7,759},{12,764},{13,765},{14,766},{15,767... | collective-permute-start | bytes 1437704 | tf_op jit(solution)/shard_map/text_parts_two_down/ppermute | solution.py:33
  79.7 30.2 %collective-permute-start.8 = (bf16[1,208,1152]{2,1,0:T(8,128)(2,1)S(1)}, bf16[1,208,1152]{2,1,0:T(8,128)(2,1)S(1)}, u32[]{:S(2)}, u32[]{:S(2)}) collective-permute-start(bf16[1,208,1152]{2,1,0:T(8,128)(2,1)S(1)} %get-tuple-element.44), channel_id=1, source_target_pairs={{0,760},{1,761},{2,762},{3,763},{4,764},{5,765},{6,766},{7,767},{8... | collective-permute-start | bytes 1437704 | tf_op jit(solution)/shard_map/text_parts_one_down/ppermute | solution.py:33
  85.3 24.6 %copy-start = (bf16[192,1152]{1,0:T(8,128)(2,1)S(1)}, bf16[192,1152]{1,0:T(8,128)(2,1)}, u32[]{:S(2)}) copy-start(bf16[192,1152]{1,0:T(8,128)(2,1)} %texts.1) | copy-start | bytes 1327108

commit v4 on v3

--- a/solution.py
+++ b/solution.py
@@ -8,6 +8,7 @@
 
 EPSILON = 1e-06
 VISITS = 4
+PLANES = 12
 TAIL = 16
 AXES = ("img", "txt")
 F32, BF16 = jnp.float32, jnp.bfloat16
@@ -20,9 +21,11 @@
 PARAMS = pltpu.CompilerParams(vmem_limit_bytes=48 * 1024 * 1024)
 
 
-def moved(value, lines, up=0, flip=0, other=0, odd_only=False):
+def moved(value, lines, up=0, flip=0, other=0, odd_only=False, round_end=None):
     route = []
     for line in range(lines):
+        if round_end is not None and round_end != (line % PLANES + up < 0):
+            continue
         for x in range(4):
             if odd_only and x < 2:
                 continue
@@ -240,10 +243,10 @@
     grad[...] = tangent(total, images, log_temp)
 
 
-def text_end_kernel(log_temp, texts, part, losses, got, c_got, b_got, grad, loss):
+def text_end_kernel(log_temp, texts, part, losses, got, c_end, b_got, b_end, c_got, grad, loss):
     r = texts.shape[0]
     total, sums = joined(part[0], losses[0][:1], got[0])
-    for ref in (c_got, b_got):
+    for ref in (c_end, b_got, b_end, c_got):
         total, sums = joined(total, sums, ref[0])
     grad[...] = tangent(total, texts, log_temp)
     loss[...] = sums / (VISITS * 4 * r)
@@ -343,8 +346,10 @@
     b_back, c_back = call(
         join_kernel, (back, back), "join", [], [part, losses, got, late_part, late_sums, late_got]
     )
-    c_got = send(c_back, "text_parts_two_down", up=-2, odd_only=True)
-    b_got = send(b_back, "text_parts_one_down", up=-1)
+    c_got = send(c_back, "text_parts_two_down", up=-2, odd_only=True, round_end=False)
+    c_end = send(c_back, "end_text_parts_two_down", up=-2, odd_only=True, round_end=True)
+    b_got = send(b_back, "text_parts_one_down", up=-1, round_end=False)
+    b_end = send(b_back, "end_text_parts_one_down", up=-1, round_end=True)
     (image_grad,) = call(
         image_end_kernel, (long,), "image_end", [log_temp], [images, image_own, back_1, back_2, back_3]
     )
@@ -353,7 +358,7 @@
         (long, shape((1, r), F32)),
         "text_end",
         [log_temp],
-        [texts, part, losses, got, c_got, b_got],
+        [texts, part, losses, got, c_end, b_got, b_end, c_got],
     )
     return jnp.reshape(loss, (r,)), image_grad, text_grad
 

time: 112 us -> 114 us (1.018)
  starting transfers between devices: 47.8 us -> 58.6 us
  waiting for transfers between devices: 32.7 us -> 24.4 us
    ppermute x12 -> x14, starting transfers between devices: 47.8 us -> 58.6 us  [moved(): return lax.ppermute(value, AXES, route)]
    ppermute x12 -> x14, waiting for transfers between devices: 32.7 us -> 24.4 us  [moved(): return lax.ppermute(value, AXES, route)]
  transfers between devices with their start and end apart: 12 -> 14, of which waited for: 5 -> 6; matrix products, arithmetic and copies ran while one was open for 0% -> 0% of each run, Pallas kernels for 15% -> 14%
where the time goes in v4:
time: 114 us
  starting transfers between devices  58.6 us (51%)
  waiting for transfers between devices  24.4 us (21%)
  Pallas kernels  17.9 us (16%)
  blocking collectives  9.15 us (8%)
  between operations  2.19 us (2%)
  local copies, waits for them, and re-layouts  1.67 us (1%)
    ppermute x14, starting transfers between devices, moved(): return lax.ppermute(value, AXES, route)  58.6 us
    ppermute x14, waiting for transfers between devices, moved(): return lax.ppermute(value, AXES, route)  24.4 us
    pallas_call x9, Pallas kernels, call(): pl.pallas_call(kernel, out_shape=outs, in_specs=[SMEM] * len(smem) + [VME...  17.9 us
    all_gather x3, blocking collectives, of_both(): lax.all_gather(value, AXES, axis_index_groups=pairs, axis=0, tiled=True)  9.15 us
  transfers between devices with their start and end apart: 14, of which 6 were waited for; matrix products, arithmetic and copies ran while one was open for 0% of the time, Pallas kernels for 14%

profile of v4, /device:TPU:4, one launch (start us, length us, event | category | flops | bytes accessed | tf_op | source)
XLA Modules:
  0.0 113.9 jit_solution(18336122752717513357)
XLA Ops:
  0.6 4.3 %collective-permute-start = (bf16[192,1152]{1,0:T(8,128)(2,1)}, bf16[192,1152]{1,0:T(8,128)(2,1)S(1)}, u32[]{:S(2)}, u32[]{:S(2)}) collective-permute-start(bf16[192,1152]{1,0:T(8,128)(2,1)} %texts.1), channel_id=1, source_target_pairs={{0,8},{1,9},{2,10},{3,11},{4,12},{5,13},{6,14},{7,15},{8,16},{9,17... | collective-permute-start | bytes 1327112 | tf_op jit(solution)/shard_map/texts_one_up/ppermute | solution.py:36
  4.9 9.1 %collective-permute-start.1 = (bf16[192,1152]{1,0:T(8,128)(2,1)}, bf16[192,1152]{1,0:T(8,128)(2,1)S(1)}, u32[]{:S(2)}, u32[]{:S(2)}) collective-permute-start(bf16[192,1152]{1,0:T(8,128)(2,1)} %images.1), channel_id=1, source_target_pairs={{0,4},{1,5},{2,6},{3,7},{4,0},{5,1},{6,2},{7,3},{8,12},{9,13},{10,... | collective-permute-start | bytes 1327112 | tf_op jit(solution)/shard_map/images_across/ppermute | solution.py:36
  14.0 1.9 %collective-permute-start.2 = (bf16[192,1152]{1,0:T(8,128)(2,1)}, bf16[192,1152]{1,0:T(8,128)(2,1)S(1)}, u32[]{:S(2)}, u32[]{:S(2)}) collective-permute-start(bf16[192,1152]{1,0:T(8,128)(2,1)} %images.1), channel_id=1, source_target_pairs={{0,2},{1,3},{2,0},{3,1},{4,6},{5,7},{6,4},{7,5},{8,10},{9,11},{10,... | collective-permute-start | bytes 1327112 | tf_op jit(solution)/shard_map/images_beside/ppermute | solution.py:36
  15.9 2.5 %collective-permute-start.3 = (bf16[192,1152]{1,0:T(8,128)(2,1)}, bf16[192,1152]{1,0:T(8,128)(2,1)S(1)}, u32[]{:S(2)}, u32[]{:S(2)}) collective-permute-start(bf16[192,1152]{1,0:T(8,128)(2,1)} %images.1), channel_id=1, source_target_pairs={{0,6},{1,7},{2,4},{3,5},{4,2},{5,3},{6,0},{7,1},{8,14},{9,15},{10,... | collective-permute-start | bytes 1327112 | tf_op jit(solution)/shard_map/images_beside_far/ppermute | solution.py:36
  18.4 2.5 %collective-permute-start.5 = (bf16[192,1152]{1,0:T(8,128)(2,1)}, bf16[192,1152]{1,0:T(8,128)(2,1)S(1)}, u32[]{:S(2)}, u32[]{:S(2)}) collective-permute-start(bf16[192,1152]{1,0:T(8,128)(2,1)} %texts.1), channel_id=1, source_target_pairs={{4,20},{5,21},{6,22},{7,23},{12,28},{13,29},{14,30},{15,31},{20,36... | collective-permute-start | bytes 1327112 | tf_op jit(solution)/shard_map/texts_two_up/ppermute | solution.py:36
  22.2 0.1 pad_add_fusion.spot
  22.3 4.1 %all_gather.10.a = bf16[384,1152]{1,0:T(8,128)(2,1)} all-gather(bf16[192,1152]{1,0:T(8,128)(2,1)} %texts.1), channel_id=1, replica_groups={{0,1},{2,3},{4,5},{6,7},{8,9},{10,11},{12,13},{14,15},{16,17},{18,19},{..., dimensions={0}, use_global_device_ids=true | all-gather | bytes 1327104 | tf_op jit(solution)/shard_map/texts_of_both_cores/all_gather | solution.py:286
  26.4 2.1 %collective-permute-done = bf16[192,1152]{1,0:T(8,128)(2,1)S(1)} collective-permute-done((bf16[192,1152]{1,0:T(8,128)(2,1)}, bf16[192,1152]{1,0:T(8,128)(2,1)S(1)}, u32[]{:S(2)}, u32[]{:S(2)}) %collective-permute-start) | collective-permute-done | bytes 442400 | tf_op jit(solution)/shard_map/texts_one_up/ppermute | solution.py:36
  28.5 2.6 %all_gather.9.b = bf16[384,1152]{1,0:T(8,128)(2,1)} all-gather(bf16[192,1152]{1,0:T(8,128)(2,1)S(1)} %collective-permute-done), channel_id=1, replica_groups={{0,1},{2,3},{4,5},{6,7},{8,9},{10,11},{12,13},{14,15},{16,17},{18,19},{..., dimensions={0}, use_global_device_ids=true | all-gather | bytes 1327104 | tf_op jit(solution)/shard_map/moved_texts_of_both_cores/all_gather | solution.py:286
  31.1 0.0 collective-permute-done.1.i2
  31.1 0.0 copy-start.2
  31.1 0.0 collective-permute-done.2.i1
  31.1 0.0 copy-start.3
  31.1 0.0 collective-permute-done.3.i3
  31.1 0.7 copy-done.2
  31.8 0.1 copy-done.3
  32.0 0.0 copy-start.4
  32.0 0.8 copy-done.4
  32.7 2.7 %halves.1 = (bf16[768,1152]{1,0:T(8,128)(2,1)S(1)}, bf16[384,1152]{1,0:T(8,128)(2,1)S(1)}, bf16[384,1152]{1,0:T(8,128)(2,1)S(1)}) custom-call(bf16[384,1152]{1,0:T(8,128)(2,1)} %all_gather.9.b, bf16[384,1152]{1,0:T(8,128)(2,1)} %all_gather.10.a, bf16[192,1152]{1,0:T(8,128)(2,1)} %copy-done.2, bf16[192,1152]{1,0:T(8,128)(2,1)} %copy-done.3, ...), custom_call_target="tpu_custom_call" | custom-call | tf_op jit(solution)/shard_map/halves/pallas_call | solution.py:256
  35.4 2.7 %own_pairs.1 = (bf16[384,384]{1,0:T(8,128)(2,1)S(1)}, bf16[384,192]{1,0:T(8,128)(2,1)S(1)}, bf16[384,192]{1,0:T(8,128)(2,1)S(1)}, f32[2,192,1152]{2,1,0:T(8,128)S(1)}, f32[2,8,192]{2,1,0:T(8,128)S(1)}) custom-call(f32[1]{0:T(128)} %bitcast.5.log_temp, f32[1]{0:T(128)} %bitcast.10.bias, s32[2]{0:T(128)S(1)} %pad_add_fusion.spot, ...), custom_call_target="tpu_custom_call" | custom-call | tf_op jit(solution)/shard_map/own_pairs/pallas_call | solution.py:256
  38.1 2.7 %sibling_pairs.1 = (bf16[384,384]{1,0:T(8,128)(2,1)S(1)}, bf16[384,192]{1,0:T(8,128)(2,1)S(1)}, bf16[384,192]{1,0:T(8,128)(2,1)S(1)}, bf16[2,208,1152]{2,1,0:T(8,128)(2,1)S(1)}) custom-call(f32[1]{0:T(128)} %bitcast.6.log_temp, f32[1]{0:T(128)} %bitcast.11.bias, s32[2]{0:T(128)S(1)} %pad_add_fusion.spot, bf16[768,1152]{1,0:T(8,128)(2,1)S(1)} %get-tuple-element.27.ih, ...), custom_call_target="tpu_custom_call" | custom-call | tf_op jit(solution)/shard_map/sibling_pairs/pallas_call | solution.py:256
  40.8 2.0 %collective-permute-start.4 = (bf16[2,208,1152]{2,1,0:T(8,128)(2,1)S(1)}, bf16[2,208,1152]{2,1,0:T(8,128)(2,1)S(1)}, u32[]{:S(2)}, u32[]{:S(2)}) collective-permute-start(bf16[2,208,1152]{2,1,0:T(8,128)(2,1)S(1)} %get-tuple-element.32), channel_id=1, source_target_pairs={{0,1},{1,0},{2,3},{3,2},{4,5},{5,4},{6,7},{7,6},{8,9},{9,8},{10,11... | collective-permute-start | bytes 2875400 | tf_op jit(solution)/shard_map/text_parts_sibling/ppermute | solution.py:36
  42.8 3.0 %spread.1 = (f32[192,1152]{1,0:T(8,128)S(1)}, bf16[208,1152]{1,0:T(8,128)(2,1)S(1)}, f32[384,1152]{1,0:T(8,128)}) custom-call(s32[2]{0:T(128)S(1)} %pad_add_fusion.spot, bf16[384,384]{1,0:T(8,128)(2,1)S(1)} %get-tuple-element.34.near_o, bf16[384,192]{1,0:T(8,128)(2,1)S(1)} %get-tuple-element.35.far_o, bf16[384,192]{1,0:T(8,128)(2,1)S(1)} %get-tuple-element.36.extra_o, ...), custom_call_target="tpu_custom_call" | custom-call | tf_op jit(solution)/shard_map/spread/pallas_call | solution.py:256
  45.8 4.3 %collective-permute-done.5.c = bf16[192,1152]{1,0:T(8,128)(2,1)S(1)} collective-permute-done((bf16[192,1152]{1,0:T(8,128)(2,1)}, bf16[192,1152]{1,0:T(8,128)(2,1)S(1)}, u32[]{:S(2)}, u32[]{:S(2)}) %collective-permute-start.5) | collective-permute-done | bytes 442400 | tf_op jit(solution)/shard_map/texts_two_up/ppermute | solution.py:36
  50.1 0.2 late_halves.1
  50.3 2.4 %all_gather.11.c = bf16[384,1152]{1,0:T(8,128)(2,1)S(1)} all-gather(bf16[192,1152]{1,0:T(8,128)(2,1)S(1)} %late_halves.1), channel_id=1, replica_groups={{0,1},{2,3},{4,5},{6,7},{8,9},{10,11},{12,13},{14,15},{16,17},{18,19},{..., dimensions={0}, use_global_device_ids=true | all-gather | bytes 1327104 | tf_op jit(solution)/shard_map/late_texts_of_both_cores/all_gather | solution.py:286
  52.8 3.6 %late_pairs.1 = (bf16[208,1152]{1,0:T(8,128)(2,1)S(1)}, bf16[208,1152]{1,0:T(8,128)(2,1)S(1)}, f32[192,1152]{1,0:T(8,128)S(1)}, f32[8,192]{1,0:T(8,128)S(1)}, bf16[1,208,1152]{2,1,0:T(8,128)(2,1)S(1)}) custom-call(f32[1]{0:T(128)} %bitcast.7.log_temp, f32[1]{0:T(128)} %bitcast.12.bias, s32[2]{0:T(128)S(1)} %pad_add_fusion.spot, ...), custom_call_target="tpu_custom_call" | custom-call | tf_op jit(solution)/shard_map/late_pairs/pallas_call | solution.py:256
  56.3 2.0 %collective-permute-start.6 = (bf16[1,208,1152]{2,1,0:T(8,128)(2,1)S(1)}, bf16[1,208,1152]{2,1,0:T(8,128)(2,1)S(1)}, u32[]{:S(2)}, u32[]{:S(2)}) collective-permute-start(bf16[1,208,1152]{2,1,0:T(8,128)(2,1)S(1)} %get-tuple-element.42), channel_id=1, source_target_pairs={{0,1},{1,0},{2,3},{3,2},{4,5},{5,4},{6,7},{7,6},{8,9},{9,8},{10,11... | collective-permute-start | bytes 1437704 | tf_op jit(solution)/shard_map/late_text_parts_sibling/ppermute | solution.py:36
  58.4 1.9 %collective-permute-start.12 = (bf16[208,1152]{1,0:T(8,128)(2,1)S(1)}, bf16[208,1152]{1,0:T(8,128)(2,1)S(1)}, u32[]{:S(2)}, u32[]{:S(2)}) collective-permute-start(bf16[208,1152]{1,0:T(8,128)(2,1)S(1)} %get-tuple-element.48), channel_id=1, source_target_pairs={{0,4},{1,5},{2,6},{3,7},{4,0},{5,1},{6,2},{7,3},{8,12},{9,13},{10,... | collective-permute-start | bytes 1437704 | tf_op jit(solution)/shard_map/image_parts_across/ppermute | solution.py:36
  60.3 4.6 %collective-permute-start.13 = (bf16[208,1152]{1,0:T(8,128)(2,1)S(1)}, bf16[208,1152]{1,0:T(8,128)(2,1)S(1)}, u32[]{:S(2)}, u32[]{:S(2)}) collective-permute-start(bf16[208,1152]{1,0:T(8,128)(2,1)S(1)} %get-tuple-element.49), channel_id=1, source_target_pairs={{0,6},{1,7},{2,4},{3,5},{4,2},{5,3},{6,0},{7,1},{8,14},{9,15},{10,... | collective-permute-start | bytes 1437704 | tf_op jit(solution)/shard_map/image_parts_beside_far/ppermute | solution.py:36
  64.9 3.9 %collective-permute-start.11 = (bf16[208,1152]{1,0:T(8,128)(2,1)S(1)}, bf16[208,1152]{1,0:T(8,128)(2,1)S(1)}, u32[]{:S(2)}, u32[]{:S(2)}) collective-permute-start(bf16[208,1152]{1,0:T(8,128)(2,1)S(1)} %get-tuple-element.47), channel_id=1, source_target_pairs={{0,2},{1,3},{2,0},{3,1},{4,6},{5,7},{6,4},{7,5},{8,10},{9,11},{10,... | collective-permute-start | bytes 1437704 | tf_op jit(solution)/shard_map/image_parts_beside/ppermute | solution.py:36
  68.9 0.0 collective-permute-done.6.late_got
  68.9 0.0 collective-permute-done.4.got
  68.9 0.0 copy-start
  68.9 0.2 join.1
  69.1 1.3 %collective-permute-start.10 = (bf16[1,208,1152]{2,1,0:T(8,128)(2,1)S(1)}, bf16[1,208,1152]{2,1,0:T(8,128)(2,1)S(1)}, u32[]{:S(2)}, u32[]{:S(2)}) collective-permute-start(bf16[1,208,1152]{2,1,0:T(8,128)(2,1)S(1)} %get-tuple-element.43), channel_id=1, source_target_pairs={{20,4},{21,5},{22,6},{23,7},{28,12},{29,13},{30,14},{31,15},{36,20... | collective-permute-start | bytes 1437704 | tf_op jit(solution)/shard_map/text_parts_two_down/ppermute | solution.py:36
  70.4 11.9 %collective-permute-start.7 = (bf16[1,208,1152]{2,1,0:T(8,128)(2,1)S(1)}, bf16[1,208,1152]{2,1,0:T(8,128)(2,1)S(1)}, u32[]{:S(2)}, u32[]{:S(2)}) collective-permute-start(bf16[1,208,1152]{2,1,0:T(8,128)(2,1)S(1)} %get-tuple-element.43), channel_id=1, source_target_pairs={{4,756},{5,757},{6,758},{7,759},{12,764},{13,765},{14,766},{15,767... | collective-permute-start | bytes 1437704 | tf_op jit(solution)/shard_map/end_text_parts_two_down/ppermute | solution.py:36
  82.2 0.0 collective-permute-done.12.b
  82.2 1.3 %collective-permute-start.8 = (bf16[1,208,1152]{2,1,0:T(8,128)(2,1)S(1)}, bf16[1,208,1152]{2,1,0:T(8,128)(2,1)S(1)}, u32[]{:S(2)}, u32[]{:S(2)}) collective-permute-start(bf16[1,208,1152]{2,1,0:T(8,128)(2,1)S(1)} %get-tuple-element.44), channel_id=1, source_target_pairs={{8,0},{9,1},{10,2},{11,3},{12,4},{13,5},{14,6},{15,7},{16,8},{17,9... | collective-permute-start | bytes 1437704 | tf_op jit(solution)/shard_map/text_parts_one_down/ppermute | solution.py:36
  83.5 1.8 %collective-permute-done.13.c = bf16[208,1152]{1,0:T(8,128)(2,1)S(1)} collective-permute-done((bf16[208,1152]{1,0:T(8,128)(2,1)S(1)}, bf16[208,1152]{1,0:T(8,128)(2,1)S(1)}, u32[]{:S(2)}, u32[]{:S(2)}) %collective-permute-start.13) | collective-permute-done | bytes 479264 | tf_op jit(solution)/shard_map/image_parts_beside_far/ppermute | solution.py:36
  85.3 9.4 %collective-permute-start.9 = (bf16[1,208,1152]{2,1,0:T(8,128)(2,1)S(1)}, bf16[1,208,1152]{2,1,0:T(8,128)(2,1)S(1)}, u32[]{:S(2)}, u32[]{:S(2)}) collective-permute-start(bf16[1,208,1152]{2,1,0:T(8,128)(2,1)S(1)} %get-tuple-element.44), channel_id=1, source_target_pairs={{0,760},{1,761},{2,762},{3,763},{4,764},{5,765},{6,766},{7,767},{9... | collective-permute-start | bytes 1437704 | tf_op jit(solution)/shard_map/end_text_parts_one_down/ppermute | solution.py:36
  94.7 0.0 collective-permute-done.11.a
  94.7 0.0 copy-done
  94.7 0.0 copy-start.1
  94.7 1.4 %image_end.1 = f32[192,1152]{1,0:T(8,128)} custom-call(f32[1]{0:T(128)} %bitcast.9.log_temp, bf16[192,1152]{1,0:T(8,128)(2,1)S(1)} %copy-done, f32[192,1152]{1,0:T(8,128)S(1)} %get-tuple-element.46.own, bf16[208,1152]{1,0:T(8,128)(2,1)S(1)} %collective-permute-done.11.a, bf16[208,1152]{1,0:T(8,128)(2,1)S(1)} %collective-permute-done.12.b, ...), custom_call_target="tpu_custom_call" | custom-call | tf_op jit(solution)/shard_map/image_end/pallas_call | solution.py:256
  96.2 0.0 collective-permute-done.10.c_got
  96.2 7.0 %collective-permute-done.7.c_end = bf16[1,208,1152]{2,1,0:T(8,128)(2,1)S(1)} collective-permute-done((bf16[1,208,1152]{2,1,0:T(8,128)(2,1)S(1)}, bf16[1,208,1152]{2,1,0:T(8,128)(2,1)S(1)}, u32[]{:S(2)}, u32[]{:S(2)}) %collective-permute-start.7) | collective-permute-done | bytes 479264 | tf_op jit(solution)/shard_map/end_text_parts_two_down/ppermute | solution.py:36
  103.2 6.4 %collective-permute-done.8.b_got = bf16[1,208,1152]{2,1,0:T(8,128)(2,1)S(1)} collective-permute-done((bf16[1,208,1152]{2,1,0:T(8,128)(2,1)S(1)}, bf16[1,208,1152]{2,1,0:T(8,128)(2,1)S(1)}, u32[]{:S(2)}, u32[]{:S(2)}) %collective-permute-start.8) | collective-permute-done | bytes 479264 | tf_op jit(solution)/shard_map/text_parts_one_down/ppermute | solution.py:36
  109.6 2.8 %collective-permute-done.9.b_end = bf16[1,208,1152]{2,1,0:T(8,128)(2,1)S(1)} collective-permute-done((bf16[1,208,1152]{2,1,0:T(8,128)(2,1)S(1)}, bf16[1,208,1152]{2,1,0:T(8,128)(2,1)S(1)}, u32[]{:S(2)}, u32[]{:S(2)}) %collective-permute-start.9) | collective-permute-done | bytes 479264 | tf_op jit(solution)/shard_map/end_text_parts_one_down/ppermute | solution.py:36
  112.4 0.0 copy-done.1
  112.4 1.5 %text_end.1 = (f32[192,1152]{1,0:T(8,128)}, f32[1,192]{1,0:T(1,128)}) custom-call(f32[1]{0:T(128)} %bitcast.8.log_temp, bf16[192,1152]{1,0:T(8,128)(2,1)S(1)} %copy-done.1, f32[2,192,1152]{2,1,0:T(8,128)S(1)} %get-tuple-element.30.part, f32[2,8,192]{2,1,0:T(8,128)S(1)} %get-tuple-element.31.after.losses, ...), custom_call_target="tpu_custom_call" | custom-call | tf_op jit(solution)/shard_map/text_end/pallas_call | solution.py:256
Async XLA Ops:
  0.6 27.9 %collective-permute-start = (bf16[192,1152]{1,0:T(8,128)(2,1)}, bf16[192,1152]{1,0:T(8,128)(2,1)S(1)}, u32[]{:S(2)}, u32[]{:S(2)}) collective-permute-start(bf16[192,1152]{1,0:T(8,128)(2,1)} %texts.1), channel_id=1, source_target_pairs={{0,8},{1,9},{2,10},{3,11},{4,12},{5,13},{6,14},{7,15},{8,16},{9,17... | collective-permute-start | bytes 1327112 | tf_op jit(solution)/shard_map/texts_one_up/ppermute | solution.py:36
  4.9 26.1 %collective-permute-start.1 = (bf16[192,1152]{1,0:T(8,128)(2,1)}, bf16[192,1152]{1,0:T(8,128)(2,1)S(1)}, u32[]{:S(2)}, u32[]{:S(2)}) collective-permute-start(bf16[192,1152]{1,0:T(8,128)(2,1)} %images.1), channel_id=1, source_target_pairs={{0,4},{1,5},{2,6},{3,7},{4,0},{5,1},{6,2},{7,3},{8,12},{9,13},{10,... | collective-permute-start | bytes 1327112 | tf_op jit(solution)/shard_map/images_across/ppermute | solution.py:36
  14.0 17.1 %collective-permute-start.2 = (bf16[192,1152]{1,0:T(8,128)(2,1)}, bf16[192,1152]{1,0:T(8,128)(2,1)S(1)}, u32[]{:S(2)}, u32[]{:S(2)}) collective-permute-start(bf16[192,1152]{1,0:T(8,128)(2,1)} %images.1), channel_id=1, source_target_pairs={{0,2},{1,3},{2,0},{3,1},{4,6},{5,7},{6,4},{7,5},{8,10},{9,11},{10,... | collective-permute-start | bytes 1327112 | tf_op jit(solution)/shard_map/images_beside/ppermute | solution.py:36
  15.9 15.2 %collective-permute-start.3 = (bf16[192,1152]{1,0:T(8,128)(2,1)}, bf16[192,1152]{1,0:T(8,128)(2,1)S(1)}, u32[]{:S(2)}, u32[]{:S(2)}) collective-permute-start(bf16[192,1152]{1,0:T(8,128)(2,1)} %images.1), channel_id=1, source_target_pairs={{0,6},{1,7},{2,4},{3,5},{4,2},{5,3},{6,0},{7,1},{8,14},{9,15},{10,... | collective-permute-start | bytes 1327112 | tf_op jit(solution)/shard_map/images_beside_far/ppermute | solution.py:36
  18.4 31.7 %collective-permute-start.5 = (bf16[192,1152]{1,0:T(8,128)(2,1)}, bf16[192,1152]{1,0:T(8,128)(2,1)S(1)}, u32[]{:S(2)}, u32[]{:S(2)}) collective-permute-start(bf16[192,1152]{1,0:T(8,128)(2,1)} %texts.1), channel_id=1, source_target_pairs={{4,20},{5,21},{6,22},{7,23},{12,28},{13,29},{14,30},{15,31},{20,36... | collective-permute-start | bytes 1327112 | tf_op jit(solution)/shard_map/texts_two_up/ppermute | solution.py:36
  31.1 0.8 copy-start.2
  31.1 0.9 copy-start.3
  32.0 0.8 copy-start.4
  40.8 28.1 %collective-permute-start.4 = (bf16[2,208,1152]{2,1,0:T(8,128)(2,1)S(1)}, bf16[2,208,1152]{2,1,0:T(8,128)(2,1)S(1)}, u32[]{:S(2)}, u32[]{:S(2)}) collective-permute-start(bf16[2,208,1152]{2,1,0:T(8,128)(2,1)S(1)} %get-tuple-element.32), channel_id=1, source_target_pairs={{0,1},{1,0},{2,3},{3,2},{4,5},{5,4},{6,7},{7,6},{8,9},{9,8},{10,11... | collective-permute-start | bytes 2875400 | tf_op jit(solution)/shard_map/text_parts_sibling/ppermute | solution.py:36
  56.3 12.5 %collective-permute-start.6 = (bf16[1,208,1152]{2,1,0:T(8,128)(2,1)S(1)}, bf16[1,208,1152]{2,1,0:T(8,128)(2,1)S(1)}, u32[]{:S(2)}, u32[]{:S(2)}) collective-permute-start(bf16[1,208,1152]{2,1,0:T(8,128)(2,1)S(1)} %get-tuple-element.42), channel_id=1, source_target_pairs={{0,1},{1,0},{2,3},{3,2},{4,5},{5,4},{6,7},{7,6},{8,9},{9,8},{10,11... | collective-permute-start | bytes 1437704 | tf_op jit(solution)/shard_map/late_text_parts_sibling/ppermute | solution.py:36
  58.4 23.8 %collective-permute-start.12 = (bf16[208,1152]{1,0:T(8,128)(2,1)S(1)}, bf16[208,1152]{1,0:T(8,128)(2,1)S(1)}, u32[]{:S(2)}, u32[]{:S(2)}) collective-permute-start(bf16[208,1152]{1,0:T(8,128)(2,1)S(1)} %get-tuple-element.48), channel_id=1, source_target_pairs={{0,4},{1,5},{2,6},{3,7},{4,0},{5,1},{6,2},{7,3},{8,12},{9,13},{10,... | collective-permute-start | bytes 1437704 | tf_op jit(solution)/shard_map/image_parts_across/ppermute | solution.py:36
  60.3 25.0 %collective-permute-start.13 = (bf16[208,1152]{1,0:T(8,128)(2,1)S(1)}, bf16[208,1152]{1,0:T(8,128)(2,1)S(1)}, u32[]{:S(2)}, u32[]{:S(2)}) collective-permute-start(bf16[208,1152]{1,0:T(8,128)(2,1)S(1)} %get-tuple-element.49), channel_id=1, source_target_pairs={{0,6},{1,7},{2,4},{3,5},{4,2},{5,3},{6,0},{7,1},{8,14},{9,15},{10,... | collective-permute-start | bytes 1437704 | tf_op jit(solution)/shard_map/image_parts_beside_far/ppermute | solution.py:36
  64.9 29.8 %collective-permute-start.11 = (bf16[208,1152]{1,0:T(8,128)(2,1)S(1)}, bf16[208,1152]{1,0:T(8,128)(2,1)S(1)}, u32[]{:S(2)}, u32[]{:S(2)}) collective-permute-start(bf16[208,1152]{1,0:T(8,128)(2,1)S(1)} %get-tuple-element.47), channel_id=1, source_target_pairs={{0,2},{1,3},{2,0},{3,1},{4,6},{5,7},{6,4},{7,5},{8,10},{9,11},{10,... | collective-permute-start | bytes 1437704 | tf_op jit(solution)/shard_map/image_parts_beside/ppermute | solution.py:36
  68.9 25.9 %copy-start = (bf16[192,1152]{1,0:T(8,128)(2,1)S(1)}, bf16[192,1152]{1,0:T(8,128)(2,1)}, u32[]{:S(2)}) copy-start(bf16[192,1152]{1,0:T(8,128)(2,1)} %images.1) | copy-start | bytes 1327108
  69.1 27.1 %collective-permute-start.10 = (bf16[1,208,1152]{2,1,0:T(8,128)(2,1)S(1)}, bf16[1,208,1152]{2,1,0:T(8,128)(2,1)S(1)}, u32[]{:S(2)}, u32[]{:S(2)}) collective-permute-start(bf16[1,208,1152]{2,1,0:T(8,128)(2,1)S(1)} %get-tuple-element.43), channel_id=1, source_target_pairs={{20,4},{21,5},{22,6},{23,7},{28,12},{29,13},{30,14},{31,15},{36,20... | collective-permute-start | bytes 1437704 | tf_op jit(solution)/shard_map/text_parts_two_down/ppermute | solution.py:36
  70.4 32.8 %collective-permute-start.7 = (bf16[1,208,1152]{2,1,0:T(8,128)(2,1)S(1)}, bf16[1,208,1152]{2,1,0:T(8,128)(2,1)S(1)}, u32[]{:S(2)}, u32[]{:S(2)}) collective-permute-start(bf16[1,208,1152]{2,1,0:T(8,128)(2,1)S(1)} %get-tuple-element.43), channel_id=1, source_target_pairs={{4,756},{5,757},{6,758},{7,759},{12,764},{13,765},{14,766},{15,767... | collective-permute-start | bytes 1437704 | tf_op jit(solution)/shard_map/end_text_parts_two_down/ppermute | solution.py:36
  82.2 27.4 %collective-permute-start.8 = (bf16[1,208,1152]{2,1,0:T(8,128)(2,1)S(1)}, bf16[1,208,1152]{2,1,0:T(8,128)(2,1)S(1)}, u32[]{:S(2)}, u32[]{:S(2)}) collective-permute-start(bf16[1,208,1152]{2,1,0:T(8,128)(2,1)S(1)} %get-tuple-element.44), channel_id=1, source_target_pairs={{8,0},{9,1},{10,2},{11,3},{12,4},{13,5},{14,6},{15,7},{16,8},{17,9... | collective-permute-start | bytes 1437704 | tf_op jit(solution)/shard_map/text_parts_one_down/ppermute | solution.py:36
  85.3 27.1 %collective-permute-start.9 = (bf16[1,208,1152]{2,1,0:T(8,128)(2,1)S(1)}, bf16[1,208,1152]{2,1,0:T(8,128)(2,1)S(1)}, u32[]{:S(2)}, u32[]{:S(2)}) collective-permute-start(bf16[1,208,1152]{2,1,0:T(8,128)(2,1)S(1)} %get-tuple-element.44), channel_id=1, source_target_pairs={{0,760},{1,761},{2,762},{3,763},{4,764},{5,765},{6,766},{7,767},{9... | collective-permute-start | bytes 1437704 | tf_op jit(solution)/shard_map/end_text_parts_one_down/ppermute | solution.py:36
  94.7 17.7 %copy-start.1 = (bf16[192,1152]{1,0:T(8,128)(2,1)S(1)}, bf16[192,1152]{1,0:T(8,128)(2,1)}, u32[]{:S(2)}) copy-start(bf16[192,1152]{1,0:T(8,128)(2,1)} %texts.1) | copy-start | bytes 1327108

commit v5 on v2

--- a/solution.py
+++ b/solution.py
@@ -84,13 +84,17 @@
         ih[pl.ds(k * r, r), :] = half_of(raw.at[3 + k])
 
 
-def band(scalars, ih, th, p, diagonal):
+def temper_of(log_temp, lanes):
+    return jnp.exp(jnp.full((1, lanes), log_temp[0], F32))
+
+
+def band(log_temp, bias, ih, th, p, diagonal):
     r = th.shape[0] // 3
     n = 2 * r
-    temper, bias = scalars[0], scalars[1]
+    temper = temper_of(log_temp, n)
     sums, parts = [], []
     for half in range(2):
-        logits = bias + temper * lax.dot_general(
+        logits = bias[0] + temper * lax.dot_general(
             ih[pl.ds(half * n, n), :], th[pl.ds(half * r, n), :], NT, preferred_element_type=F32
         )
         margin = logits
@@ -101,16 +105,17 @@
             margin = jnp.where(positive, -logits, logits)
         grown = jnp.exp(margin)
         whole = 1.0 + grown
-        slope = grown / whole
-        losses = jnp.where(
-            grown < 0.00390625,
-            grown * (1.0 - grown * (0.5 - grown * (1.0 / 3.0))),
-            jnp.log(whole),
-        )
+        inverse = pl.reciprocal(whole, approx=True)
+        inverse = inverse * (2.0 - whole * inverse)
+        slope = grown * inverse
+        left = (grown - (whole - 1.0)) * inverse
         if diagonal and half == 0:
             slope = jnp.where(positive, -slope, slope)
         p[pl.ds(half * n, n), :] = slope.astype(BF16)
-        losses = jnp.sum(losses.reshape(n // 8, 8, n), axis=0)
+        q = n // 4
+        product = (whole[:q] * whole[q : 2 * q]) * (whole[2 * q : 3 * q] * whole[3 * q :])
+        left = (left[:q] + left[q : 2 * q]) + (left[2 * q : 3 * q] + left[3 * q :])
+        losses = jnp.sum((jnp.log(product) + left).reshape(q // 8, 8, n), axis=0)
         sums.append(jnp.broadcast_to(jnp.sum(losses, axis=0, keepdims=True), (8, n)))
     for half in range(2):
         parts.append(
@@ -125,16 +130,16 @@
     )
 
 
-def own_pairs_kernel(scalars, ih, th, p, own, sums):
-    parts, losses = band(scalars, ih, th, p, True)
+def own_pairs_kernel(log_temp, bias, ih, th, p, own, sums):
+    parts, losses = band(log_temp, bias, ih, th, p, True)
     for place in range(3):
         own[place] = parts[place]
         sums[place] = losses[place]
 
 
-def sibling_pairs_kernel(scalars, ih, th, after, p, send):
+def sibling_pairs_kernel(log_temp, bias, ih, th, after, p, send):
     del after
-    parts, losses = band(scalars, ih, th, p, False)
+    parts, losses = band(log_temp, bias, ih, th, p, False)
     r, width = parts[0].shape
     for place in range(3):
         send[place, pl.ds(0, r), :] = parts[place].astype(BF16)
@@ -166,18 +171,18 @@
         out[pl.ds(r, TAIL), pl.ds(0, n)] = tail_of(loss)
 
 
-def tangent(total, ref, temper):
+def tangent(total, ref, log_temp):
     unit, scale = unit_of(ref)
-    total = temper * total
+    total = temper_of(log_temp, ref.shape[1]) * total
     return (total - unit * jnp.sum(unit * total, axis=-1, keepdims=True)) * scale
 
 
-def image_end_kernel(scalars, images, own, a, b, c, grad):
+def image_end_kernel(log_temp, images, own, a, b, c, grad):
     total = own[...] + a[...].astype(F32) + b[...].astype(F32) + c[...].astype(F32)
-    grad[...] = tangent(total, images, scalars[0])
-
-
-def text_end_kernel(scalars, spot, texts, own, got, sums, b_got, c_got, grad, loss):
+    grad[...] = tangent(total, images, log_temp)
+
+
+def text_end_kernel(log_temp, spot, texts, own, got, sums, b_got, c_got, grad, loss):
     r = texts.shape[0]
     n = sums.shape[2]
 
@@ -193,8 +198,8 @@
     for ref in (b_got, c_got):
         total = total + ref[pl.ds(0, r), :].astype(F32)
         losses = losses + tail_sum(ref[pl.ds(r, TAIL), :], n)
-    grad[...] = tangent(total, texts, scalars[0])
-    loss[...] = jnp.broadcast_to(losses / (VISITS * 4 * r), loss.shape)
+    grad[...] = tangent(total, texts, log_temp)
+    loss[...] = losses[:, :r] / (VISITS * 4 * r)
 
 
 def call(kernel, outs, name, smem, vmem, hbm=(), scratch=()):
@@ -219,7 +224,7 @@
         with jax.named_scope(name):
             return moved(value, lines, **way)
 
-    scalars = jnp.stack([jnp.exp(log_temp), bias])
+    log_temp, bias = jnp.reshape(log_temp, (1,)), jnp.reshape(bias, (1,))
     spot = lax.axis_index("img") % 2 * 2 + lax.axis_index("txt") // 2
     spot = jnp.reshape(spot, (1,)).astype(jnp.int32)
     c_own = send(texts, "texts_two_up", up=2, odd_only=True)
@@ -242,14 +247,14 @@
         own_pairs_kernel,
         (slopes, shape((3, r, width), F32), shape((3, 8, n), F32)),
         "own_pairs",
-        [scalars],
+        [log_temp, bias],
         [ih, t_own],
     )
     p_sib, text_send = call(
         sibling_pairs_kernel,
         (slopes, shape((3, r + TAIL, width), BF16)),
         "sibling_pairs",
-        [scalars],
+        [log_temp, bias],
         [ih, t_sib, sums],
     )
     got = send(text_send, "text_parts_sibling", other=1)
@@ -264,16 +269,16 @@
     c_got = send(c_back, "text_parts_two_down", up=-2, odd_only=True)
     b_got = send(b_back, "text_parts_one_down", up=-1)
     (image_grad,) = call(
-        image_end_kernel, (long,), "image_end", [scalars], [images, image_own, back_1, back_2, back_3]
+        image_end_kernel, (long,), "image_end", [log_temp], [images, image_own, back_1, back_2, back_3]
     )
     text_grad, loss = call(
         text_end_kernel,
-        (long, shape((8, n), F32)),
+        (long, shape((1, r), F32)),
         "text_end",
-        [scalars, spot],
+        [log_temp, spot],
         [texts, own, got, sums, b_got, c_got],
     )
-    return loss[0, :r], image_grad, text_grad
+    return jnp.reshape(loss, (r,)), image_grad, text_grad
 
 
 def solution(mesh):

time: 106 us -> 103 us (0.972)
  Pallas kernels: 18.3 us -> 16.8 us
    pallas_call x7, Pallas kernels: 18.3 us -> 16.8 us  [call(): pl.pallas_call(kernel, out_shape=outs, in_specs=[SMEM] * len(smem) + [VME...]
  transfers between devices with their start and end apart: 12 -> 12, of which waited for: 5 -> 5; matrix products, arithmetic and copies ran while one was open for 0% -> 0% of each run, Pallas kernels for 10% -> 9%
where the time goes in v5:
time: 103 us
  starting transfers between devices  48.8 us (47%)
  waiting for transfers between devices  34.4 us (33%)
  Pallas kernels  16.8 us (16%)
  between operations  2.15 us (2%)
    ppermute x12, starting transfers between devices, moved(): return lax.ppermute(value, AXES, route)  48.8 us
    ppermute x12, waiting for transfers between devices, moved(): return lax.ppermute(value, AXES, route)  34.4 us
    pallas_call x7, Pallas kernels, call(): pl.pallas_call(kernel, out_shape=outs, in_specs=[SMEM] * len(smem) + [VME...  16.8 us
  transfers between devices with their start and end apart: 12, of which 5 were waited for; matrix products, arithmetic and copies ran while one was open for 0% of the time, Pallas kernels for 9%

profile of v5, /device:TPU:1, one launch (start us, length us, event | category | flops | bytes accessed | tf_op | source)
XLA Modules:
  0.0 102.9 jit_solution(10174430894722787955)
XLA Ops:
  0.6 0.7 collective-permute-start
  1.3 10.6 %collective-permute-start.1 = (bf16[192,1152]{1,0:T(8,128)(2,1)}, bf16[192,1152]{1,0:T(8,128)(2,1)S(1)}, u32[]{:S(2)}, u32[]{:S(2)}) collective-permute-start(bf16[192,1152]{1,0:T(8,128)(2,1)} %images.1), channel_id=1, source_target_pairs={{0,4},{1,5},{2,6},{3,7},{4,0},{5,1},{6,2},{7,3},{8,12},{9,13},{10,... | collective-permute-start | bytes 1327112 | tf_op jit(solution)/shard_map/images_across/ppermute | solution.py:33
  11.9 2.2 %collective-permute-start.2 = (bf16[192,1152]{1,0:T(8,128)(2,1)}, bf16[192,1152]{1,0:T(8,128)(2,1)S(1)}, u32[]{:S(2)}, u32[]{:S(2)}) collective-permute-start(bf16[192,1152]{1,0:T(8,128)(2,1)} %images.1), channel_id=1, source_target_pairs={{0,2},{1,3},{2,0},{3,1},{4,6},{5,7},{6,4},{7,5},{8,10},{9,11},{10,... | collective-permute-start | bytes 1327112 | tf_op jit(solution)/shard_map/images_beside/ppermute | solution.py:33
  14.2 1.9 %collective-permute-start.3 = (bf16[192,1152]{1,0:T(8,128)(2,1)}, bf16[192,1152]{1,0:T(8,128)(2,1)S(1)}, u32[]{:S(2)}, u32[]{:S(2)}) collective-permute-start(bf16[192,1152]{1,0:T(8,128)(2,1)} %images.1), channel_id=1, source_target_pairs={{0,6},{1,7},{2,4},{3,5},{4,2},{5,3},{6,0},{7,1},{8,14},{9,15},{10,... | collective-permute-start | bytes 1327112 | tf_op jit(solution)/shard_map/images_beside_far/ppermute | solution.py:33
  16.1 4.0 %collective-permute-start.4 = (bf16[192,1152]{1,0:T(8,128)(2,1)}, bf16[192,1152]{1,0:T(8,128)(2,1)S(1)}, u32[]{:S(2)}, u32[]{:S(2)}) collective-permute-start(bf16[192,1152]{1,0:T(8,128)(2,1)} %texts.1), channel_id=1, source_target_pairs={{0,8},{1,9},{2,10},{3,11},{4,12},{5,13},{6,14},{7,15},{8,16},{9,17... | collective-permute-start | bytes 1327112 | tf_op jit(solution)/shard_map/texts_one_up/ppermute | solution.py:33
  20.1 0.0 collective-permute-done.c
  20.1 0.0 copy-start.3
  20.2 0.0 collective-permute-done.1.i2
  20.2 0.0 copy-start.4
  20.2 11.0 %collective-permute-done.2.i1 = bf16[192,1152]{1,0:T(8,128)(2,1)S(1)} collective-permute-done((bf16[192,1152]{1,0:T(8,128)(2,1)}, bf16[192,1152]{1,0:T(8,128)(2,1)S(1)}, u32[]{:S(2)}, u32[]{:S(2)}) %collective-permute-start.2) | collective-permute-done | bytes 442400 | tf_op jit(solution)/shard_map/images_beside/ppermute | solution.py:33
  31.2 0.0 copy-start.5
  31.2 1.0 collective-permute-done.3.i3
  32.2 0.0 copy-start.6
  32.2 6.7 %collective-permute-done.4.b = bf16[192,1152]{1,0:T(8,128)(2,1)S(1)} collective-permute-done((bf16[192,1152]{1,0:T(8,128)(2,1)}, bf16[192,1152]{1,0:T(8,128)(2,1)S(1)}, u32[]{:S(2)}, u32[]{:S(2)}) %collective-permute-start.4) | collective-permute-done | bytes 442400 | tf_op jit(solution)/shard_map/texts_one_up/ppermute | solution.py:33
  38.9 0.0 copy-done.4
  38.9 0.0 copy-done.5
  38.9 0.0 copy-done.6
  38.9 0.0 copy-start.7
  38.9 0.8 copy-done.7
  39.7 0.0 copy-done.3
  39.7 2.3 %halves.1 = (bf16[768,1152]{1,0:T(8,128)(2,1)S(1)}, bf16[576,1152]{1,0:T(8,128)(2,1)S(1)}) custom-call(s32[1]{0:T(128)} %bitcast.1.spot, bf16[192,1152]{1,0:T(8,128)(2,1)} %copy-done.3, bf16[192,1152]{1,0:T(8,128)(2,1)} %copy-done.4, bf16[192,1152]{1,0:T(8,128)(2,1)} %copy-done.5, bf16[192,1152]{1,0:T(8,128)(2,1)} %copy-done.6, bf16[192,1152]{1,0:T(8,128)(2,1)} %copy-done.7, ...), custom_call_target="tpu_custom_call" | custom-call | tf_op jit(solution)/shard_map/halves/pallas_call | solution.py:206
  42.0 3.8 %collective-permute-start.5 = (bf16[576,1152]{1,0:T(8,128)(2,1)S(1)}, bf16[576,1152]{1,0:T(8,128)(2,1)}, u32[]{:S(2)}, u32[]{:S(2)}) collective-permute-start(bf16[576,1152]{1,0:T(8,128)(2,1)S(1)} %get-tuple-element.19.th.t_own), channel_id=1, source_target_pairs={{0,1},{1,0},{2,3},{3,2},{4,5},{5,4},{6,7},{7,6},{8,9},{9,8},{10,11... | collective-permute-start | bytes 3981320 | tf_op jit(solution)/shard_map/texts_sibling/ppermute | solution.py:33
  47.0 4.0 %own_pairs.1 = (bf16[768,384]{1,0:T(8,128)(2,1)S(1)}, f32[3,192,1152]{2,1,0:T(8,128)}, f32[3,8,384]{2,1,0:T(8,128)S(1)}) custom-call(f32[1]{0:T(128)} %bitcast.4.log_temp, f32[1]{0:T(128)} %bitcast.8.bias, bf16[768,1152]{1,0:T(8,128)(2,1)S(1)} %get-tuple-element.18.ih, bf16[576,1152]{1,0:T(8,128)(2,1)S(1)} %get-tuple-element.19.th.t_own), custom_call_target="tpu_custom_call" | custom-call | tf_op jit(solution)/shard_map/own_pairs/pallas_call | solution.py:206
  51.0 0.0 collective-permute-done.5.th.t_sib
  51.0 3.8 %sibling_pairs.1 = (bf16[768,384]{1,0:T(8,128)(2,1)S(1)}, bf16[3,208,1152]{2,1,0:T(8,128)(2,1)S(1)}) custom-call(f32[1]{0:T(128)} %bitcast.5.log_temp, f32[1]{0:T(128)} %bitcast.9.bias, bf16[768,1152]{1,0:T(8,128)(2,1)S(1)} %get-tuple-element.18.ih, bf16[576,1152]{1,0:T(8,128)(2,1)} %collective-permute-done.5.th.t_sib, ...), custom_call_target="tpu_custom_call" | custom-call | tf_op jit(solution)/shard_map/sibling_pairs/pallas_call | solution.py:206
  54.8 1.9 %collective-permute-start.6 = (bf16[3,208,1152]{2,1,0:T(8,128)(2,1)S(1)}, bf16[3,208,1152]{2,1,0:T(8,128)(2,1)S(1)}, u32[]{:S(2)}, u32[]{:S(2)}) collective-permute-start(bf16[3,208,1152]{2,1,0:T(8,128)(2,1)S(1)} %get-tuple-element.22), channel_id=1, source_target_pairs={{0,1},{1,0},{2,3},{3,2},{4,5},{5,4},{6,7},{7,6},{8,9},{9,8},{10,11... | collective-permute-start | bytes 4313096 | tf_op jit(solution)/shard_map/text_parts_sibling/ppermute | solution.py:33
  56.7 0.0 copy-start
  56.7 3.6 %spread.1 = (f32[192,1152]{1,0:T(8,128)S(1)}, bf16[192,1152]{1,0:T(8,128)(2,1)S(1)}, bf16[192,1152]{1,0:T(8,128)(2,1)S(1)}, bf16[192,1152]{1,0:T(8,128)(2,1)S(1)}) custom-call(bf16[768,384]{1,0:T(8,128)(2,1)S(1)} %get-tuple-element.23.p_own, bf16[768,384]{1,0:T(8,128)(2,1)S(1)} %get-tuple-element.24.p_sib, bf16[576,1152]{1,0:T(8,128)(2,1)S(1)} %get-tuple-element.19.th.t_own, ...), custom_call_target="tpu_custom_call" | custom-call | tf_op jit(solution)/shard_map/spread/pallas_call | solution.py:206
  60.3 0.0 collective-permute-done.6.got
  60.4 0.0 copy-done
  60.4 0.0 copy-start.2
  60.4 0.2 join.1
  60.6 6.6 %collective-permute-start.7 = (bf16[208,1152]{1,0:T(8,128)(2,1)S(1)}, bf16[208,1152]{1,0:T(8,128)(2,1)S(1)}, u32[]{:S(2)}, u32[]{:S(2)}) collective-permute-start(bf16[208,1152]{1,0:T(8,128)(2,1)S(1)} %get-tuple-element.26), channel_id=1, source_target_pairs={{0,760},{1,761},{2,762},{3,763},{4,764},{5,765},{6,766},{7,767},{8... | collective-permute-start | bytes 1437704 | tf_op jit(solution)/shard_map/text_parts_one_down/ppermute | solution.py:33
  67.1 0.7 collective-permute-start.8
  67.8 12.2 %collective-permute-start.10 = (bf16[192,1152]{1,0:T(8,128)(2,1)S(1)}, bf16[192,1152]{1,0:T(8,128)(2,1)S(1)}, u32[]{:S(2)}, u32[]{:S(2)}) collective-permute-start(bf16[192,1152]{1,0:T(8,128)(2,1)S(1)} %get-tuple-element.25.after), channel_id=1, source_target_pairs={{0,4},{1,5},{2,6},{3,7},{4,0},{5,1},{6,2},{7,3},{8,12},{9,13},{10,... | collective-permute-start | bytes 1327112 | tf_op jit(solution)/shard_map/image_parts_across/ppermute | solution.py:33
  80.1 2.2 %collective-permute-start.9 = (bf16[192,1152]{1,0:T(8,128)(2,1)S(1)}, bf16[192,1152]{1,0:T(8,128)(2,1)S(1)}, u32[]{:S(2)}, u32[]{:S(2)}) collective-permute-start(bf16[192,1152]{1,0:T(8,128)(2,1)S(1)} %get-tuple-element.30), channel_id=1, source_target_pairs={{0,2},{1,3},{2,0},{3,1},{4,6},{5,7},{6,4},{7,5},{8,10},{9,11},{10,... | collective-permute-start | bytes 1327112 | tf_op jit(solution)/shard_map/image_parts_beside/ppermute | solution.py:33
  82.3 1.9 %collective-permute-start.11 = (bf16[192,1152]{1,0:T(8,128)(2,1)S(1)}, bf16[192,1152]{1,0:T(8,128)(2,1)S(1)}, u32[]{:S(2)}, u32[]{:S(2)}) collective-permute-start(bf16[192,1152]{1,0:T(8,128)(2,1)S(1)} %get-tuple-element.31), channel_id=1, source_target_pairs={{0,6},{1,7},{2,4},{3,5},{4,2},{5,3},{6,0},{7,1},{8,14},{9,15},{10,... | collective-permute-start | bytes 1327112 | tf_op jit(solution)/shard_map/image_parts_beside_far/ppermute | solution.py:33
  84.2 14.8 %collective-permute-done.9.a = bf16[192,1152]{1,0:T(8,128)(2,1)S(1)} collective-permute-done((bf16[192,1152]{1,0:T(8,128)(2,1)S(1)}, bf16[192,1152]{1,0:T(8,128)(2,1)S(1)}, u32[]{:S(2)}, u32[]{:S(2)}) %collective-permute-start.9) | collective-permute-done | bytes 442400 | tf_op jit(solution)/shard_map/image_parts_beside/ppermute | solution.py:33
  99.0 0.0 collective-permute-done.10.b
  99.0 0.9 collective-permute-done.11.c
  99.9 0.0 copy-done.2
  99.9 0.0 copy-start.1
  99.9 1.4 %image_end.1 = f32[192,1152]{1,0:T(8,128)} custom-call(f32[1]{0:T(128)} %bitcast.7.log_temp, bf16[192,1152]{1,0:T(8,128)(2,1)S(1)} %copy-done.2, f32[192,1152]{1,0:T(8,128)S(1)} %get-tuple-element.29.own, bf16[192,1152]{1,0:T(8,128)(2,1)S(1)} %collective-permute-done.9.a, bf16[192,1152]{1,0:T(8,128)(2,1)S(1)} %collective-permute-done.10.b, ...), custom_call_target="tpu_custom_call" | custom-call | tf_op jit(solution)/shard_map/image_end/pallas_call | solution.py:206
  101.4 0.0 collective-permute-done.7.b_got
  101.4 0.0 collective-permute-done.8.c_got
  101.4 0.0 copy-done.1
  101.4 1.5 %text_end.1 = (f32[192,1152]{1,0:T(8,128)}, f32[1,192]{1,0:T(1,128)}) custom-call(f32[1]{0:T(128)} %bitcast.6.log_temp, s32[1]{0:T(128)} %bitcast.1.spot, bf16[192,1152]{1,0:T(8,128)(2,1)S(1)} %copy-done.1, f32[3,192,1152]{2,1,0:T(8,128)S(1)} %copy-done, bf16[3,208,1152]{2,1,0:T(8,128)(2,1)S(1)} %collective-permute-done.6.got, ...), custom_call_target="tpu_custom_call" | custom-call | tf_op jit(solution)/shard_map/text_end/pallas_call | solution.py:206
Async XLA Ops:
  0.6 19.5 %collective-permute-start = (bf16[192,1152]{1,0:T(8,128)(2,1)}, bf16[192,1152]{1,0:T(8,128)(2,1)S(1)}, u32[]{:S(2)}, u32[]{:S(2)}) collective-permute-start(bf16[192,1152]{1,0:T(8,128)(2,1)} %texts.1), channel_id=1, source_target_pairs={{4,20},{5,21},{6,22},{7,23},{12,28},{13,29},{14,30},{15,31},{20,36... | collective-permute-start | bytes 1327112 | tf_op jit(solution)/shard_map/texts_two_up/ppermute | solution.py:33
  1.3 18.9 %collective-permute-start.1 = (bf16[192,1152]{1,0:T(8,128)(2,1)}, bf16[192,1152]{1,0:T(8,128)(2,1)S(1)}, u32[]{:S(2)}, u32[]{:S(2)}) collective-permute-start(bf16[192,1152]{1,0:T(8,128)(2,1)} %images.1), channel_id=1, source_target_pairs={{0,4},{1,5},{2,6},{3,7},{4,0},{5,1},{6,2},{7,3},{8,12},{9,13},{10,... | collective-permute-start | bytes 1327112 | tf_op jit(solution)/shard_map/images_across/ppermute | solution.py:33
  11.9 19.3 %collective-permute-start.2 = (bf16[192,1152]{1,0:T(8,128)(2,1)}, bf16[192,1152]{1,0:T(8,128)(2,1)S(1)}, u32[]{:S(2)}, u32[]{:S(2)}) collective-permute-start(bf16[192,1152]{1,0:T(8,128)(2,1)} %images.1), channel_id=1, source_target_pairs={{0,2},{1,3},{2,0},{3,1},{4,6},{5,7},{6,4},{7,5},{8,10},{9,11},{10,... | collective-permute-start | bytes 1327112 | tf_op jit(solution)/shard_map/images_beside/ppermute | solution.py:33
  14.2 18.0 %collective-permute-start.3 = (bf16[192,1152]{1,0:T(8,128)(2,1)}, bf16[192,1152]{1,0:T(8,128)(2,1)S(1)}, u32[]{:S(2)}, u32[]{:S(2)}) collective-permute-start(bf16[192,1152]{1,0:T(8,128)(2,1)} %images.1), channel_id=1, source_target_pairs={{0,6},{1,7},{2,4},{3,5},{4,2},{5,3},{6,0},{7,1},{8,14},{9,15},{10,... | collective-permute-start | bytes 1327112 | tf_op jit(solution)/shard_map/images_beside_far/ppermute | solution.py:33
  16.1 22.8 %collective-permute-start.4 = (bf16[192,1152]{1,0:T(8,128)(2,1)}, bf16[192,1152]{1,0:T(8,128)(2,1)S(1)}, u32[]{:S(2)}, u32[]{:S(2)}) collective-permute-start(bf16[192,1152]{1,0:T(8,128)(2,1)} %texts.1), channel_id=1, source_target_pairs={{0,8},{1,9},{2,10},{3,11},{4,12},{5,13},{6,14},{7,15},{8,16},{9,17... | collective-permute-start | bytes 1327112 | tf_op jit(solution)/shard_map/texts_one_up/ppermute | solution.py:33
  20.1 19.5 %copy-start.3 = (bf16[192,1152]{1,0:T(8,128)(2,1)}, bf16[192,1152]{1,0:T(8,128)(2,1)S(1)}, u32[]{:S(2)}) copy-start(bf16[192,1152]{1,0:T(8,128)(2,1)S(1)} %collective-permute-done.c) | copy-start | bytes 1327108
  20.2 18.7 %copy-start.4 = (bf16[192,1152]{1,0:T(8,128)(2,1)}, bf16[192,1152]{1,0:T(8,128)(2,1)S(1)}, u32[]{:S(2)}) copy-start(bf16[192,1152]{1,0:T(8,128)(2,1)S(1)} %collective-permute-done.1.i2) | copy-start | bytes 1327108
  31.2 7.7 %copy-start.5 = (bf16[192,1152]{1,0:T(8,128)(2,1)}, bf16[192,1152]{1,0:T(8,128)(2,1)S(1)}, u32[]{:S(2)}) copy-start(bf16[192,1152]{1,0:T(8,128)(2,1)S(1)} %collective-permute-done.2.i1) | copy-start | bytes 1327108
  32.2 6.7 %copy-start.6 = (bf16[192,1152]{1,0:T(8,128)(2,1)}, bf16[192,1152]{1,0:T(8,128)(2,1)S(1)}, u32[]{:S(2)}) copy-start(bf16[192,1152]{1,0:T(8,128)(2,1)S(1)} %collective-permute-done.3.i3) | copy-start | bytes 1327108
  38.9 0.8 copy-start.7
  42.0 9.1 %collective-permute-start.5 = (bf16[576,1152]{1,0:T(8,128)(2,1)S(1)}, bf16[576,1152]{1,0:T(8,128)(2,1)}, u32[]{:S(2)}, u32[]{:S(2)}) collective-permute-start(bf16[576,1152]{1,0:T(8,128)(2,1)S(1)} %get-tuple-element.19.th.t_own), channel_id=1, source_target_pairs={{0,1},{1,0},{2,3},{3,2},{4,5},{5,4},{6,7},{7,6},{8,9},{9,8},{10,11... | collective-permute-start | bytes 3981320 | tf_op jit(solution)/shard_map/texts_sibling/ppermute | solution.py:33
  54.8 5.5 %collective-permute-start.6 = (bf16[3,208,1152]{2,1,0:T(8,128)(2,1)S(1)}, bf16[3,208,1152]{2,1,0:T(8,128)(2,1)S(1)}, u32[]{:S(2)}, u32[]{:S(2)}) collective-permute-start(bf16[3,208,1152]{2,1,0:T(8,128)(2,1)S(1)} %get-tuple-element.22), channel_id=1, source_target_pairs={{0,1},{1,0},{2,3},{3,2},{4,5},{5,4},{6,7},{7,6},{8,9},{9,8},{10,11... | collective-permute-start | bytes 4313096 | tf_op jit(solution)/shard_map/text_parts_sibling/ppermute | solution.py:33
  56.7 3.6 %copy-start = (f32[3,192,1152]{2,1,0:T(8,128)S(1)}, f32[3,192,1152]{2,1,0:T(8,128)}, u32[]{:S(2)}) copy-start(f32[3,192,1152]{2,1,0:T(8,128)} %get-tuple-element.20.own) | copy-start | bytes 7962628
  60.4 39.6 %copy-start.2 = (bf16[192,1152]{1,0:T(8,128)(2,1)S(1)}, bf16[192,1152]{1,0:T(8,128)(2,1)}, u32[]{:S(2)}) copy-start(bf16[192,1152]{1,0:T(8,128)(2,1)} %images.1) | copy-start | bytes 1327108
  60.6 40.8 %collective-permute-start.7 = (bf16[208,1152]{1,0:T(8,128)(2,1)S(1)}, bf16[208,1152]{1,0:T(8,128)(2,1)S(1)}, u32[]{:S(2)}, u32[]{:S(2)}) collective-permute-start(bf16[208,1152]{1,0:T(8,128)(2,1)S(1)} %get-tuple-element.26), channel_id=1, source_target_pairs={{0,760},{1,761},{2,762},{3,763},{4,764},{5,765},{6,766},{7,767},{8... | collective-permute-start | bytes 1437704 | tf_op jit(solution)/shard_map/text_parts_one_down/ppermute | solution.py:33
  67.1 34.3 %collective-permute-start.8 = (bf16[208,1152]{1,0:T(8,128)(2,1)S(1)}, bf16[208,1152]{1,0:T(8,128)(2,1)S(1)}, u32[]{:S(2)}, u32[]{:S(2)}) collective-permute-start(bf16[208,1152]{1,0:T(8,128)(2,1)S(1)} %get-tuple-element.27), channel_id=1, source_target_pairs={{4,756},{5,757},{6,758},{7,759},{12,764},{13,765},{14,766},{15,767... | collective-permute-start | bytes 1437704 | tf_op jit(solution)/shard_map/text_parts_two_down/ppermute | solution.py:33
  67.8 31.2 %collective-permute-start.10 = (bf16[192,1152]{1,0:T(8,128)(2,1)S(1)}, bf16[192,1152]{1,0:T(8,128)(2,1)S(1)}, u32[]{:S(2)}, u32[]{:S(2)}) collective-permute-start(bf16[192,1152]{1,0:T(8,128)(2,1)S(1)} %get-tuple-element.25.after), channel_id=1, source_target_pairs={{0,4},{1,5},{2,6},{3,7},{4,0},{5,1},{6,2},{7,3},{8,12},{9,13},{10,... | collective-permute-start | bytes 1327112 | tf_op jit(solution)/shard_map/image_parts_across/ppermute | solution.py:33
  80.1 19.0 %collective-permute-start.9 = (bf16[192,1152]{1,0:T(8,128)(2,1)S(1)}, bf16[192,1152]{1,0:T(8,128)(2,1)S(1)}, u32[]{:S(2)}, u32[]{:S(2)}) collective-permute-start(bf16[192,1152]{1,0:T(8,128)(2,1)S(1)} %get-tuple-element.30), channel_id=1, source_target_pairs={{0,2},{1,3},{2,0},{3,1},{4,6},{5,7},{6,4},{7,5},{8,10},{9,11},{10,... | collective-permute-start | bytes 1327112 | tf_op jit(solution)/shard_map/image_parts_beside/ppermute | solution.py:33
  82.3 17.6 %collective-permute-start.11 = (bf16[192,1152]{1,0:T(8,128)(2,1)S(1)}, bf16[192,1152]{1,0:T(8,128)(2,1)S(1)}, u32[]{:S(2)}, u32[]{:S(2)}) collective-permute-start(bf16[192,1152]{1,0:T(8,128)(2,1)S(1)} %get-tuple-element.31), channel_id=1, source_target_pairs={{0,6},{1,7},{2,4},{3,5},{4,2},{5,3},{6,0},{7,1},{8,14},{9,15},{10,... | collective-permute-start | bytes 1327112 | tf_op jit(solution)/shard_map/image_parts_beside_far/ppermute | solution.py:33
  99.9 1.4 %copy-start.1 = (bf16[192,1152]{1,0:T(8,128)(2,1)S(1)}, bf16[192,1152]{1,0:T(8,128)(2,1)}, u32[]{:S(2)}) copy-start(bf16[192,1152]{1,0:T(8,128)(2,1)} %texts.1) | copy-start | bytes 1327108
